TPU v7x, 32 devices: a whole 2x2x4 slice. The times are simulated.
32 devices in a mesh: section: 2 (over x), hid: 4 (over z), wid: 4 (over y, core).
Axes of the slice: x: 2, y: 2, z: 4, core: 2. Of those that a mesh axis runs over, the one named last changes fastest.
Arguments:
- grad_out: float32 [2, 256, 6144], P(None, None, 'wid'), may hold values from -6 to 6
- weight_in: bfloat16 [2, 6144, 24576], P('section', 'wid', 'hid'), may hold values from -0.078125 to 0.078125
- weight_out: bfloat16 [2, 24576, 6144], P('section', 'hid', 'wid'), may hold values from -0.0390625 to 0.0390625
- pre_act: float32 [2, 2, 256, 24576], P('section', None, None, 'hid'), may hold values from -6 to 6
Outputs:
- grads: float32 [2, 2, 256, 6144], P('section', None, None, 'wid')
All inputs are finite; a program needn't handle non-finite values.
Results may differ from a plain program's by a relative error of at most 0.003.
Values may be sent and summed in bfloat16 or wider, within the bound.
No kernel may reach another device: no remote copies, remote signals or barrier semaphores. Data moves between devices by JAX's collectives and lax.ppermute only.
A program may use at most 192 MiB of HBM per device.

v0:
```python
import jax
import jax.numpy as jnp
from jax import lax
from jax.experimental import pallas as pl
from jax.experimental.pallas import tpu as pltpu
from jax.sharding import PartitionSpec as P

SHARES = (1, 1)
PARTS = 4
LANES = 128
WEIGHT = 4096
LIMIT = 46 * 1024 * 1024
LOW = jnp.bfloat16
F32 = jnp.float32


def gelu_slope(pre):
    normal_cdf = 0.5 * (1.0 + lax.erf(pre * 0.7071067811865476))
    density = jnp.exp(-0.5 * pre * pre) * 0.3989422804014327
    return normal_cdf + pre * density


def params():
    return pltpu.CompilerParams(vmem_limit_bytes=LIMIT)


def divisor(size, most):
    return max(r for r in range(16, most + 1, 16) if size % r == 0)


SMEM = pl.BlockSpec(memory_space=pltpu.SMEM)
VMEM = pl.BlockSpec(memory_space=pltpu.VMEM)
ANY = pl.BlockSpec(memory_space=pl.ANY)


def product(flags, mat, block, place, steps, sources, prepare, tokens, outs, base=None, base_row=None, apart=False):
    rows, depth = block
    slots = min(4, steps)
    bare = prepare is None
    count = len(sources)

    def body(s, mat_ref, *refs):
        source_refs, refs = refs[:count], refs[count:]
        base_ref = None
        if base is not None:
            base_ref, refs = refs[0], refs[1:]
        out_refs, (buf, sem) = refs[:-2], refs[-2:]

        def fetch(i):
            row, col = place(i, s)
            piece = mat_ref.at[pl.ds(pl.multiple_of(row, 16), rows), pl.ds(pl.multiple_of(col, LANES), depth)]
            slot = lax.rem(i, slots)
            return pltpu.make_async_copy(piece, buf.at[slot], sem.at[slot])

        @pl.when(s[0] == 1)
        def _():
            for i in range(slots):
                fetch(i).start()
            right_ref = source_refs[0]
            if not bare:
                right_ref = out_refs[-1]
                prepare(right_ref, *source_refs)

            @pl.loop(0, steps)
            def _(i):
                fetch(i).wait()
                got = jnp.dot(buf[lax.rem(i, slots)], right_ref[...], preferred_element_type=F32)

                @pl.when(i + slots < steps)
                def _():
                    fetch(i + slots).start()

                if base_ref is not None:
                    start = pl.multiple_of(base_row(i, s), 16)
                    got = got + base_ref[pl.ds(start, rows)].astype(F32)
                if apart:
                    for which, ref in enumerate(out_refs[:steps]):

                        @pl.when(i == which)
                        def _(ref=ref):
                            ref[...] = got.astype(ref.dtype)
                else:
                    at = pl.ds(pl.multiple_of(i * rows, 16), rows)
                    for ref in out_refs[: len(outs)]:
                        ref[at] = got.astype(ref.dtype)

    shapes = [jax.ShapeDtypeStruct((size, tokens), kind) for size, kind in outs]
    if not bare:
        shapes.append(jax.ShapeDtypeStruct((depth, tokens), LOW))
    return pl.pallas_call(
        body,
        in_specs=[SMEM, ANY] + [VMEM] * (count + (base is not None)),
        out_specs=[VMEM] * len(shapes),
        out_shape=shapes,
        scratch_shapes=[
            pltpu.VMEM((slots, rows, depth), LOW),
            pltpu.SemaphoreType.DMA((slots,)),
        ],
        compiler_params=params(),
        cost_estimate=pl.CostEstimate(
            flops=2 * tokens * rows * depth * steps // WEIGHT,
            bytes_accessed=2 * rows * depth * steps // WEIGHT,
            transcendentals=0,
        ),
    )(flags, mat, *sources, *([] if base is None else [base]))


def turned(right_ref, grad_ref):
    right_ref[...] = grad_ref[...].T.astype(LOW)


def hidden_of(right_ref, own_ref, other_ref, slope_ref):
    total = own_ref[...] + other_ref[...].astype(F32)
    right_ref[...] = (total * slope_ref[...]).astype(LOW)


def split_rows(flags, mat):
    rows, cols = mat.shape
    step = 256
    half = step // 2
    count = rows // step
    slots = 4

    def body(s, mat_ref, out_ref, buf, done, sem_in, sem_out):
        def fetch(i, slot):
            piece = mat_ref.at[pl.ds(pl.multiple_of(i * step, step), step)]
            return pltpu.make_async_copy(piece, buf.at[slot], sem_in.at[slot])

        def put(i, slot):
            piece = out_ref.at[:, pl.ds(pl.multiple_of(i * half, half), half)]
            return pltpu.make_async_copy(done.at[slot], piece, sem_out.at[slot])

        @pl.when(s[0] == 1)
        def _():
            to = lax.broadcasted_iota(jnp.int32, (step, step), 0)
            source = lax.broadcasted_iota(jnp.int32, (step, step), 1)
            wanted = jnp.where(to < half, 2 * to, 2 * (to - half) + 1)
            pick = jnp.where(source == wanted, 1.0, 0.0).astype(LOW)
            for i in range(slots):
                fetch(i, i).start()

            @pl.loop(0, count // slots)
            def _(turn):
                for slot in range(slots):
                    i = turn * slots + slot
                    fetch(i, slot).wait()

                    @pl.when(turn > 0)
                    def _():
                        put(i - slots, slot).wait()

                    got = jnp.dot(pick, buf[slot], preferred_element_type=F32).astype(LOW)
                    done[slot, 0] = got[:half]
                    done[slot, 1] = got[half:]

                    @pl.when(turn < count // slots - 1)
                    def _():
                        fetch(i + slots, slot).start()

                    put(i, slot).start()

            for slot in range(slots):
                put(count - slots + slot, slot).wait()

    out = pl.pallas_call(
        body,
        in_specs=[SMEM, ANY],
        out_specs=ANY,
        out_shape=jax.ShapeDtypeStruct((2, rows // 2, cols), LOW),
        scratch_shapes=[
            pltpu.VMEM((slots, step, cols), LOW),
            pltpu.VMEM((slots, 2, half, cols), LOW),
            pltpu.SemaphoreType.DMA((slots,)),
            pltpu.SemaphoreType.DMA((slots,)),
        ],
        compiler_params=params(),
        cost_estimate=pl.CostEstimate(
            flops=2 * rows * step * cols // WEIGHT, bytes_accessed=4 * rows * cols // WEIGHT, transcendentals=0
        ),
    )(flags, mat)
    return out.reshape(rows, cols)


def slope_of(flags, pre, start, tokens, half):
    cols = divisor(half, 768)
    per_half = half // cols

    def body(s, pre_ref, out_ref):
        out_ref[...] = gelu_slope(pre_ref[...]).T

    return pl.pallas_call(
        body,
        grid_spec=pltpu.PrefetchScalarGridSpec(
            num_scalar_prefetch=1,
            grid=(tokens // LANES, per_half),
            in_specs=[
                pl.BlockSpec((LANES, cols), lambda i, j, s: (start // LANES + i, s[1] * per_half + j))
            ],
            out_specs=pl.BlockSpec((cols, LANES), lambda i, j, s: (j, i)),
        ),
        out_shape=jax.ShapeDtypeStruct((half, tokens), F32),
        compiler_params=params(),
        cost_estimate=pl.CostEstimate(
            flops=half * tokens // WEIGHT, bytes_accessed=8 * half * tokens // WEIGHT, transcendentals=0
        ),
    )(flags, pre)


def join(flags, grad, parts):
    tokens, columns = grad.shape
    width = columns // PARTS

    def body(s, grad_ref, *refs):
        part_refs, (low_ref, term_ref) = refs[:PARTS], refs[PARTS:]

        @pl.when(s[0] == 1)
        def _():
            for slot, ref in enumerate(part_refs):
                start = pl.multiple_of(lax.bitwise_xor(s[2], slot) * width, LANES)
                term = ref[...]
                term_ref[pl.ds(start, width)] = term
                total = grad_ref[:, pl.ds(start, width)].T + term.astype(F32)
                low_ref[pl.ds(start, width)] = total.astype(LOW)

    shape = jax.ShapeDtypeStruct((columns, tokens), LOW)
    return pl.pallas_call(
        body,
        in_specs=[SMEM] + [VMEM] * (1 + PARTS),
        out_specs=[VMEM, VMEM],
        out_shape=[shape, shape],
        compiler_params=params(),
        cost_estimate=pl.CostEstimate(
            flops=4 * columns * tokens, bytes_accessed=4 * columns * tokens, transcendentals=0
        ),
    )(flags, grad, *parts)


def finish(flags, out, grad, start, term, parts):
    columns, tokens = term.shape
    width = columns // PARTS
    total_tokens = grad.shape[0]

    def body(s, *refs):
        grad_ref, term_ref, *part_refs = refs[int(out is not None) : -2]
        out_ref, joined = refs[-2:]
        for slot, ref in enumerate(part_refs):
            start = pl.multiple_of(lax.bitwise_xor(s[2], slot) * width, LANES)
            joined[pl.ds(start, width)] = ref[...]

        @pl.when(s[0] == 0)
        def _():
            out_ref[...] = grad_ref[...] + joined[...].astype(F32).T

        @pl.when(s[0] == 1)
        def _():
            source = lax.broadcasted_iota(jnp.int32, (2 * LANES, 2 * LANES), 1)
            to = lax.broadcasted_iota(jnp.int32, (2 * LANES, 2 * LANES), 0)
            wanted = jnp.where(source < LANES, 2 * source, 2 * (source - LANES) + 1)
            pick = jnp.where(to == wanted, 1.0, 0.0).astype(LOW)
            for group in range(columns // (2 * LANES)):
                even_at = group * LANES
                odd_at = columns // 2 + group * LANES
                even = joined[even_at : even_at + LANES]
                odd = joined[odd_at : odd_at + LANES]
                pair = jnp.concatenate([even, odd], axis=0)
                woven = jnp.dot(pick, pair, preferred_element_type=F32)
                at = slice(group * 2 * LANES, (group + 1) * 2 * LANES)
                first = term_ref[at].astype(F32).T
                out_ref[:, at] = grad_ref[:, at] + first + woven.T

    earlier = [] if out is None else [out]
    piece = pl.BlockSpec((width, LANES), lambda i, s: (0, i))
    rows = pl.BlockSpec((LANES, columns), lambda i, s: (start // LANES + i, 0))
    return pl.pallas_call(
        body,
        grid_spec=pltpu.PrefetchScalarGridSpec(
            num_scalar_prefetch=1,
            grid=(tokens // LANES,),
            in_specs=[ANY] * len(earlier)
            + [rows, pl.BlockSpec((columns, LANES), lambda i, s: (0, i))]
            + [piece] * PARTS,
            out_specs=rows,
            scratch_shapes=[pltpu.VMEM((columns, LANES), LOW)],
        ),
        out_shape=jax.ShapeDtypeStruct((total_tokens, columns), F32),
        input_output_aliases={1: 0} if earlier else {},
        compiler_params=params(),
    )(flags, *earlier, grad, term, *parts)


def local(grad_out, weight_in, weight_out, pre_act):
    hids = lax.axis_size("hid")
    section = lax.axis_index("section")
    side = lax.axis_index("wid") % 2
    is_up = section == 1

    def scalars(active_section):
        active = (section == active_section).astype(jnp.int32)
        return jnp.stack([active, side, lax.axis_index("hid") % PARTS]).astype(jnp.int32)

    down, up = scalars(0), scalars(1)

    def within(active, distance, block, axis="wid"):
        size = lax.axis_size(axis)
        pairs = [(active * size + i, active * size + (i ^ distance)) for i in range(size)]
        return lax.ppermute(block, ("section", axis), pairs)

    def everywhere(distance, block, axis="hid"):
        size = lax.axis_size(axis)
        return lax.ppermute(block, axis, [(i, i ^ distance) for i in range(size)])

    mat_in = weight_in[0]
    mat_out = weight_out[0]
    quarter, hid_tile = mat_in.shape
    half = hid_tile // 2
    batches, batch_tokens, _ = grad_out.shape
    total = batches * batch_tokens
    unit = total // sum(SHARES)
    starts = [unit * sum(SHARES[:k]) for k in range(len(SHARES))]
    sizes = [unit * share for share in SHARES]
    chunks = range(len(SHARES))
    grad = grad_out.reshape(total, quarter)
    pre = pre_act[0].reshape(total, hid_tile)
    grads = [grad[starts[k] : starts[k] + sizes[k]] for k in chunks]

    split_out = split_rows(up, mat_out)

    hid_rows = divisor(half, 512)
    hid_steps = half // hid_rows
    part_rows = quarter // PARTS

    def product_out(flags, mat, first_row, sources, prepare, tokens, kinds, base=None):
        return product(
            flags, mat, (hid_rows, quarter),
            lambda i, s: (first_row(s) + i * hid_rows, 0), hid_steps,
            sources, prepare, tokens, [(half, kind) for kind in kinds],
            base, lambda i, s: i * hid_rows,
        )

    def product_in(flags, place, sources, prepare, tokens, kind):
        return product(
            flags, mat_in, (part_rows, half), place, PARTS, sources, prepare, tokens,
            [(quarter, kind)],
        )

    def product_parts(flags, place, right, tokens, base):
        def part_of(i, s):
            return lax.bitwise_xor(s[2], lax.rem(i + 1, PARTS))

        return product(
            flags, mat_in, (part_rows, half), lambda i, s: place(part_of(i, s), s), PARTS,
            [right], None, tokens, [(part_rows, LOW)] * 3 + [(part_rows, F32)],
            base, lambda i, s: part_of(i, s) * part_rows, True,
        )

    def scatter_hid(active, parts):
        *others, own = parts
        got = [within(active, d + 1, part, "hid") for d, part in enumerate(others)]
        for part in got:
            own = own + part.astype(F32)
        distance = PARTS
        while distance < hids:
            own = own + within(active, distance, own, "hid")
            distance *= 2
        return own.astype(LOW)

    class Steps:
        def __init__(self):
            self.last = None

        def after(self, value):
            if self.last is None:
                return value
            return lax.optimization_barrier((value, self.last))[0]

    steps = Steps()
    steps.last = split_out
    hidden_full, hidden_other, slopes, parts_out, terms, gathered = {}, {}, {}, {}, {}, {}
    lows, core_got = {}, {}
    up_full, up_other, up_parts, up_terms, lasts = {}, {}, {}, {}, {}

    def down_send(k):
        sent, lows[k] = product_out(
            steps.after(down), mat_out, lambda s: (1 - s[1]) * half, [grads[k]], turned,
            sizes[k], (LOW,),
        )
        steps.last = sent
        core_got[k] = within(0, 1, sent)

    def down_hidden(k):
        full, low_grad = product_out(
            steps.after(down), mat_out, lambda s: s[1] * half, [lows[k]], None, sizes[k],
            (F32, LOW), core_got[k],
        )
        steps.last = low_grad
        if k > 0:
            low_grad = lax.optimization_barrier((low_grad, hidden_other[k - 1]))[0]
        hidden_full[k], hidden_other[k] = full, within(0, 2, low_grad)

    def slope(k):
        slopes[k] = slope_of(steps.after(down), pre, starts[k], sizes[k], half)
        steps.last = slopes[k]

    def down_back(k):
        tokens = sizes[k]
        full = steps.after(hidden_full[k])
        hidden = ((full + hidden_other[k].astype(F32)) * slopes[k]).astype(LOW)
        swapped = within(0, 1, hidden)
        (partial,) = product_in(
            down, lambda i, s: (i * part_rows, s[1] * half), [hidden], None, tokens, F32
        )
        parts_out[k] = product_parts(
            down, lambda i, s: (i * part_rows, (1 - s[1]) * half), swapped, tokens, partial
        )
        steps.last = parts_out[k][0]

    def cross(k):
        *others, own = parts_out[k]
        terms[k] = scatter_hid(0, others + [steps.after(own)])
        crossed = lax.ppermute(terms[k], "section", [(0, 1)])
        steps.last = crossed
        gathered[k] = [crossed] + [within(1, d, crossed, "hid") for d in range(1, PARTS)]

    def up_hidden(k):
        tokens = sizes[k]
        low, up_terms[k] = join(steps.after(up), grads[k], gathered[k])
        low_other = within(1, 1, low)
        (partial,) = product_out(
            up, split_out, lambda s: s[1] * half, [low], None, tokens, (F32,)
        )
        full, low_grad = product_out(
            up, split_out, lambda s: (1 - s[1]) * half, [low_other], None, tokens, (F32, LOW), partial
        )
        steps.last = low_grad
        if k > 0:
            low_grad = lax.optimization_barrier((low_grad, up_other[k - 1]))[0]
        up_full[k], up_other[k] = full, within(1, 2, low_grad)

    def place(part, core):
        row = core * (PARTS // 2) + lax.rem(part, PARTS // 2)
        return row * part_rows, lax.div(part, PARTS // 2) * half

    def up_back(k):
        tokens = sizes[k]
        sent, hidden = product_in(
            steps.after(up), lambda i, s: place(i, 1 - s[1]),
            [up_full[k], up_other[k], slopes[k]], hidden_of, tokens, F32,
        )
        got = within(1, 1, sent)
        up_parts[k] = product_parts(up, lambda i, s: place(i, s[1]), hidden, tokens, got)
        steps.last = up_parts[k][0]

    def gather(k):
        *others, own = up_parts[k]
        last = jnp.where(is_up, scatter_hid(1, others + [steps.after(own)]), terms[k])
        steps.last = last
        lasts[k] = [last] + [everywhere(d, last) for d in range(1, PARTS)]

    for k in chunks:
        down_send(k)
    for k in chunks:
        down_hidden(k)
    for k in chunks:
        slope(k)
    for k in chunks:
        down_back(k)
        cross(k)
        up_hidden(k)
    for k in chunks:
        up_back(k)
        gather(k)
    out = None
    for k in chunks:
        out = finish(up, out, grad, starts[k], up_terms[k], lasts[k])
    return out.reshape(1, batches, batch_tokens, quarter)


def solution(mesh):
    return jax.shard_map(
        local,
        mesh=mesh,
        in_specs=(
            P(None, None, "wid"),
            P("section", "wid", "hid"),
            P("section", "hid", "wid"),
            P("section", None, None, "hid"),
        ),
        out_specs=P("section", None, None, "wid"),
        check_vma=False,
    )
```

profile of v0, /device:TPU:2, one launch (start us, length us, event | category | flops | bytes accessed | tf_op | source)
XLA Modules:
  0.0 333.9 jit_solution(10924789085967913751)
XLA Ops:
  2.2 14.2 %shard_map.46 = bf16[2,3072,1536]{2,1,0:T(8,128)(2,1)} custom-call(s32[3]{0:T(128)S(1)} %get-tuple-element.103.s, bf16[6144,1536]{1,0:T(8,128)(2,1)} %bitcast.24), custom_call_target="tpu_custom_call" | custom-call | flops 1179648 | bytes 9216 | tf_op jit(solution)/shard_map/pallas_call | solution.py:165
  24.9 6.3 %shard_map.51.refs_2_ = f32[3072,256]{1,0:T(8,128)S(1)} custom-call(s32[3]{0:T(128)S(1)} %get-tuple-element.71.s, f32[512,6144]{1,0:T(8,128)} %bitcast.33), custom_call_target="tpu_custom_call" | custom-call | flops 192 | bytes 1536 | tf_op jit(solution)/shard_map/pallas_call | solution.py:191
  31.2 7.3 %shard_map.52.refs_2_ = f32[3072,256]{1,0:T(8,128)S(1)} custom-call(s32[3]{0:T(128)S(1)} %get-tuple-element.71.s, f32[512,6144]{1,0:T(8,128)} %bitcast.34), custom_call_target="tpu_custom_call" | custom-call | flops 192 | bytes 1536 | tf_op jit(solution)/shard_map/pallas_call | solution.py:191
  48.9 59.4 %collective-permute-done.7.refs_0_ = bf16[384,256]{1,0:T(8,128)(2,1)S(1)} collective-permute-done((bf16[384,256]{1,0:T(8,128)(2,1)S(1)}, bf16[384,256]{1,0:T(8,128)(2,1)S(1)}, u32[]{:S(2)}, u32[]{:S(2)}) %collective-permute-start.7) | collective-permute-done | bytes 196640 | tf_op jit(solution)/shard_map/ppermute | solution.py:420
  108.3 5.4 %collective-permute-start.10 = (bf16[384,256]{1,0:T(8,128)(2,1)S(1)}, bf16[384,256]{1,0:T(8,128)(2,1)S(1)}, u32[]{:S(2)}, u32[]{:S(2)}) collective-permute-start(bf16[384,256]{1,0:T(8,128)(2,1)S(1)} %collective-permute-done.7.refs_0_), channel_id=1, source_target_pairs={{16,28},{20,24},{24,20},{28,16},{17,29},{21,25},{25,21},{29,17},{1... | collective-permute-start | bytes 589832 | tf_op jit(solution)/shard_map/ppermute | solution.py:306
  119.1 11.2 %collective-permute-done.9.refs_2_ = bf16[384,256]{1,0:T(8,128)(2,1)S(1)} collective-permute-done((bf16[384,256]{1,0:T(8,128)(2,1)S(1)}, bf16[384,256]{1,0:T(8,128)(2,1)S(1)}, u32[]{:S(2)}, u32[]{:S(2)}) %collective-permute-start.9) | collective-permute-done | bytes 196640 | tf_op jit(solution)/shard_map/ppermute | solution.py:306
  134.1 5.5 %shard_map.56.refs_1_ = f32[3072,256]{1,0:T(8,128)S(1)} custom-call(s32[3]{0:T(128)S(1)} %get-tuple-element.103.s, bf16[6144,1536]{1,0:T(8,128)(2,1)} %bitcast.29, bf16[1536,256]{1,0:T(8,128)(2,1)S(1)} %get-tuple-element.81.refs_0_), custom_call_target="tpu_custom_call" | custom-call | flops 589824 | bytes 2304 | tf_op jit(solution)/shard_map/pallas_call | solution.py:90
  141.3 8.1 %shard_map.57 = (f32[3072,256]{1,0:T(8,128)S(1)}, bf16[3072,256]{1,0:T(8,128)(2,1)}) custom-call(s32[3]{0:T(128)S(1)} %get-tuple-element.103.s, bf16[6144,1536]{1,0:T(8,128)(2,1)} %bitcast.30, bf16[1536,256]{1,0:T(8,128)(2,1)S(1)} %collective-permute-done.11.refs_0_, f32[3072,256]{1,0:T(8,128)} %copy-done.4), custom_call_target="tpu_custom_call" | custom-call | flops 589824 | bytes 2304 | tf_op jit(solution)/shard_map/pallas_call | solution.py:90
  160.3 11.1 %collective-permute-done.17.refs_0_ = bf16[384,256]{1,0:T(8,128)(2,1)S(1)} collective-permute-done((bf16[384,256]{1,0:T(8,128)(2,1)S(1)}, bf16[384,256]{1,0:T(8,128)(2,1)S(1)}, u32[]{:S(2)}, u32[]{:S(2)}) %collective-permute-start.17) | collective-permute-done | bytes 196640 | tf_op jit(solution)/shard_map/ppermute | solution.py:420
  171.4 4.5 %collective-permute-start.20 = (bf16[384,256]{1,0:T(8,128)(2,1)S(1)}, bf16[384,256]{1,0:T(8,128)(2,1)S(1)}, u32[]{:S(2)}, u32[]{:S(2)}) collective-permute-start(bf16[384,256]{1,0:T(8,128)(2,1)S(1)} %collective-permute-done.17.refs_0_), channel_id=1, source_target_pairs={{16,28},{20,24},{24,20},{28,16},{17,29},{21,25},{25,21},{29,17},{1... | collective-permute-start | bytes 589832 | tf_op jit(solution)/shard_map/ppermute | solution.py:306
  182.9 8.7 %collective-permute-done.19.refs_2_ = bf16[384,256]{1,0:T(8,128)(2,1)S(1)} collective-permute-done((bf16[384,256]{1,0:T(8,128)(2,1)S(1)}, bf16[384,256]{1,0:T(8,128)(2,1)S(1)}, u32[]{:S(2)}, u32[]{:S(2)}) %collective-permute-start.19) | collective-permute-done | bytes 196640 | tf_op jit(solution)/shard_map/ppermute | solution.py:306
  195.7 5.5 %shard_map.61.refs_1_ = f32[3072,256]{1,0:T(8,128)S(1)} custom-call(s32[3]{0:T(128)S(1)} %get-tuple-element.103.s, bf16[6144,1536]{1,0:T(8,128)(2,1)} %bitcast.31, bf16[1536,256]{1,0:T(8,128)(2,1)S(1)} %get-tuple-element.91.refs_0_), custom_call_target="tpu_custom_call" | custom-call | flops 589824 | bytes 2304 | tf_op jit(solution)/shard_map/pallas_call | solution.py:90
  202.8 6.8 %shard_map.62 = (f32[3072,256]{1,0:T(8,128)S(1)}, bf16[3072,256]{1,0:T(8,128)(2,1)S(1)}) custom-call(s32[3]{0:T(128)S(1)} %get-tuple-element.103.s, bf16[6144,1536]{1,0:T(8,128)(2,1)} %bitcast.32, bf16[1536,256]{1,0:T(8,128)(2,1)S(1)} %collective-permute-done.21.refs_0_, f32[3072,256]{1,0:T(8,128)} %copy-done.3), custom_call_target="tpu_custom_call" | custom-call | flops 589824 | bytes 2304 | tf_op jit(solution)/shard_map/pallas_call | solution.py:90
  209.6 6.7 %shard_map.63 = (f32[1536,256]{1,0:T(8,128)S(1)}, bf16[3072,256]{1,0:T(8,128)(2,1)S(1)}) custom-call(s32[3]{0:T(128)S(1)} %get-tuple-element.103.s, bf16[1536,6144]{1,0:T(8,128)(2,1)} %bitcast.20, f32[3072,256]{1,0:T(8,128)S(1)} %get-tuple-element.94.refs_0_, bf16[3072,256]{1,0:T(8,128)(2,1)S(1)} %collective-permute-done.22.refs_1_, f32[3072,256]{1,0:T(8,128)} %copy-done.2), custom_call_target="tpu_custom_call" | custom-call | flops 589824 | bytes 2304 | tf_op jit(solution)/shard_map/pallas_call | solution.py:90
  222.2 5.5 %shard_map.64 = (bf16[384,256]{1,0:T(8,128)(2,1)S(1)}, bf16[384,256]{1,0:T(8,128)(2,1)S(1)}, bf16[384,256]{1,0:T(8,128)(2,1)S(1)}, f32[384,256]{1,0:T(8,128)S(1)}) custom-call(s32[3]{0:T(128)S(1)} %get-tuple-element.103.s, bf16[1536,6144]{1,0:T(8,128)(2,1)} %bitcast.21, bf16[3072,256]{1,0:T(8,128)(2,1)S(1)} %get-tuple-element.95.refs_0_, ...), custom_call_target="tpu_custom_call" | custom-call | flops 589824 | bytes 2304 | tf_op jit(solution)/shard_map/pallas_call | solution.py:90
  236.9 8.9 %collective-permute-done.25 = bf16[384,256]{1,0:T(8,128)(2,1)S(1)} collective-permute-done((bf16[384,256]{1,0:T(8,128)(2,1)S(1)}, bf16[384,256]{1,0:T(8,128)(2,1)S(1)}, u32[]{:S(2)}, u32[]{:S(2)}) %collective-permute-start.25) | collective-permute-done | bytes 196640 | tf_op jit(solution)/shard_map/ppermute | solution.py:306
  250.0 7.0 %collective-permute-done.30.refs_1_ = bf16[3072,256]{1,0:T(8,128)(2,1)S(1)} collective-permute-done((bf16[3072,256]{1,0:T(8,128)(2,1)S(1)}, bf16[3072,256]{1,0:T(8,128)(2,1)S(1)}, u32[]{:S(2)}, u32[]{:S(2)}) %collective-permute-start.30) | collective-permute-done | bytes 1572896 | tf_op jit(solution)/shard_map/ppermute | solution.py:306
  257.0 6.7 %shard_map.66 = (f32[1536,256]{1,0:T(8,128)S(1)}, bf16[3072,256]{1,0:T(8,128)(2,1)S(1)}) custom-call(s32[3]{0:T(128)S(1)} %get-tuple-element.103.s, bf16[1536,6144]{1,0:T(8,128)(2,1)} %bitcast.22, f32[3072,256]{1,0:T(8,128)S(1)} %get-tuple-element.104.refs_0_, bf16[3072,256]{1,0:T(8,128)(2,1)S(1)} %collective-permute-done.30.refs_1_, f32[3072,256]{1,0:T(8,128)} %copy-done.1), custom_call_target="tpu_custom_call" | custom-call | flops 589824 | bytes 2304 | tf_op jit(solution)/shard_map/pallas_call | solution.py:90
  269.0 5.8 %shard_map.67 = (bf16[384,256]{1,0:T(8,128)(2,1)S(1)}, bf16[384,256]{1,0:T(8,128)(2,1)S(1)}, bf16[384,256]{1,0:T(8,128)(2,1)S(1)}, f32[384,256]{1,0:T(8,128)S(1)}) custom-call(s32[3]{0:T(128)S(1)} %get-tuple-element.103.s, bf16[1536,6144]{1,0:T(8,128)(2,1)} %bitcast.23, bf16[3072,256]{1,0:T(8,128)(2,1)S(1)} %get-tuple-element.106.refs_0_, ...), custom_call_target="tpu_custom_call" | custom-call | flops 589824 | bytes 2304 | tf_op jit(solution)/shard_map/pallas_call | solution.py:90
  286.9 6.8 %collective-permute-done.33 = bf16[384,256]{1,0:T(8,128)(2,1)S(1)} collective-permute-done((bf16[384,256]{1,0:T(8,128)(2,1)S(1)}, bf16[384,256]{1,0:T(8,128)(2,1)S(1)}, u32[]{:S(2)}, u32[]{:S(2)}) %collective-permute-start.33) | collective-permute-done | bytes 196640 | tf_op jit(solution)/shard_map/ppermute | solution.py:306
  293.7 7.9 %collective-permute-done.32 = bf16[384,256]{1,0:T(8,128)(2,1)S(1)} collective-permute-done((bf16[384,256]{1,0:T(8,128)(2,1)S(1)}, bf16[384,256]{1,0:T(8,128)(2,1)S(1)}, u32[]{:S(2)}, u32[]{:S(2)}) %collective-permute-start.32) | collective-permute-done | bytes 196640 | tf_op jit(solution)/shard_map/ppermute | solution.py:306
  303.0 5.1 %collective-permute-start.36 = (bf16[384,256]{1,0:T(8,128)(2,1)S(1)}, bf16[384,256]{1,0:T(8,128)(2,1)S(1)}, u32[]{:S(2)}, u32[]{:S(2)}) collective-permute-start(bf16[384,256]{1,0:T(8,128)(2,1)S(1)} %fusion.1.refs_3_), channel_id=1, source_target_pairs={{0,8},{4,12},{8,0},{12,4},{1,9},{5,13},{9,1},{13,5},{2,10},{6,14},... | collective-permute-start | bytes 589832 | tf_op jit(solution)/shard_map/ppermute | solution.py:310
  308.1 11.0 %collective-permute-start.35 = (bf16[384,256]{1,0:T(8,128)(2,1)S(1)}, bf16[384,256]{1,0:T(8,128)(2,1)S(1)}, u32[]{:S(2)}, u32[]{:S(2)}) collective-permute-start(bf16[384,256]{1,0:T(8,128)(2,1)S(1)} %fusion.1.refs_3_), channel_id=1, source_target_pairs={{0,4},{4,0},{8,12},{12,8},{1,5},{5,1},{9,13},{13,9},{2,6},{6,2},{1... | collective-permute-start | bytes 589832 | tf_op jit(solution)/shard_map/ppermute | solution.py:310
  325.5 5.6 %collective-permute-done.36.refs_5_ = bf16[384,256]{1,0:T(8,128)(2,1)S(1)} collective-permute-done((bf16[384,256]{1,0:T(8,128)(2,1)S(1)}, bf16[384,256]{1,0:T(8,128)(2,1)S(1)}, u32[]{:S(2)}, u32[]{:S(2)}) %collective-permute-start.36) | collective-permute-done | bytes 196640 | tf_op jit(solution)/shard_map/ppermute | solution.py:310
  (109 shorter events, 102.4 us)
Async XLA Ops:
  20.9 17.6 %collective-permute-start.2 = (bf16[3072,256]{1,0:T(8,128)(2,1)}, bf16[3072,256]{1,0:T(8,128)(2,1)}, u32[]{:S(2)}, u32[]{:S(2)}) collective-permute-start(bf16[3072,256]{1,0:T(8,128)(2,1)} %get-tuple-element.66), channel_id=1, source_target_pairs={{0,2},{1,3},{2,0},{3,1},{4,6},{5,7},{6,4},{7,5},{8,10},{9,11},{10,... | collective-permute-start | bytes 4718600 | tf_op jit(solution)/shard_map/ppermute | solution.py:306
  45.7 103.8 %collective-permute-start.12 = (bf16[3072,256]{1,0:T(8,128)(2,1)}, bf16[3072,256]{1,0:T(8,128)(2,1)}, u32[]{:S(2)}, u32[]{:S(2)}) collective-permute-start(bf16[3072,256]{1,0:T(8,128)(2,1)} %get-tuple-element.84), channel_id=1, source_target_pairs={{0,2},{1,3},{2,0},{3,1},{4,6},{5,7},{6,4},{7,5},{8,10},{9,11},{10,... | collective-permute-start | bytes 4718600 | tf_op jit(solution)/shard_map/ppermute | solution.py:306
  47.6 60.7 %collective-permute-start.7 = (bf16[384,256]{1,0:T(8,128)(2,1)S(1)}, bf16[384,256]{1,0:T(8,128)(2,1)S(1)}, u32[]{:S(2)}, u32[]{:S(2)}) collective-permute-start(bf16[384,256]{1,0:T(8,128)(2,1)S(1)} %add_convert_fusion.3), channel_id=1, source_target_pairs={{0,16},{1,17},{2,18},{3,19},{4,20},{5,21},{6,22},{7,23},{8,24},{9,... | collective-permute-start | bytes 589832 | tf_op jit(solution)/shard_map/ppermute | solution.py:420
  108.3 10.8 %collective-permute-start.10 = (bf16[384,256]{1,0:T(8,128)(2,1)S(1)}, bf16[384,256]{1,0:T(8,128)(2,1)S(1)}, u32[]{:S(2)}, u32[]{:S(2)}) collective-permute-start(bf16[384,256]{1,0:T(8,128)(2,1)S(1)} %collective-permute-done.7.refs_0_), channel_id=1, source_target_pairs={{16,28},{20,24},{24,20},{28,16},{17,29},{21,25},{25,21},{29,17},{1... | collective-permute-start | bytes 589832 | tf_op jit(solution)/shard_map/ppermute | solution.py:306
  113.7 16.6 %collective-permute-start.9 = (bf16[384,256]{1,0:T(8,128)(2,1)S(1)}, bf16[384,256]{1,0:T(8,128)(2,1)S(1)}, u32[]{:S(2)}, u32[]{:S(2)}) collective-permute-start(bf16[384,256]{1,0:T(8,128)(2,1)S(1)} %collective-permute-done.7.refs_0_), channel_id=1, source_target_pairs={{16,24},{20,28},{24,16},{28,20},{17,25},{21,29},{25,17},{29,21},{1... | collective-permute-start | bytes 589832 | tf_op jit(solution)/shard_map/ppermute | solution.py:306
  115.6 14.6 %collective-permute-start.8 = (bf16[384,256]{1,0:T(8,128)(2,1)S(1)}, bf16[384,256]{1,0:T(8,128)(2,1)S(1)}, u32[]{:S(2)}, u32[]{:S(2)}) collective-permute-start(bf16[384,256]{1,0:T(8,128)(2,1)S(1)} %collective-permute-done.7.refs_0_), channel_id=1, source_target_pairs={{16,20},{20,16},{24,28},{28,24},{17,21},{21,17},{25,29},{29,25},{1... | collective-permute-start | bytes 589832 | tf_op jit(solution)/shard_map/ppermute | solution.py:306
  155.4 54.2 %collective-permute-start.22 = (bf16[3072,256]{1,0:T(8,128)(2,1)}, bf16[3072,256]{1,0:T(8,128)(2,1)S(1)}, u32[]{:S(2)}, u32[]{:S(2)}) collective-permute-start(bf16[3072,256]{1,0:T(8,128)(2,1)} %get-tuple-element.82), channel_id=1, source_target_pairs={{16,18},{17,19},{18,16},{19,17},{20,22},{21,23},{22,20},{23,21},{2... | collective-permute-start | bytes 4718600 | tf_op jit(solution)/shard_map/ppermute | solution.py:306
  159.0 12.4 %collective-permute-start.17 = (bf16[384,256]{1,0:T(8,128)(2,1)S(1)}, bf16[384,256]{1,0:T(8,128)(2,1)S(1)}, u32[]{:S(2)}, u32[]{:S(2)}) collective-permute-start(bf16[384,256]{1,0:T(8,128)(2,1)S(1)} %add_convert_fusion.2), channel_id=1, source_target_pairs={{0,16},{1,17},{2,18},{3,19},{4,20},{5,21},{6,22},{7,23},{8,24},{9,... | collective-permute-start | bytes 589832 | tf_op jit(solution)/shard_map/ppermute | solution.py:420
  171.4 11.6 %collective-permute-start.20 = (bf16[384,256]{1,0:T(8,128)(2,1)S(1)}, bf16[384,256]{1,0:T(8,128)(2,1)S(1)}, u32[]{:S(2)}, u32[]{:S(2)}) collective-permute-start(bf16[384,256]{1,0:T(8,128)(2,1)S(1)} %collective-permute-done.17.refs_0_), channel_id=1, source_target_pairs={{16,28},{20,24},{24,20},{28,16},{17,29},{21,25},{25,21},{29,17},{1... | collective-permute-start | bytes 589832 | tf_op jit(solution)/shard_map/ppermute | solution.py:306
  175.9 15.7 %collective-permute-start.19 = (bf16[384,256]{1,0:T(8,128)(2,1)S(1)}, bf16[384,256]{1,0:T(8,128)(2,1)S(1)}, u32[]{:S(2)}, u32[]{:S(2)}) collective-permute-start(bf16[384,256]{1,0:T(8,128)(2,1)S(1)} %collective-permute-done.17.refs_0_), channel_id=1, source_target_pairs={{16,24},{20,28},{24,16},{28,20},{17,25},{21,29},{25,17},{29,21},{1... | collective-permute-start | bytes 589832 | tf_op jit(solution)/shard_map/ppermute | solution.py:306
  177.8 13.8 %collective-permute-start.18 = (bf16[384,256]{1,0:T(8,128)(2,1)S(1)}, bf16[384,256]{1,0:T(8,128)(2,1)S(1)}, u32[]{:S(2)}, u32[]{:S(2)}) collective-permute-start(bf16[384,256]{1,0:T(8,128)(2,1)S(1)} %collective-permute-done.17.refs_0_), channel_id=1, source_target_pairs={{16,20},{20,16},{24,28},{28,24},{17,21},{21,17},{25,29},{29,25},{1... | collective-permute-start | bytes 589832 | tf_op jit(solution)/shard_map/ppermute | solution.py:306
  218.8 38.2 %collective-permute-start.30 = (bf16[3072,256]{1,0:T(8,128)(2,1)S(1)}, bf16[3072,256]{1,0:T(8,128)(2,1)S(1)}, u32[]{:S(2)}, u32[]{:S(2)}) collective-permute-start(bf16[3072,256]{1,0:T(8,128)(2,1)S(1)} %get-tuple-element.105), channel_id=1, source_target_pairs={{16,18},{17,19},{18,16},{19,17},{20,22},{21,23},{22,20},{23,21},{2... | collective-permute-start | bytes 4718600 | tf_op jit(solution)/shard_map/ppermute | solution.py:306
  227.7 18.1 %collective-permute-start.25 = (bf16[384,256]{1,0:T(8,128)(2,1)S(1)}, bf16[384,256]{1,0:T(8,128)(2,1)S(1)}, u32[]{:S(2)}, u32[]{:S(2)}) collective-permute-start(bf16[384,256]{1,0:T(8,128)(2,1)S(1)} %get-tuple-element.100), channel_id=1, source_target_pairs={{16,24},{20,28},{24,16},{28,20},{17,25},{21,29},{25,17},{29,21},{1... | collective-permute-start | bytes 589832 | tf_op jit(solution)/shard_map/ppermute | solution.py:306
  229.6 16.2 %collective-permute-start.26 = (bf16[384,256]{1,0:T(8,128)(2,1)S(1)}, bf16[384,256]{1,0:T(8,128)(2,1)S(1)}, u32[]{:S(2)}, u32[]{:S(2)}) collective-permute-start(bf16[384,256]{1,0:T(8,128)(2,1)S(1)} %get-tuple-element.101), channel_id=1, source_target_pairs={{16,28},{20,24},{24,20},{28,16},{17,29},{21,25},{25,21},{29,17},{1... | collective-permute-start | bytes 589832 | tf_op jit(solution)/shard_map/ppermute | solution.py:306
  234.2 15.7 %collective-permute-start.24 = (bf16[384,256]{1,0:T(8,128)(2,1)S(1)}, bf16[384,256]{1,0:T(8,128)(2,1)S(1)}, u32[]{:S(2)}, u32[]{:S(2)}) collective-permute-start(bf16[384,256]{1,0:T(8,128)(2,1)S(1)} %get-tuple-element.98), channel_id=1, source_target_pairs={{16,20},{20,16},{24,28},{28,24},{17,21},{21,17},{25,29},{29,25},{1... | collective-permute-start | bytes 589832 | tf_op jit(solution)/shard_map/ppermute | solution.py:306
  274.8 18.9 %collective-permute-start.33 = (bf16[384,256]{1,0:T(8,128)(2,1)S(1)}, bf16[384,256]{1,0:T(8,128)(2,1)S(1)}, u32[]{:S(2)}, u32[]{:S(2)}) collective-permute-start(bf16[384,256]{1,0:T(8,128)(2,1)S(1)} %get-tuple-element.111), channel_id=1, source_target_pairs={{16,24},{20,28},{24,16},{28,20},{17,25},{21,29},{25,17},{29,21},{1... | collective-permute-start | bytes 589832 | tf_op jit(solution)/shard_map/ppermute | solution.py:306
  276.9 16.9 %collective-permute-start.34 = (bf16[384,256]{1,0:T(8,128)(2,1)S(1)}, bf16[384,256]{1,0:T(8,128)(2,1)S(1)}, u32[]{:S(2)}, u32[]{:S(2)}) collective-permute-start(bf16[384,256]{1,0:T(8,128)(2,1)S(1)} %get-tuple-element.112), channel_id=1, source_target_pairs={{16,28},{20,24},{24,20},{28,16},{17,29},{21,25},{25,21},{29,17},{1... | collective-permute-start | bytes 589832 | tf_op jit(solution)/shard_map/ppermute | solution.py:306
  281.4 20.2 %collective-permute-start.32 = (bf16[384,256]{1,0:T(8,128)(2,1)S(1)}, bf16[384,256]{1,0:T(8,128)(2,1)S(1)}, u32[]{:S(2)}, u32[]{:S(2)}) collective-permute-start(bf16[384,256]{1,0:T(8,128)(2,1)S(1)} %get-tuple-element.109), channel_id=1, source_target_pairs={{16,20},{20,16},{24,28},{28,24},{17,21},{21,17},{25,29},{29,25},{1... | collective-permute-start | bytes 589832 | tf_op jit(solution)/shard_map/ppermute | solution.py:306
  284.2 23.9 %collective-permute-start.29 = (bf16[384,256]{1,0:T(8,128)(2,1)S(1)}, bf16[384,256]{1,0:T(8,128)(2,1)S(1)}, u32[]{:S(2)}, u32[]{:S(2)}) collective-permute-start(bf16[384,256]{1,0:T(8,128)(2,1)S(1)} %fusion.refs_2_), channel_id=1, source_target_pairs={{0,12},{4,8},{8,4},{12,0},{1,13},{5,9},{9,5},{13,1},{2,14},{6,10},... | collective-permute-start | bytes 589832 | tf_op jit(solution)/shard_map/ppermute | solution.py:310
  286.9 35.9 %collective-permute-start.28 = (bf16[384,256]{1,0:T(8,128)(2,1)S(1)}, bf16[384,256]{1,0:T(8,128)(2,1)S(1)}, u32[]{:S(2)}, u32[]{:S(2)}) collective-permute-start(bf16[384,256]{1,0:T(8,128)(2,1)S(1)} %fusion.refs_2_), channel_id=1, source_target_pairs={{0,8},{4,12},{8,0},{12,4},{1,9},{5,13},{9,1},{13,5},{2,10},{6,14},... | collective-permute-start | bytes 589832 | tf_op jit(solution)/shard_map/ppermute | solution.py:310
  293.7 29.0 %collective-permute-start.27 = (bf16[384,256]{1,0:T(8,128)(2,1)S(1)}, bf16[384,256]{1,0:T(8,128)(2,1)S(1)}, u32[]{:S(2)}, u32[]{:S(2)}) collective-permute-start(bf16[384,256]{1,0:T(8,128)(2,1)S(1)} %fusion.refs_2_), channel_id=1, source_target_pairs={{0,4},{4,0},{8,12},{12,8},{1,5},{5,1},{9,13},{13,9},{2,6},{6,2},{1... | collective-permute-start | bytes 589832 | tf_op jit(solution)/shard_map/ppermute | solution.py:310
  301.7 23.8 %collective-permute-start.37 = (bf16[384,256]{1,0:T(8,128)(2,1)S(1)}, bf16[384,256]{1,0:T(8,128)(2,1)S(1)}, u32[]{:S(2)}, u32[]{:S(2)}) collective-permute-start(bf16[384,256]{1,0:T(8,128)(2,1)S(1)} %fusion.1.refs_3_), channel_id=1, source_target_pairs={{0,12},{4,8},{8,4},{12,0},{1,13},{5,9},{9,5},{13,1},{2,14},{6,10},... | collective-permute-start | bytes 589832 | tf_op jit(solution)/shard_map/ppermute | solution.py:310
  303.0 28.1 %collective-permute-start.36 = (bf16[384,256]{1,0:T(8,128)(2,1)S(1)}, bf16[384,256]{1,0:T(8,128)(2,1)S(1)}, u32[]{:S(2)}, u32[]{:S(2)}) collective-permute-start(bf16[384,256]{1,0:T(8,128)(2,1)S(1)} %fusion.1.refs_3_), channel_id=1, source_target_pairs={{0,8},{4,12},{8,0},{12,4},{1,9},{5,13},{9,1},{13,5},{2,10},{6,14},... | collective-permute-start | bytes 589832 | tf_op jit(solution)/shard_map/ppermute | solution.py:310
  308.1 23.0 %collective-permute-start.35 = (bf16[384,256]{1,0:T(8,128)(2,1)S(1)}, bf16[384,256]{1,0:T(8,128)(2,1)S(1)}, u32[]{:S(2)}, u32[]{:S(2)}) collective-permute-start(bf16[384,256]{1,0:T(8,128)(2,1)S(1)} %fusion.1.refs_3_), channel_id=1, source_target_pairs={{0,4},{4,0},{8,12},{12,8},{1,5},{5,1},{9,13},{13,9},{2,6},{6,2},{1... | collective-permute-start | bytes 589832 | tf_op jit(solution)/shard_map/ppermute | solution.py:310
  (27 other events, 322.0 us)
where the time goes:
time: 335 us; the launch traced here: 334 us
  waiting for transfers between devices  140 us (42%)
  Pallas kernels  93.2 us (28%)
  starting transfers between devices  87.4 us (26%)
  local copies, waits for them, and re-layouts  7.26 us (2%)
  other arithmetic  5.59 us (2%)
    ppermute x2, waiting for transfers between devices, cross(): crossed = lax.ppermute(terms[k], 'section', [(0, 1)])  70.5 us
    ppermute x30, starting transfers between devices, within(): return lax.ppermute(block, ('section', axis), pairs)  64.8 us
    ppermute x30, waiting for transfers between devices, within(): return lax.ppermute(block, ('section', axis), pairs)  60.1 us
    pallas_call x16, Pallas kernels, product(): pl.pallas_call(body, in_specs=[SMEM, ANY] + [VMEM] * (count + (base is no...  57.6 us
    ppermute x6, starting transfers between devices, everywhere(): return lax.ppermute(block, axis, [(i, i ^ distance) for i in range(size)])  20 us
    pallas_call x1, Pallas kernels, split_rows(): pl.pallas_call(body, in_specs=[SMEM, ANY], out_specs=ANY, out_shape=jax.S...  14.2 us
    pallas_call x2, Pallas kernels, slope_of(): pl.pallas_call(body, grid_spec=pltpu.PrefetchScalarGridSpec(num_scalar_pr...  13.6 us
    ppermute x6, waiting for transfers between devices, everywhere(): return lax.ppermute(block, axis, [(i, i ^ distance) for i in range(size)])  9.27 us
  transfers between devices with their start and end apart: 38, of which 14 were waited for; matrix products, arithmetic and copies ran while one was open for 0% of the time, Pallas kernels for 17%

commit v1 on v0

--- a/solution.py
+++ b/solution.py
@@ -33,7 +33,7 @@
 ANY = pl.BlockSpec(memory_space=pl.ANY)
 
 
-def product(flags, mat, block, place, steps, sources, prepare, tokens, outs, base=None, base_row=None, apart=False):
+def product(flags, mat, block, place, steps, sources, prepare, tokens, outs, base=None, base_row=None, apart=False, first=None):
     rows, depth = block
     slots = min(4, steps)
     bare = prepare is None
@@ -44,6 +44,9 @@
         base_ref = None
         if base is not None:
             base_ref, refs = refs[0], refs[1:]
+        if first is not None:
+            chunk_ref, chunk_sem = refs[-2:]
+            refs = refs[:-2]
         out_refs, (buf, sem) = refs[:-2], refs[-2:]
 
         def fetch(i):
@@ -54,12 +57,20 @@
 
         @pl.when(s[0] == 1)
         def _():
+            given = source_refs
+            if first is not None:
+                piece = source_refs[0].at[pl.ds(first, tokens)]
+                chunk = pltpu.make_async_copy(piece, chunk_ref, chunk_sem)
+                chunk.start()
+                given = [chunk_ref]
             for i in range(slots):
                 fetch(i).start()
+            if first is not None:
+                chunk.wait()
             right_ref = source_refs[0]
             if not bare:
                 right_ref = out_refs[-1]
-                prepare(right_ref, *source_refs)
+                prepare(right_ref, *given)
 
             @pl.loop(0, steps)
             def _(i):
@@ -80,22 +91,28 @@
                         def _(ref=ref):
                             ref[...] = got.astype(ref.dtype)
                 else:
-                    at = pl.ds(pl.multiple_of(i * rows, 16), rows)
-                    for ref in out_refs[: len(outs)]:
-                        ref[at] = got.astype(ref.dtype)
-
-    shapes = [jax.ShapeDtypeStruct((size, tokens), kind) for size, kind in outs]
+                    for ref, (size, begin, _) in zip(out_refs, outs):
+
+                        @pl.when((i * rows >= begin) & (i * rows < begin + size))
+                        def _(ref=ref, begin=begin):
+                            at = pl.multiple_of(i * rows - begin, 16)
+                            ref[pl.ds(at, rows)] = got.astype(ref.dtype)
+
+    shapes = [jax.ShapeDtypeStruct((size, tokens), kind) for size, _, kind in outs]
     if not bare:
         shapes.append(jax.ShapeDtypeStruct((depth, tokens), LOW))
     return pl.pallas_call(
         body,
-        in_specs=[SMEM, ANY] + [VMEM] * (count + (base is not None)),
+        in_specs=[SMEM, ANY]
+        + [VMEM if first is None else ANY] * count
+        + [VMEM] * (base is not None),
         out_specs=[VMEM] * len(shapes),
         out_shape=shapes,
         scratch_shapes=[
             pltpu.VMEM((slots, rows, depth), LOW),
             pltpu.SemaphoreType.DMA((slots,)),
-        ],
+        ]
+        + ([] if first is None else [pltpu.VMEM((tokens, depth), F32), pltpu.SemaphoreType.DMA(())]),
         compiler_params=params(),
         cost_estimate=pl.CostEstimate(
             flops=2 * tokens * rows * depth * steps // WEIGHT,
@@ -109,9 +126,31 @@
     right_ref[...] = grad_ref[...].T.astype(LOW)
 
 
-def hidden_of(right_ref, own_ref, other_ref, slope_ref):
-    total = own_ref[...] + other_ref[...].astype(F32)
-    right_ref[...] = (total * slope_ref[...]).astype(LOW)
+def hidden_of(right_ref, own_ref, slope_ref, *other_refs):
+    row = 0
+    for other_ref in other_refs:
+        at = slice(row, row + other_ref.shape[0])
+        total = own_ref[at] + other_ref[...].astype(F32)
+        right_ref[at] = (total * slope_ref[at]).astype(LOW)
+        row = at.stop
+
+
+def hidden(flags, own, slope, others):
+    def body(s, own_ref, slope_ref, *refs):
+        @pl.when(s[0] == 1)
+        def _():
+            hidden_of(refs[-1], own_ref, slope_ref, *refs[:-1])
+
+    return pl.pallas_call(
+        body,
+        in_specs=[SMEM] + [VMEM] * (2 + len(others)),
+        out_specs=VMEM,
+        out_shape=jax.ShapeDtypeStruct(own.shape, LOW),
+        compiler_params=params(),
+        cost_estimate=pl.CostEstimate(
+            flops=own.size // WEIGHT, bytes_accessed=own.size // WEIGHT, transcendentals=0
+        ),
+    )(flags, own, slope, *others)
 
 
 def split_rows(flags, mat):
@@ -325,22 +364,31 @@
 
     split_out = split_rows(up, mat_out)
 
-    hid_rows = divisor(half, 512)
+    hid_rows = divisor(half // 2, 512)
     hid_steps = half // hid_rows
     part_rows = quarter // PARTS
 
-    def product_out(flags, mat, first_row, sources, prepare, tokens, kinds, base=None):
+    def product_out(flags, mat, first_row, sources, prepare, tokens, outs, base=None, first=None):
         return product(
             flags, mat, (hid_rows, quarter),
             lambda i, s: (first_row(s) + i * hid_rows, 0), hid_steps,
-            sources, prepare, tokens, [(half, kind) for kind in kinds],
-            base, lambda i, s: i * hid_rows,
-        )
+            sources, prepare, tokens, outs, base, lambda i, s: i * hid_rows, first=first,
+        )
+
+    def in_pieces(k):
+        count = 1 if k == 0 else 2
+        size = half // count
+        return [(half, 0, F32)] + [(size, n * size, LOW) for n in range(count)]
+
+    def exchange(k, active, pieces, earlier):
+        if k > 0:
+            pieces = [lax.optimization_barrier((piece, earlier))[0] for piece in pieces]
+        return [within(active, 2, piece) for piece in pieces]
 
     def product_in(flags, place, sources, prepare, tokens, kind):
         return product(
             flags, mat_in, (part_rows, half), place, PARTS, sources, prepare, tokens,
-            [(quarter, kind)],
+            [(quarter, 0, kind)],
         )
 
     def product_parts(flags, place, right, tokens, base):
@@ -349,7 +397,7 @@
 
         return product(
             flags, mat_in, (part_rows, half), lambda i, s: place(part_of(i, s), s), PARTS,
-            [right], None, tokens, [(part_rows, LOW)] * 3 + [(part_rows, F32)],
+            [right], None, tokens, [(part_rows, 0, LOW)] * 3 + [(part_rows, 0, F32)],
             base, lambda i, s: part_of(i, s) * part_rows, True,
         )
 
@@ -381,21 +429,20 @@
 
     def down_send(k):
         sent, lows[k] = product_out(
-            steps.after(down), mat_out, lambda s: (1 - s[1]) * half, [grads[k]], turned,
-            sizes[k], (LOW,),
+            steps.after(down), mat_out, lambda s: (1 - s[1]) * half, [grad], turned,
+            sizes[k], [(half, 0, LOW)], first=starts[k],
         )
         steps.last = sent
         core_got[k] = within(0, 1, sent)
 
     def down_hidden(k):
-        full, low_grad = product_out(
+        full, *pieces = product_out(
             steps.after(down), mat_out, lambda s: s[1] * half, [lows[k]], None, sizes[k],
-            (F32, LOW), core_got[k],
-        )
-        steps.last = low_grad
-        if k > 0:
-            low_grad = lax.optimization_barrier((low_grad, hidden_other[k - 1]))[0]
-        hidden_full[k], hidden_other[k] = full, within(0, 2, low_grad)
+            in_pieces(k), core_got[k],
+        )
+        steps.last = full
+        hidden_full[k] = full
+        hidden_other[k] = exchange(k, 0, pieces, hidden_other[k - 1][-1] if k else None)
 
     def slope(k):
         slopes[k] = slope_of(steps.after(down), pre, starts[k], sizes[k], half)
@@ -403,11 +450,10 @@
 
     def down_back(k):
         tokens = sizes[k]
-        full = steps.after(hidden_full[k])
-        hidden = ((full + hidden_other[k].astype(F32)) * slopes[k]).astype(LOW)
-        swapped = within(0, 1, hidden)
+        right = hidden(steps.after(down), hidden_full[k], slopes[k], hidden_other[k])
+        swapped = within(0, 1, right)
         (partial,) = product_in(
-            down, lambda i, s: (i * part_rows, s[1] * half), [hidden], None, tokens, F32
+            down, lambda i, s: (i * part_rows, s[1] * half), [right], None, tokens, F32
         )
         parts_out[k] = product_parts(
             down, lambda i, s: (i * part_rows, (1 - s[1]) * half), swapped, tokens, partial
@@ -416,6 +462,8 @@
 
     def cross(k):
         *others, own = parts_out[k]
+        if k + 1 in hidden_other:
+            own = lax.optimization_barrier((own, hidden_other[k + 1][0]))[0]
         terms[k] = scatter_hid(0, others + [steps.after(own)])
         crossed = lax.ppermute(terms[k], "section", [(0, 1)])
         steps.last = crossed
@@ -426,15 +474,15 @@
         low, up_terms[k] = join(steps.after(up), grads[k], gathered[k])
         low_other = within(1, 1, low)
         (partial,) = product_out(
-            up, split_out, lambda s: s[1] * half, [low], None, tokens, (F32,)
-        )
-        full, low_grad = product_out(
-            up, split_out, lambda s: (1 - s[1]) * half, [low_other], None, tokens, (F32, LOW), partial
-        )
-        steps.last = low_grad
-        if k > 0:
-            low_grad = lax.optimization_barrier((low_grad, up_other[k - 1]))[0]
-        up_full[k], up_other[k] = full, within(1, 2, low_grad)
+            up, split_out, lambda s: s[1] * half, [low], None, tokens, [(half, 0, F32)]
+        )
+        full, *pieces = product_out(
+            up, split_out, lambda s: (1 - s[1]) * half, [low_other], None, tokens,
+            in_pieces(k), partial,
+        )
+        steps.last = full
+        up_full[k] = full
+        up_other[k] = exchange(k, 1, pieces, up_other[k - 1][-1] if k else None)
 
     def place(part, core):
         row = core * (PARTS // 2) + lax.rem(part, PARTS // 2)
@@ -442,16 +490,18 @@
 
     def up_back(k):
         tokens = sizes[k]
-        sent, hidden = product_in(
+        sent, right = product_in(
             steps.after(up), lambda i, s: place(i, 1 - s[1]),
-            [up_full[k], up_other[k], slopes[k]], hidden_of, tokens, F32,
+            [up_full[k], slopes[k]] + up_other[k], hidden_of, tokens, F32,
         )
         got = within(1, 1, sent)
-        up_parts[k] = product_parts(up, lambda i, s: place(i, s[1]), hidden, tokens, got)
+        up_parts[k] = product_parts(up, lambda i, s: place(i, s[1]), right, tokens, got)
         steps.last = up_parts[k][0]
 
     def gather(k):
         *others, own = up_parts[k]
+        if k + 1 in up_other:
+            own = lax.optimization_barrier((own, up_other[k + 1][0]))[0]
         last = jnp.where(is_up, scatter_hid(1, others + [steps.after(own)]), terms[k])
         steps.last = last
         lasts[k] = [last] + [everywhere(d, last) for d in range(1, PARTS)]
@@ -462,16 +512,20 @@
         down_hidden(k)
     for k in chunks:
         slope(k)
+    down_back(0)
+    out = None
     for k in chunks:
-        down_back(k)
         cross(k)
+        if k + 1 < len(SHARES):
+            down_back(k + 1)
         up_hidden(k)
     for k in chunks:
         up_back(k)
+        if k > 0:
+            out = finish(steps.after(up), out, grad, starts[k - 1], up_terms[k - 1], lasts[k - 1])
+            steps.last = out
         gather(k)
-    out = None
-    for k in chunks:
-        out = finish(up, out, grad, starts[k], up_terms[k], lasts[k])
+    out = finish(up, out, grad, starts[k], up_terms[k], lasts[k])
     return out.reshape(1, batches, batch_tokens, quarter)
 
 

time: 335 us -> 326 us (0.973)
  starting transfers between devices: 87.4 us -> 76.8 us
  other arithmetic: 5.59 us -> 0.53 us
  Pallas kernels: 93.2 us -> 97.6 us
    ppermute x30 -> x32, waiting for transfers between devices: 60.1 us -> 41.1 us  [within(): return lax.ppermute(block, ('section', axis), pairs)]
    ppermute x6, waiting for transfers between devices: 9.27 us -> 23.7 us  [everywhere(): return lax.ppermute(block, axis, [(i, i ^ distance) for i in range(size)])]
    ppermute x6, starting transfers between devices: 20 us -> 8.91 us  [everywhere(): return lax.ppermute(block, axis, [(i, i ^ distance) for i in range(size)])]
    pallas_call x16 -> x18, Pallas kernels: 57.6 us -> 63.5 us  [the longest x16 59.7 us: product(): pl.pallas_call(body, in_specs=[SMEM, ANY] + [VMEM if first is None else A...]
    convert_element_type x2 -> x0, other arithmetic: 5.09 us -> none  [down_back(): hidden = ((full + hidden_other[k].astype(F32)) * slopes[k]).astype(LOW)]
    ppermute x2, waiting for transfers between devices: 70.5 us -> 75.3 us  [cross(): crossed = lax.ppermute(terms[k], 'section', [(0, 1)])]
    unnamed x26 -> x18, local copies, waits for them, and re-layouts: 5.17 us -> 9.28 us
    ppermute x30 -> x32, starting transfers between devices: 64.8 us -> 65.3 us  [within(): return lax.ppermute(block, ('section', axis), pairs)]
  transfers between devices with their start and end apart: 38 -> 40, of which waited for: 14 -> 14; matrix products, arithmetic and copies ran while one was open for 0% -> 0% of each run, Pallas kernels for 17% -> 19%
where the time goes in v1:
time: 326 us; the launch traced here: 325 us
  waiting for transfers between devices  140 us (43%)
  Pallas kernels  97.6 us (30%)
  starting transfers between devices  76.8 us (24%)
  local copies, waits for them, and re-layouts  9.49 us (3%)
    ppermute x2, waiting for transfers between devices, cross(): crossed = lax.ppermute(terms[k], 'section', [(0, 1)])  75.3 us
    ppermute x32, starting transfers between devices, within(): return lax.ppermute(block, ('section', axis), pairs)  65.3 us
    pallas_call x16, Pallas kernels, product(): pl.pallas_call(body, in_specs=[SMEM, ANY] + [VMEM if first is None else A...  59.7 us
    ppermute x32, waiting for transfers between devices, within(): return lax.ppermute(block, ('section', axis), pairs)  41.1 us
    ppermute x6, waiting for transfers between devices, everywhere(): return lax.ppermute(block, axis, [(i, i ^ distance) for i in range(size)])  23.7 us
    pallas_call x1, Pallas kernels, split_rows(): pl.pallas_call(body, in_specs=[SMEM, ANY], out_specs=ANY, out_shape=jax.S...  14.5 us
    pallas_call x2, Pallas kernels, slope_of(): pl.pallas_call(body, grid_spec=pltpu.PrefetchScalarGridSpec(num_scalar_pr...  11.7 us
    unnamed x18, local copies, waits for them, and re-layouts  9.28 us
  transfers between devices with their start and end apart: 40, of which 14 were waited for; matrix products, arithmetic and copies ran while one was open for 0% of the time, Pallas kernels for 19%

profile of v1, /device:TPU:2, one launch (start us, length us, event | category | flops | bytes accessed | tf_op | source)
XLA Modules:
  0.0 325.2 jit_solution(12577174763085132170)
XLA Ops:
  0.1 14.5 %shard_map.46 = bf16[2,3072,1536]{2,1,0:T(8,128)(2,1)} custom-call(s32[3]{0:T(128)S(1)} %get-tuple-element.120.s, bf16[6144,1536]{1,0:T(8,128)(2,1)} %bitcast.26), custom_call_target="tpu_custom_call" | custom-call | flops 1179648 | bytes 9216 | tf_op jit(solution)/shard_map/pallas_call | solution.py:204
  21.7 5.9 %shard_map.51.slope_ref.refs_1_ = f32[3072,256]{1,0:T(8,128)S(1)} custom-call(s32[3]{0:T(128)S(1)} %get-tuple-element.88.s, f32[512,6144]{1,0:T(8,128)} %bitcast.35), custom_call_target="tpu_custom_call" | custom-call | flops 192 | bytes 1536 | tf_op jit(solution)/shard_map/pallas_call | solution.py:230
  29.2 5.9 %shard_map.52.slope_ref.refs_1_ = f32[3072,256]{1,0:T(8,128)S(1)} custom-call(s32[3]{0:T(128)S(1)} %get-tuple-element.88.s, f32[512,6144]{1,0:T(8,128)} %bitcast.36), custom_call_target="tpu_custom_call" | custom-call | flops 192 | bytes 1536 | tf_op jit(solution)/shard_map/pallas_call | solution.py:230
  48.2 67.7 %collective-permute-done.8.refs_0_ = bf16[384,256]{1,0:T(8,128)(2,1)S(1)} collective-permute-done((bf16[384,256]{1,0:T(8,128)(2,1)S(1)}, bf16[384,256]{1,0:T(8,128)(2,1)S(1)}, u32[]{:S(2)}, u32[]{:S(2)}) %collective-permute-start.8) | collective-permute-done | bytes 196640 | tf_op jit(solution)/shard_map/ppermute | solution.py:468
  118.5 5.4 %collective-permute-start.13 = (bf16[384,256]{1,0:T(8,128)(2,1)S(1)}, bf16[384,256]{1,0:T(8,128)(2,1)S(1)}, u32[]{:S(2)}, u32[]{:S(2)}) collective-permute-start(bf16[384,256]{1,0:T(8,128)(2,1)S(1)} %collective-permute-done.8.refs_0_), channel_id=1, source_target_pairs={{16,28},{20,24},{24,20},{28,16},{17,29},{21,25},{25,21},{29,17},{1... | collective-permute-start | bytes 589832 | tf_op jit(solution)/shard_map/ppermute | solution.py:345
  130.1 10.2 %collective-permute-done.12.refs_2_ = bf16[384,256]{1,0:T(8,128)(2,1)S(1)} collective-permute-done((bf16[384,256]{1,0:T(8,128)(2,1)S(1)}, bf16[384,256]{1,0:T(8,128)(2,1)S(1)}, u32[]{:S(2)}, u32[]{:S(2)}) %collective-permute-start.12) | collective-permute-done | bytes 196640 | tf_op jit(solution)/shard_map/ppermute | solution.py:345
  145.3 5.6 %shard_map.60.refs_1_ = f32[3072,256]{1,0:T(8,128)S(1)} custom-call(s32[3]{0:T(128)S(1)} %get-tuple-element.120.s, bf16[6144,1536]{1,0:T(8,128)(2,1)} %bitcast.31, bf16[1536,256]{1,0:T(8,128)(2,1)S(1)} %get-tuple-element.94.refs_0_), custom_call_target="tpu_custom_call" | custom-call | flops 589824 | bytes 2304 | tf_op jit(solution)/shard_map/pallas_call | solution.py:104
  152.7 8.2 %shard_map.61 = (f32[3072,256]{1,0:T(8,128)S(1)}, bf16[3072,256]{1,0:T(8,128)(2,1)}) custom-call(s32[3]{0:T(128)S(1)} %get-tuple-element.120.s, bf16[6144,1536]{1,0:T(8,128)(2,1)} %bitcast.32, bf16[1536,256]{1,0:T(8,128)(2,1)S(1)} %collective-permute-done.14.refs_0_, f32[3072,256]{1,0:T(8,128)} %copy-done.4), custom_call_target="tpu_custom_call" | custom-call | flops 589824 | bytes 2304 | tf_op jit(solution)/shard_map/pallas_call | solution.py:104
  165.8 7.6 %collective-permute-done.18.refs_0_ = bf16[384,256]{1,0:T(8,128)(2,1)S(1)} collective-permute-done((bf16[384,256]{1,0:T(8,128)(2,1)S(1)}, bf16[384,256]{1,0:T(8,128)(2,1)S(1)}, u32[]{:S(2)}, u32[]{:S(2)}) %collective-permute-start.18) | collective-permute-done | bytes 196640 | tf_op jit(solution)/shard_map/ppermute | solution.py:468
  173.4 4.5 %collective-permute-start.21 = (bf16[384,256]{1,0:T(8,128)(2,1)S(1)}, bf16[384,256]{1,0:T(8,128)(2,1)S(1)}, u32[]{:S(2)}, u32[]{:S(2)}) collective-permute-start(bf16[384,256]{1,0:T(8,128)(2,1)S(1)} %collective-permute-done.18.refs_0_), channel_id=1, source_target_pairs={{16,28},{20,24},{24,20},{28,16},{17,29},{21,25},{25,21},{29,17},{1... | collective-permute-start | bytes 589832 | tf_op jit(solution)/shard_map/ppermute | solution.py:345
  185.0 8.5 %collective-permute-done.20.refs_2_ = bf16[384,256]{1,0:T(8,128)(2,1)S(1)} collective-permute-done((bf16[384,256]{1,0:T(8,128)(2,1)S(1)}, bf16[384,256]{1,0:T(8,128)(2,1)S(1)}, u32[]{:S(2)}, u32[]{:S(2)}) %collective-permute-start.20) | collective-permute-done | bytes 196640 | tf_op jit(solution)/shard_map/ppermute | solution.py:345
  196.7 5.6 %shard_map.63.refs_1_ = f32[3072,256]{1,0:T(8,128)S(1)} custom-call(s32[3]{0:T(128)S(1)} %get-tuple-element.120.s, bf16[6144,1536]{1,0:T(8,128)(2,1)} %bitcast.33, bf16[1536,256]{1,0:T(8,128)(2,1)S(1)} %get-tuple-element.100.refs_0_), custom_call_target="tpu_custom_call" | custom-call | flops 589824 | bytes 2304 | tf_op jit(solution)/shard_map/pallas_call | solution.py:104
  204.0 8.0 %shard_map.64 = (f32[3072,256]{1,0:T(8,128)S(1)}, bf16[1536,256]{1,0:T(8,128)(2,1)}, bf16[1536,256]{1,0:T(8,128)(2,1)S(1)}) custom-call(s32[3]{0:T(128)S(1)} %get-tuple-element.120.s, bf16[6144,1536]{1,0:T(8,128)(2,1)} %bitcast.34, bf16[1536,256]{1,0:T(8,128)(2,1)S(1)} %collective-permute-done.22.refs_0_, f32[3072,256]{1,0:T(8,128)} %copy-done.3), custom_call_target="tpu_custom_call" | custom-call | flops 589824 | bytes 2304 | tf_op jit(solution)/shard_map/pallas_call | solution.py:104
  212.1 7.3 %shard_map.65 = (f32[1536,256]{1,0:T(8,128)S(1)}, bf16[3072,256]{1,0:T(8,128)(2,1)S(1)}) custom-call(s32[3]{0:T(128)S(1)} %get-tuple-element.120.s, bf16[1536,6144]{1,0:T(8,128)(2,1)} %bitcast.22, f32[3072,256]{1,0:T(8,128)S(1)} %get-tuple-element.95.refs_0_, f32[3072,256]{1,0:T(8,128)} %copy-done.2, bf16[3072,256]{1,0:T(8,128)(2,1)} %collective-permute-done.23.refs_2_), custom_call_target="tpu_custom_call" | custom-call | flops 589824 | bytes 2304 | tf_op jit(solution)/shard_map/pallas_call | solution.py:104
  227.6 5.5 %shard_map.66 = (bf16[384,256]{1,0:T(8,128)(2,1)S(1)}, bf16[384,256]{1,0:T(8,128)(2,1)S(1)}, bf16[384,256]{1,0:T(8,128)(2,1)S(1)}, f32[384,256]{1,0:T(8,128)S(1)}) custom-call(s32[3]{0:T(128)S(1)} %get-tuple-element.120.s, bf16[1536,6144]{1,0:T(8,128)(2,1)} %bitcast.23, bf16[3072,256]{1,0:T(8,128)(2,1)S(1)} %get-tuple-element.104.refs_0_, ...), custom_call_target="tpu_custom_call" | custom-call | flops 589824 | bytes 2304 | tf_op jit(solution)/shard_map/pallas_call | solution.py:104
  244.3 5.6 %collective-permute-done.27 = bf16[384,256]{1,0:T(8,128)(2,1)S(1)} collective-permute-done((bf16[384,256]{1,0:T(8,128)(2,1)S(1)}, bf16[384,256]{1,0:T(8,128)(2,1)S(1)}, u32[]{:S(2)}, u32[]{:S(2)}) %collective-permute-start.27) | collective-permute-done | bytes 196640 | tf_op jit(solution)/shard_map/ppermute | solution.py:345
  249.8 4.1 %collective-permute-done.26 = bf16[384,256]{1,0:T(8,128)(2,1)S(1)} collective-permute-done((bf16[384,256]{1,0:T(8,128)(2,1)S(1)}, bf16[384,256]{1,0:T(8,128)(2,1)S(1)}, u32[]{:S(2)}, u32[]{:S(2)}) %collective-permute-start.26) | collective-permute-done | bytes 196640 | tf_op jit(solution)/shard_map/ppermute | solution.py:345
  254.0 6.1 %collective-permute-done.29.refs_3_ = bf16[1536,256]{1,0:T(8,128)(2,1)S(1)} collective-permute-done((bf16[1536,256]{1,0:T(8,128)(2,1)S(1)}, bf16[1536,256]{1,0:T(8,128)(2,1)S(1)}, u32[]{:S(2)}, u32[]{:S(2)}) %collective-permute-start.29) | collective-permute-done | bytes 786464 | tf_op jit(solution)/shard_map/ppermute | solution.py:345
  260.2 6.8 %shard_map.67 = (f32[1536,256]{1,0:T(8,128)S(1)}, bf16[3072,256]{1,0:T(8,128)(2,1)S(1)}) custom-call(s32[3]{0:T(128)S(1)} %get-tuple-element.120.s, bf16[1536,6144]{1,0:T(8,128)(2,1)} %bitcast.24, f32[3072,256]{1,0:T(8,128)S(1)} %get-tuple-element.101.refs_0_, f32[3072,256]{1,0:T(8,128)} %copy-done.1, bf16[1536,256]{1,0:T(8,128)(2,1)S(1)} %collective-permute-done.25.refs_2_, ...), custom_call_target="tpu_custom_call" | custom-call | flops 589824 | bytes 2304 | tf_op jit(solution)/shard_map/pallas_call | solution.py:104
  273.4 5.5 %shard_map.68 = (bf16[384,256]{1,0:T(8,128)(2,1)S(1)}, bf16[384,256]{1,0:T(8,128)(2,1)S(1)}, bf16[384,256]{1,0:T(8,128)(2,1)S(1)}, f32[384,256]{1,0:T(8,128)S(1)}) custom-call(s32[3]{0:T(128)S(1)} %get-tuple-element.120.s, bf16[1536,6144]{1,0:T(8,128)(2,1)} %bitcast.25, bf16[3072,256]{1,0:T(8,128)(2,1)S(1)} %get-tuple-element.117.refs_0_, ...), custom_call_target="tpu_custom_call" | custom-call | flops 589824 | bytes 2304 | tf_op jit(solution)/shard_map/pallas_call | solution.py:104
  281.1 4.0 %collective-permute-start.36 = (bf16[384,256]{1,0:T(8,128)(2,1)S(1)}, bf16[384,256]{1,0:T(8,128)(2,1)S(1)}, u32[]{:S(2)}, u32[]{:S(2)}) collective-permute-start(bf16[384,256]{1,0:T(8,128)(2,1)S(1)} %get-tuple-element.126), channel_id=1, source_target_pairs={{16,28},{20,24},{24,20},{28,16},{17,29},{21,25},{25,21},{29,17},{1... | collective-permute-start | bytes 589832 | tf_op jit(solution)/shard_map/ppermute | solution.py:345
  288.2 8.4 %collective-permute-done.32.refs_4_ = bf16[384,256]{1,0:T(8,128)(2,1)S(1)} collective-permute-done((bf16[384,256]{1,0:T(8,128)(2,1)S(1)}, bf16[384,256]{1,0:T(8,128)(2,1)S(1)}, u32[]{:S(2)}, u32[]{:S(2)}) %collective-permute-start.32) | collective-permute-done | bytes 196640 | tf_op jit(solution)/shard_map/ppermute | solution.py:349
  307.1 4.5 %collective-permute-done.39.refs_6_ = bf16[384,256]{1,0:T(8,128)(2,1)S(1)} collective-permute-done((bf16[384,256]{1,0:T(8,128)(2,1)S(1)}, bf16[384,256]{1,0:T(8,128)(2,1)S(1)}, u32[]{:S(2)}, u32[]{:S(2)}) %collective-permute-start.39) | collective-permute-done | bytes 196640 | tf_op jit(solution)/shard_map/ppermute | solution.py:349
  311.6 10.8 %collective-permute-done.38.refs_5_ = bf16[384,256]{1,0:T(8,128)(2,1)S(1)} collective-permute-done((bf16[384,256]{1,0:T(8,128)(2,1)S(1)}, bf16[384,256]{1,0:T(8,128)(2,1)S(1)}, u32[]{:S(2)}, u32[]{:S(2)}) %collective-permute-start.38) | collective-permute-done | bytes 196640 | tf_op jit(solution)/shard_map/ppermute | solution.py:349
  (105 shorter events, 98.2 us)
Async XLA Ops:
  19.1 17.7 %collective-permute-start.2 = (bf16[3072,256]{1,0:T(8,128)(2,1)}, bf16[3072,256]{1,0:T(8,128)(2,1)S(1)}, u32[]{:S(2)}, u32[]{:S(2)}) collective-permute-start(bf16[3072,256]{1,0:T(8,128)(2,1)} %get-tuple-element.79), channel_id=1, source_target_pairs={{0,2},{1,3},{2,0},{3,1},{4,6},{5,7},{6,4},{7,5},{8,10},{9,11},{10,... | collective-permute-start | bytes 4718600 | tf_op jit(solution)/shard_map/ppermute | solution.py:345
  42.8 73.1 %collective-permute-start.9 = (bf16[1536,256]{1,0:T(8,128)(2,1)}, bf16[1536,256]{1,0:T(8,128)(2,1)S(1)}, u32[]{:S(2)}, u32[]{:S(2)}) collective-permute-start(bf16[1536,256]{1,0:T(8,128)(2,1)} %get-tuple-element.90), channel_id=1, source_target_pairs={{0,2},{1,3},{2,0},{3,1},{4,6},{5,7},{6,4},{7,5},{8,10},{9,11},{10,... | collective-permute-start | bytes 2359304 | tf_op jit(solution)/shard_map/ppermute | solution.py:345
  46.9 69.0 %collective-permute-start.8 = (bf16[384,256]{1,0:T(8,128)(2,1)S(1)}, bf16[384,256]{1,0:T(8,128)(2,1)S(1)}, u32[]{:S(2)}, u32[]{:S(2)}) collective-permute-start(bf16[384,256]{1,0:T(8,128)(2,1)S(1)} %add_convert_fusion.3), channel_id=1, source_target_pairs={{0,16},{1,17},{2,18},{3,19},{4,20},{5,21},{6,22},{7,23},{8,24},{9,... | collective-permute-start | bytes 589832 | tf_op jit(solution)/shard_map/ppermute | solution.py:468
  123.9 16.4 %collective-permute-start.12 = (bf16[384,256]{1,0:T(8,128)(2,1)S(1)}, bf16[384,256]{1,0:T(8,128)(2,1)S(1)}, u32[]{:S(2)}, u32[]{:S(2)}) collective-permute-start(bf16[384,256]{1,0:T(8,128)(2,1)S(1)} %collective-permute-done.8.refs_0_), channel_id=1, source_target_pairs={{16,24},{20,28},{24,16},{28,20},{17,25},{21,29},{25,17},{29,21},{1... | collective-permute-start | bytes 589832 | tf_op jit(solution)/shard_map/ppermute | solution.py:345
  125.9 14.5 %collective-permute-start.11 = (bf16[384,256]{1,0:T(8,128)(2,1)S(1)}, bf16[384,256]{1,0:T(8,128)(2,1)S(1)}, u32[]{:S(2)}, u32[]{:S(2)}) collective-permute-start(bf16[384,256]{1,0:T(8,128)(2,1)S(1)} %collective-permute-done.8.refs_0_), channel_id=1, source_target_pairs={{16,20},{20,16},{24,28},{28,24},{17,21},{21,17},{25,29},{29,25},{1... | collective-permute-start | bytes 589832 | tf_op jit(solution)/shard_map/ppermute | solution.py:345
  143.3 21.1 %collective-permute-start.16 = (bf16[384,256]{1,0:T(8,128)(2,1)S(1)}, bf16[384,256]{1,0:T(8,128)(2,1)S(1)}, u32[]{:S(2)}, u32[]{:S(2)}) collective-permute-start(bf16[384,256]{1,0:T(8,128)(2,1)S(1)} %get-tuple-element.97), channel_id=1, source_target_pairs={{0,8},{4,12},{8,0},{12,4},{1,9},{5,13},{9,1},{13,5},{2,10},{6,14},... | collective-permute-start | bytes 589832 | tf_op jit(solution)/shard_map/ppermute | solution.py:345
  144.0 20.4 %collective-permute-start.17 = (bf16[384,256]{1,0:T(8,128)(2,1)S(1)}, bf16[384,256]{1,0:T(8,128)(2,1)S(1)}, u32[]{:S(2)}, u32[]{:S(2)}) collective-permute-start(bf16[384,256]{1,0:T(8,128)(2,1)S(1)} %get-tuple-element.98), channel_id=1, source_target_pairs={{0,12},{4,8},{8,4},{12,0},{1,13},{5,9},{9,5},{13,1},{2,14},{6,10},... | collective-permute-start | bytes 589832 | tf_op jit(solution)/shard_map/ppermute | solution.py:345
  144.7 19.7 %collective-permute-start.15 = (bf16[384,256]{1,0:T(8,128)(2,1)S(1)}, bf16[384,256]{1,0:T(8,128)(2,1)S(1)}, u32[]{:S(2)}, u32[]{:S(2)}) collective-permute-start(bf16[384,256]{1,0:T(8,128)(2,1)S(1)} %get-tuple-element.92), channel_id=1, source_target_pairs={{0,4},{4,0},{8,12},{12,8},{1,5},{5,1},{9,13},{13,9},{2,6},{6,2},{1... | collective-permute-start | bytes 589832 | tf_op jit(solution)/shard_map/ppermute | solution.py:345
  160.9 51.1 %collective-permute-start.23 = (bf16[3072,256]{1,0:T(8,128)(2,1)}, bf16[3072,256]{1,0:T(8,128)(2,1)}, u32[]{:S(2)}, u32[]{:S(2)}) collective-permute-start(bf16[3072,256]{1,0:T(8,128)(2,1)} %get-tuple-element.103), channel_id=1, source_target_pairs={{16,18},{17,19},{18,16},{19,17},{20,22},{21,23},{22,20},{23,21},{2... | collective-permute-start | bytes 4718600 | tf_op jit(solution)/shard_map/ppermute | solution.py:345
  177.9 15.6 %collective-permute-start.20 = (bf16[384,256]{1,0:T(8,128)(2,1)S(1)}, bf16[384,256]{1,0:T(8,128)(2,1)S(1)}, u32[]{:S(2)}, u32[]{:S(2)}) collective-permute-start(bf16[384,256]{1,0:T(8,128)(2,1)S(1)} %collective-permute-done.18.refs_0_), channel_id=1, source_target_pairs={{16,24},{20,28},{24,16},{28,20},{17,25},{21,29},{25,17},{29,21},{1... | collective-permute-start | bytes 589832 | tf_op jit(solution)/shard_map/ppermute | solution.py:345
  179.9 13.6 %collective-permute-start.19 = (bf16[384,256]{1,0:T(8,128)(2,1)S(1)}, bf16[384,256]{1,0:T(8,128)(2,1)S(1)}, u32[]{:S(2)}, u32[]{:S(2)}) collective-permute-start(bf16[384,256]{1,0:T(8,128)(2,1)S(1)} %collective-permute-done.18.refs_0_), channel_id=1, source_target_pairs={{16,20},{20,16},{24,28},{28,24},{17,21},{21,17},{25,29},{29,25},{1... | collective-permute-start | bytes 589832 | tf_op jit(solution)/shard_map/ppermute | solution.py:345
  221.8 22.5 %collective-permute-start.25 = (bf16[1536,256]{1,0:T(8,128)(2,1)}, bf16[1536,256]{1,0:T(8,128)(2,1)S(1)}, u32[]{:S(2)}, u32[]{:S(2)}) collective-permute-start(bf16[1536,256]{1,0:T(8,128)(2,1)} %get-tuple-element.108), channel_id=1, source_target_pairs={{16,18},{17,19},{18,16},{19,17},{20,22},{21,23},{22,20},{23,21},{2... | collective-permute-start | bytes 2359304 | tf_op jit(solution)/shard_map/ppermute | solution.py:345
  224.2 36.0 %collective-permute-start.29 = (bf16[1536,256]{1,0:T(8,128)(2,1)S(1)}, bf16[1536,256]{1,0:T(8,128)(2,1)S(1)}, u32[]{:S(2)}, u32[]{:S(2)}) collective-permute-start(bf16[1536,256]{1,0:T(8,128)(2,1)S(1)} %get-tuple-element.116), channel_id=1, source_target_pairs={{16,18},{17,19},{18,16},{19,17},{20,22},{21,23},{22,20},{23,21},{2... | collective-permute-start | bytes 2359304 | tf_op jit(solution)/shard_map/ppermute | solution.py:345
  233.2 16.7 %collective-permute-start.27 = (bf16[384,256]{1,0:T(8,128)(2,1)S(1)}, bf16[384,256]{1,0:T(8,128)(2,1)S(1)}, u32[]{:S(2)}, u32[]{:S(2)}) collective-permute-start(bf16[384,256]{1,0:T(8,128)(2,1)S(1)} %get-tuple-element.112), channel_id=1, source_target_pairs={{16,24},{20,28},{24,16},{28,20},{17,25},{21,29},{25,17},{29,21},{1... | collective-permute-start | bytes 589832 | tf_op jit(solution)/shard_map/ppermute | solution.py:345
  235.1 14.8 %collective-permute-start.28 = (bf16[384,256]{1,0:T(8,128)(2,1)S(1)}, bf16[384,256]{1,0:T(8,128)(2,1)S(1)}, u32[]{:S(2)}, u32[]{:S(2)}) collective-permute-start(bf16[384,256]{1,0:T(8,128)(2,1)S(1)} %get-tuple-element.113), channel_id=1, source_target_pairs={{16,28},{20,24},{24,20},{28,16},{17,29},{21,25},{25,21},{29,17},{1... | collective-permute-start | bytes 589832 | tf_op jit(solution)/shard_map/ppermute | solution.py:345
  238.7 15.2 %collective-permute-start.26 = (bf16[384,256]{1,0:T(8,128)(2,1)S(1)}, bf16[384,256]{1,0:T(8,128)(2,1)S(1)}, u32[]{:S(2)}, u32[]{:S(2)}) collective-permute-start(bf16[384,256]{1,0:T(8,128)(2,1)S(1)} %get-tuple-element.110), channel_id=1, source_target_pairs={{16,20},{20,16},{24,28},{28,24},{17,21},{21,17},{25,29},{29,25},{1... | collective-permute-start | bytes 589832 | tf_op jit(solution)/shard_map/ppermute | solution.py:345
  268.9 16.2 %collective-permute-start.33 = (bf16[384,256]{1,0:T(8,128)(2,1)S(1)}, bf16[384,256]{1,0:T(8,128)(2,1)S(1)}, u32[]{:S(2)}, u32[]{:S(2)}) collective-permute-start(bf16[384,256]{1,0:T(8,128)(2,1)S(1)} %fusion.refs_2_), channel_id=1, source_target_pairs={{0,12},{4,8},{8,4},{12,0},{1,13},{5,9},{9,5},{13,1},{2,14},{6,10},... | collective-permute-start | bytes 589832 | tf_op jit(solution)/shard_map/ppermute | solution.py:349
  270.7 25.8 %collective-permute-start.32 = (bf16[384,256]{1,0:T(8,128)(2,1)S(1)}, bf16[384,256]{1,0:T(8,128)(2,1)S(1)}, u32[]{:S(2)}, u32[]{:S(2)}) collective-permute-start(bf16[384,256]{1,0:T(8,128)(2,1)S(1)} %fusion.refs_2_), channel_id=1, source_target_pairs={{0,8},{4,12},{8,0},{12,4},{1,9},{5,13},{9,1},{13,5},{2,10},{6,14},... | collective-permute-start | bytes 589832 | tf_op jit(solution)/shard_map/ppermute | solution.py:349
  270.7 25.8 %collective-permute-start.31 = (bf16[384,256]{1,0:T(8,128)(2,1)S(1)}, bf16[384,256]{1,0:T(8,128)(2,1)S(1)}, u32[]{:S(2)}, u32[]{:S(2)}) collective-permute-start(bf16[384,256]{1,0:T(8,128)(2,1)S(1)} %fusion.refs_2_), channel_id=1, source_target_pairs={{0,4},{4,0},{8,12},{12,8},{1,5},{5,1},{9,13},{13,9},{2,6},{6,2},{1... | collective-permute-start | bytes 589832 | tf_op jit(solution)/shard_map/ppermute | solution.py:349
  278.9 21.8 %collective-permute-start.35 = (bf16[384,256]{1,0:T(8,128)(2,1)S(1)}, bf16[384,256]{1,0:T(8,128)(2,1)S(1)}, u32[]{:S(2)}, u32[]{:S(2)}) collective-permute-start(bf16[384,256]{1,0:T(8,128)(2,1)S(1)} %get-tuple-element.125), channel_id=1, source_target_pairs={{16,24},{20,28},{24,16},{28,20},{17,25},{21,29},{25,17},{29,21},{1... | collective-permute-start | bytes 589832 | tf_op jit(solution)/shard_map/ppermute | solution.py:345
  281.1 19.6 %collective-permute-start.36 = (bf16[384,256]{1,0:T(8,128)(2,1)S(1)}, bf16[384,256]{1,0:T(8,128)(2,1)S(1)}, u32[]{:S(2)}, u32[]{:S(2)}) collective-permute-start(bf16[384,256]{1,0:T(8,128)(2,1)S(1)} %get-tuple-element.126), channel_id=1, source_target_pairs={{16,28},{20,24},{24,20},{28,16},{17,29},{21,25},{25,21},{29,17},{1... | collective-permute-start | bytes 589832 | tf_op jit(solution)/shard_map/ppermute | solution.py:345
  285.1 17.4 %collective-permute-start.34 = (bf16[384,256]{1,0:T(8,128)(2,1)S(1)}, bf16[384,256]{1,0:T(8,128)(2,1)S(1)}, u32[]{:S(2)}, u32[]{:S(2)}) collective-permute-start(bf16[384,256]{1,0:T(8,128)(2,1)S(1)} %get-tuple-element.119), channel_id=1, source_target_pairs={{16,20},{20,16},{24,28},{28,24},{17,21},{21,17},{25,29},{29,25},{1... | collective-permute-start | bytes 589832 | tf_op jit(solution)/shard_map/ppermute | solution.py:345
  304.8 17.6 %collective-permute-start.38 = (bf16[384,256]{1,0:T(8,128)(2,1)S(1)}, bf16[384,256]{1,0:T(8,128)(2,1)S(1)}, u32[]{:S(2)}, u32[]{:S(2)}) collective-permute-start(bf16[384,256]{1,0:T(8,128)(2,1)S(1)} %fusion.1.refs_3_), channel_id=1, source_target_pairs={{0,8},{4,12},{8,0},{12,4},{1,9},{5,13},{9,1},{13,5},{2,10},{6,14},... | collective-permute-start | bytes 589832 | tf_op jit(solution)/shard_map/ppermute | solution.py:349
  306.7 15.7 %collective-permute-start.37 = (bf16[384,256]{1,0:T(8,128)(2,1)S(1)}, bf16[384,256]{1,0:T(8,128)(2,1)S(1)}, u32[]{:S(2)}, u32[]{:S(2)}) collective-permute-start(bf16[384,256]{1,0:T(8,128)(2,1)S(1)} %fusion.1.refs_3_), channel_id=1, source_target_pairs={{0,4},{4,0},{8,12},{12,8},{1,5},{5,1},{9,13},{13,9},{2,6},{6,2},{1... | collective-permute-start | bytes 589832 | tf_op jit(solution)/shard_map/ppermute | solution.py:349
  (25 other events, 159.6 us)

commit v2 on v1

--- a/solution.py
+++ b/solution.py
@@ -375,15 +375,23 @@
             sources, prepare, tokens, outs, base, lambda i, s: i * hid_rows, first=first,
         )
 
-    def in_pieces(k):
-        count = 1 if k == 0 else 2
-        size = half // count
-        return [(half, 0, F32)] + [(size, n * size, LOW) for n in range(count)]
-
-    def exchange(k, active, pieces, earlier):
-        if k > 0:
+    def in_pieces(*shares):
+        blocks = [max(1, hid_steps * sum(shares[: n + 1]) // sum(shares)) for n in range(len(shares))]
+        ends = [0] + [hid_rows * block for block in blocks]
+        return [(half, 0, F32)] + [(ends[n + 1] - ends[n], ends[n], LOW) for n in range(len(shares))]
+
+    def exchange(active, pieces, earlier):
+        if earlier is not None:
             pieces = [lax.optimization_barrier((piece, earlier))[0] for piece in pieces]
         return [within(active, 2, piece) for piece in pieces]
+
+    def detour(piece):
+        size = lax.axis_size("wid")
+        return lax.ppermute(piece, ("section", "wid"), [(i, size + (i ^ 2)) for i in range(size)])
+
+    def returned(piece):
+        size = lax.axis_size("wid")
+        return lax.ppermute(piece, ("section", "wid"), [(size + i, i) for i in range(size)])
 
     def product_in(flags, place, sources, prepare, tokens, kind):
         return product(
@@ -438,11 +446,17 @@
     def down_hidden(k):
         full, *pieces = product_out(
             steps.after(down), mat_out, lambda s: s[1] * half, [lows[k]], None, sizes[k],
-            in_pieces(k), core_got[k],
+            in_pieces(*((1,) if k else (2, 1))), core_got[k],
         )
         steps.last = full
         hidden_full[k] = full
-        hidden_other[k] = exchange(k, 0, pieces, hidden_other[k - 1][-1] if k else None)
+        if k > 0:
+            hidden_other[k] = exchange(0, pieces, hidden_other[0][0])
+        else:
+            hidden_other[0] = [within(0, 2, pieces[0]), detour(pieces[1])]
+
+    def down_return():
+        hidden_other[0][1] = returned(steps.after(hidden_other[0][1]))
 
     def slope(k):
         slopes[k] = slope_of(steps.after(down), pre, starts[k], sizes[k], half)
@@ -462,8 +476,6 @@
 
     def cross(k):
         *others, own = parts_out[k]
-        if k + 1 in hidden_other:
-            own = lax.optimization_barrier((own, hidden_other[k + 1][0]))[0]
         terms[k] = scatter_hid(0, others + [steps.after(own)])
         crossed = lax.ppermute(terms[k], "section", [(0, 1)])
         steps.last = crossed
@@ -478,11 +490,11 @@
         )
         full, *pieces = product_out(
             up, split_out, lambda s: (1 - s[1]) * half, [low_other], None, tokens,
-            in_pieces(k), partial,
+            in_pieces(1), partial,
         )
         steps.last = full
         up_full[k] = full
-        up_other[k] = exchange(k, 1, pieces, up_other[k - 1][-1] if k else None)
+        up_other[k] = exchange(1, pieces, up_other[k - 1][-1] if k else None)
 
     def place(part, core):
         row = core * (PARTS // 2) + lax.rem(part, PARTS // 2)
@@ -500,8 +512,6 @@
 
     def gather(k):
         *others, own = up_parts[k]
-        if k + 1 in up_other:
-            own = lax.optimization_barrier((own, up_other[k + 1][0]))[0]
         last = jnp.where(is_up, scatter_hid(1, others + [steps.after(own)]), terms[k])
         steps.last = last
         lasts[k] = [last] + [everywhere(d, last) for d in range(1, PARTS)]
@@ -510,11 +520,13 @@
         down_send(k)
     for k in chunks:
         down_hidden(k)
-    for k in chunks:
-        slope(k)
+    slope(0)
+    down_return()
     down_back(0)
     out = None
     for k in chunks:
+        if k + 1 < len(SHARES):
+            slope(k + 1)
         cross(k)
         if k + 1 < len(SHARES):
             down_back(k + 1)

time: 326 us -> 316 us (0.969)
  waiting for transfers between devices: 140 us -> 129 us
  starting transfers between devices: 76.8 us -> 81 us
    ppermute x2, waiting for transfers between devices: 75.3 us -> 41 us  [cross(): crossed = lax.ppermute(terms[k], 'section', [(0, 1)])]
    ppermute x0 -> x2, waiting for transfers between devices: none -> 20 us  [the longest x1 11 us: returned(): lax.ppermute(piece, ('section', 'wid'), [(size + i, i) for i in range(siz...]
    ppermute x0 -> x2, starting transfers between devices: none -> 8.11 us  [the longest x1 6.82 us: returned(): lax.ppermute(piece, ('section', 'wid'), [(size + i, i) for i in range(siz...]
    ppermute x32 -> x30, starting transfers between devices: 65.3 us -> 61.4 us  [within(): return lax.ppermute(block, ('section', axis), pairs)]
    ppermute x32 -> x30, waiting for transfers between devices: 41.1 us -> 44.2 us  [within(): return lax.ppermute(block, ('section', axis), pairs)]
    unnamed x18 -> x14, local copies, waits for them, and re-layouts: 9.28 us -> 6.75 us
  transfers between devices with their start and end apart: 40 -> 40, of which waited for: 14 -> 16; matrix products, arithmetic and copies ran while one was open for 0% -> 0% of each run, Pallas kernels for 19% -> 19%
where the time goes in v2:
time: 316 us; the launch traced here: 314 us
  waiting for transfers between devices  129 us (41%)
  Pallas kernels  96.2 us (30%)
  starting transfers between devices  81 us (26%)
  local copies, waits for them, and re-layouts  6.96 us (2%)
    ppermute x30, starting transfers between devices, within(): return lax.ppermute(block, ('section', axis), pairs)  61.4 us
    pallas_call x16, Pallas kernels, product(): pl.pallas_call(body, in_specs=[SMEM, ANY] + [VMEM if first is None else A...  58.5 us
    ppermute x30, waiting for transfers between devices, within(): return lax.ppermute(block, ('section', axis), pairs)  44.2 us
    ppermute x2, waiting for transfers between devices, cross(): crossed = lax.ppermute(terms[k], 'section', [(0, 1)])  41 us
    ppermute x6, waiting for transfers between devices, everywhere(): return lax.ppermute(block, axis, [(i, i ^ distance) for i in range(size)])  23.7 us
    pallas_call x1, Pallas kernels, split_rows(): pl.pallas_call(body, in_specs=[SMEM, ANY], out_specs=ANY, out_shape=jax.S...  14.5 us
    pallas_call x2, Pallas kernels, slope_of(): pl.pallas_call(body, grid_spec=pltpu.PrefetchScalarGridSpec(num_scalar_pr...  11.7 us
    ppermute x1, waiting for transfers between devices, returned(): lax.ppermute(piece, ('section', 'wid'), [(size + i, i) for i in range(siz...  11 us
  transfers between devices with their start and end apart: 40, of which 16 were waited for; matrix products, arithmetic and copies ran while one was open for 0% of the time, Pallas kernels for 19%

profile of v2, /device:TPU:2, one launch (start us, length us, event | category | flops | bytes accessed | tf_op | source)
XLA Modules:
  0.0 314.3 jit_solution(12546501341516161080)
XLA Ops:
  0.1 14.5 %shard_map.46 = bf16[2,3072,1536]{2,1,0:T(8,128)(2,1)} custom-call(s32[3]{0:T(128)S(1)} %get-tuple-element.112.s, bf16[6144,1536]{1,0:T(8,128)(2,1)} %bitcast.26), custom_call_target="tpu_custom_call" | custom-call | flops 1179648 | bytes 9216 | tf_op jit(solution)/shard_map/pallas_call | solution.py:204
  22.8 5.9 %shard_map.51.slope_ref.refs_1_ = f32[3072,256]{1,0:T(8,128)S(1)} custom-call(s32[3]{0:T(128)S(1)} %get-tuple-element.83.s, f32[512,6144]{1,0:T(8,128)} %bitcast.35), custom_call_target="tpu_custom_call" | custom-call | flops 192 | bytes 1536 | tf_op jit(solution)/shard_map/pallas_call | solution.py:230
  30.3 9.0 %collective-permute-done.3 = bf16[1024,256]{1,0:T(8,128)(2,1)S(1)} collective-permute-done((bf16[1024,256]{1,0:T(8,128)(2,1)S(1)}, bf16[1024,256]{1,0:T(8,128)(2,1)S(1)}, u32[]{:S(2)}, u32[]{:S(2)}) %collective-permute-start.3) | collective-permute-done | bytes 524320 | tf_op jit(solution)/shard_map/ppermute | solution.py:390
  39.3 6.8 %collective-permute-start.4 = (bf16[1024,256]{1,0:T(8,128)(2,1)S(1)}, bf16[1024,256]{1,0:T(8,128)(2,1)S(1)}, u32[]{:S(2)}, u32[]{:S(2)}) collective-permute-start(bf16[1024,256]{1,0:T(8,128)(2,1)S(1)} %collective-permute-done.3), channel_id=1, source_target_pairs={{16,0},{17,1},{18,2},{19,3},{20,4},{21,5},{22,6},{23,7},{24,8},{25... | collective-permute-start | bytes 1572872 | tf_op jit(solution)/shard_map/ppermute | solution.py:394
  46.2 11.0 %collective-permute-done.4.refs_1_ = bf16[1024,256]{1,0:T(8,128)(2,1)S(1)} collective-permute-done((bf16[1024,256]{1,0:T(8,128)(2,1)S(1)}, bf16[1024,256]{1,0:T(8,128)(2,1)S(1)}, u32[]{:S(2)}, u32[]{:S(2)}) %collective-permute-start.4) | collective-permute-done | bytes 524320 | tf_op jit(solution)/shard_map/ppermute | solution.py:394
  63.9 5.9 %shard_map.55.slope_ref.refs_1_ = f32[3072,256]{1,0:T(8,128)S(1)} custom-call(s32[3]{0:T(128)S(1)} %get-tuple-element.83.s, f32[512,6144]{1,0:T(8,128)} %bitcast.36), custom_call_target="tpu_custom_call" | custom-call | flops 192 | bytes 1536 | tf_op jit(solution)/shard_map/pallas_call | solution.py:230
  72.9 33.4 %collective-permute-done.9.refs_0_ = bf16[384,256]{1,0:T(8,128)(2,1)S(1)} collective-permute-done((bf16[384,256]{1,0:T(8,128)(2,1)S(1)}, bf16[384,256]{1,0:T(8,128)(2,1)S(1)}, u32[]{:S(2)}, u32[]{:S(2)}) %collective-permute-start.9) | collective-permute-done | bytes 196640 | tf_op jit(solution)/shard_map/ppermute | solution.py:480
  108.9 5.4 %collective-permute-start.14 = (bf16[384,256]{1,0:T(8,128)(2,1)S(1)}, bf16[384,256]{1,0:T(8,128)(2,1)S(1)}, u32[]{:S(2)}, u32[]{:S(2)}) collective-permute-start(bf16[384,256]{1,0:T(8,128)(2,1)S(1)} %collective-permute-done.9.refs_0_), channel_id=1, source_target_pairs={{16,28},{20,24},{24,20},{28,16},{17,29},{21,25},{25,21},{29,17},{1... | collective-permute-start | bytes 589832 | tf_op jit(solution)/shard_map/ppermute | solution.py:345
  120.5 10.3 %collective-permute-done.13.refs_2_ = bf16[384,256]{1,0:T(8,128)(2,1)S(1)} collective-permute-done((bf16[384,256]{1,0:T(8,128)(2,1)S(1)}, bf16[384,256]{1,0:T(8,128)(2,1)S(1)}, u32[]{:S(2)}, u32[]{:S(2)}) %collective-permute-start.13) | collective-permute-done | bytes 196640 | tf_op jit(solution)/shard_map/ppermute | solution.py:345
  135.8 5.6 %shard_map.60.refs_1_ = f32[3072,256]{1,0:T(8,128)S(1)} custom-call(s32[3]{0:T(128)S(1)} %get-tuple-element.112.s, bf16[6144,1536]{1,0:T(8,128)(2,1)} %bitcast.31, bf16[1536,256]{1,0:T(8,128)(2,1)S(1)} %get-tuple-element.89.refs_0_), custom_call_target="tpu_custom_call" | custom-call | flops 589824 | bytes 2304 | tf_op jit(solution)/shard_map/pallas_call | solution.py:104
  143.1 8.2 %shard_map.61 = (f32[3072,256]{1,0:T(8,128)S(1)}, bf16[3072,256]{1,0:T(8,128)(2,1)}) custom-call(s32[3]{0:T(128)S(1)} %get-tuple-element.112.s, bf16[6144,1536]{1,0:T(8,128)(2,1)} %bitcast.32, bf16[1536,256]{1,0:T(8,128)(2,1)S(1)} %collective-permute-done.15.refs_0_, f32[3072,256]{1,0:T(8,128)} %copy-done.4), custom_call_target="tpu_custom_call" | custom-call | flops 589824 | bytes 2304 | tf_op jit(solution)/shard_map/pallas_call | solution.py:104
  156.2 7.6 %collective-permute-done.19.refs_0_ = bf16[384,256]{1,0:T(8,128)(2,1)S(1)} collective-permute-done((bf16[384,256]{1,0:T(8,128)(2,1)S(1)}, bf16[384,256]{1,0:T(8,128)(2,1)S(1)}, u32[]{:S(2)}, u32[]{:S(2)}) %collective-permute-start.19) | collective-permute-done | bytes 196640 | tf_op jit(solution)/shard_map/ppermute | solution.py:480
  163.9 4.5 %collective-permute-start.22 = (bf16[384,256]{1,0:T(8,128)(2,1)S(1)}, bf16[384,256]{1,0:T(8,128)(2,1)S(1)}, u32[]{:S(2)}, u32[]{:S(2)}) collective-permute-start(bf16[384,256]{1,0:T(8,128)(2,1)S(1)} %collective-permute-done.19.refs_0_), channel_id=1, source_target_pairs={{16,28},{20,24},{24,20},{28,16},{17,29},{21,25},{25,21},{29,17},{1... | collective-permute-start | bytes 589832 | tf_op jit(solution)/shard_map/ppermute | solution.py:345
  175.4 8.5 %collective-permute-done.21.refs_2_ = bf16[384,256]{1,0:T(8,128)(2,1)S(1)} collective-permute-done((bf16[384,256]{1,0:T(8,128)(2,1)S(1)}, bf16[384,256]{1,0:T(8,128)(2,1)S(1)}, u32[]{:S(2)}, u32[]{:S(2)}) %collective-permute-start.21) | collective-permute-done | bytes 196640 | tf_op jit(solution)/shard_map/ppermute | solution.py:345
  186.9 5.6 %shard_map.63.refs_1_ = f32[3072,256]{1,0:T(8,128)S(1)} custom-call(s32[3]{0:T(128)S(1)} %get-tuple-element.112.s, bf16[6144,1536]{1,0:T(8,128)(2,1)} %bitcast.33, bf16[1536,256]{1,0:T(8,128)(2,1)S(1)} %get-tuple-element.95.refs_0_), custom_call_target="tpu_custom_call" | custom-call | flops 589824 | bytes 2304 | tf_op jit(solution)/shard_map/pallas_call | solution.py:104
  194.3 7.1 %shard_map.64 = (f32[3072,256]{1,0:T(8,128)S(1)}, bf16[3072,256]{1,0:T(8,128)(2,1)S(1)}) custom-call(s32[3]{0:T(128)S(1)} %get-tuple-element.112.s, bf16[6144,1536]{1,0:T(8,128)(2,1)} %bitcast.34, bf16[1536,256]{1,0:T(8,128)(2,1)S(1)} %collective-permute-done.23.refs_0_, f32[3072,256]{1,0:T(8,128)} %copy-done.3), custom_call_target="tpu_custom_call" | custom-call | flops 589824 | bytes 2304 | tf_op jit(solution)/shard_map/pallas_call | solution.py:104
  201.4 7.3 %shard_map.65 = (f32[1536,256]{1,0:T(8,128)S(1)}, bf16[3072,256]{1,0:T(8,128)(2,1)S(1)}) custom-call(s32[3]{0:T(128)S(1)} %get-tuple-element.112.s, bf16[1536,6144]{1,0:T(8,128)(2,1)} %bitcast.22, f32[3072,256]{1,0:T(8,128)S(1)} %get-tuple-element.90.refs_0_, f32[3072,256]{1,0:T(8,128)} %copy-done.2, bf16[3072,256]{1,0:T(8,128)(2,1)} %collective-permute-done.24.refs_2_), custom_call_target="tpu_custom_call" | custom-call | flops 589824 | bytes 2304 | tf_op jit(solution)/shard_map/pallas_call | solution.py:104
  214.1 5.5 %shard_map.66 = (bf16[384,256]{1,0:T(8,128)(2,1)S(1)}, bf16[384,256]{1,0:T(8,128)(2,1)S(1)}, bf16[384,256]{1,0:T(8,128)(2,1)S(1)}, f32[384,256]{1,0:T(8,128)S(1)}) custom-call(s32[3]{0:T(128)S(1)} %get-tuple-element.112.s, bf16[1536,6144]{1,0:T(8,128)(2,1)} %bitcast.23, bf16[3072,256]{1,0:T(8,128)(2,1)S(1)} %get-tuple-element.99.refs_0_, ...), custom_call_target="tpu_custom_call" | custom-call | flops 589824 | bytes 2304 | tf_op jit(solution)/shard_map/pallas_call | solution.py:104
  228.8 8.3 %collective-permute-done.27 = bf16[384,256]{1,0:T(8,128)(2,1)S(1)} collective-permute-done((bf16[384,256]{1,0:T(8,128)(2,1)S(1)}, bf16[384,256]{1,0:T(8,128)(2,1)S(1)}, u32[]{:S(2)}, u32[]{:S(2)}) %collective-permute-start.27) | collective-permute-done | bytes 196640 | tf_op jit(solution)/shard_map/ppermute | solution.py:345
  241.4 7.9 %collective-permute-done.29.refs_2_ = bf16[3072,256]{1,0:T(8,128)(2,1)S(1)} collective-permute-done((bf16[3072,256]{1,0:T(8,128)(2,1)S(1)}, bf16[3072,256]{1,0:T(8,128)(2,1)S(1)}, u32[]{:S(2)}, u32[]{:S(2)}) %collective-permute-start.29) | collective-permute-done | bytes 1572896 | tf_op jit(solution)/shard_map/ppermute | solution.py:345
  249.3 6.8 %shard_map.67 = (f32[1536,256]{1,0:T(8,128)S(1)}, bf16[3072,256]{1,0:T(8,128)(2,1)S(1)}) custom-call(s32[3]{0:T(128)S(1)} %get-tuple-element.112.s, bf16[1536,6144]{1,0:T(8,128)(2,1)} %bitcast.24, f32[3072,256]{1,0:T(8,128)S(1)} %get-tuple-element.96.refs_0_, f32[3072,256]{1,0:T(8,128)} %copy-done.1, bf16[3072,256]{1,0:T(8,128)(2,1)S(1)} %collective-permute-done.29.refs_2_), custom_call_target="tpu_custom_call" | custom-call | flops 589824 | bytes 2304 | tf_op jit(solution)/shard_map/pallas_call | solution.py:104
  262.5 5.5 %shard_map.68 = (bf16[384,256]{1,0:T(8,128)(2,1)S(1)}, bf16[384,256]{1,0:T(8,128)(2,1)S(1)}, bf16[384,256]{1,0:T(8,128)(2,1)S(1)}, f32[384,256]{1,0:T(8,128)S(1)}) custom-call(s32[3]{0:T(128)S(1)} %get-tuple-element.112.s, bf16[1536,6144]{1,0:T(8,128)(2,1)} %bitcast.25, bf16[3072,256]{1,0:T(8,128)(2,1)S(1)} %get-tuple-element.109.refs_0_, ...), custom_call_target="tpu_custom_call" | custom-call | flops 589824 | bytes 2304 | tf_op jit(solution)/shard_map/pallas_call | solution.py:104
  277.2 8.4 %collective-permute-done.32.refs_4_ = bf16[384,256]{1,0:T(8,128)(2,1)S(1)} collective-permute-done((bf16[384,256]{1,0:T(8,128)(2,1)S(1)}, bf16[384,256]{1,0:T(8,128)(2,1)S(1)}, u32[]{:S(2)}, u32[]{:S(2)}) %collective-permute-start.32) | collective-permute-done | bytes 196640 | tf_op jit(solution)/shard_map/ppermute | solution.py:349
  300.7 10.8 %collective-permute-done.38.refs_5_ = bf16[384,256]{1,0:T(8,128)(2,1)S(1)} collective-permute-done((bf16[384,256]{1,0:T(8,128)(2,1)S(1)}, bf16[384,256]{1,0:T(8,128)(2,1)S(1)}, u32[]{:S(2)}, u32[]{:S(2)}) %collective-permute-start.38) | collective-permute-done | bytes 196640 | tf_op jit(solution)/shard_map/ppermute | solution.py:349
  (101 shorter events, 103.7 us)
Async XLA Ops:
  19.0 20.3 %collective-permute-start.3 = (bf16[1024,256]{1,0:T(8,128)(2,1)S(1)}, bf16[1024,256]{1,0:T(8,128)(2,1)S(1)}, u32[]{:S(2)}, u32[]{:S(2)}) collective-permute-start(bf16[1024,256]{1,0:T(8,128)(2,1)S(1)} %get-tuple-element.75), channel_id=1, source_target_pairs={{0,18},{1,19},{2,16},{3,17},{4,22},{5,23},{6,20},{7,21},{8,26},{9,... | collective-permute-start | bytes 1572872 | tf_op jit(solution)/shard_map/ppermute | solution.py:390
  20.3 25.9 %collective-permute-start.2 = (bf16[2048,256]{1,0:T(8,128)(2,1)}, bf16[2048,256]{1,0:T(8,128)(2,1)S(1)}, u32[]{:S(2)}, u32[]{:S(2)}) collective-permute-start(bf16[2048,256]{1,0:T(8,128)(2,1)} %get-tuple-element.74), channel_id=1, source_target_pairs={{0,2},{1,3},{2,0},{3,1},{4,6},{5,7},{6,4},{7,5},{8,10},{9,11},{10,... | collective-permute-start | bytes 3145736 | tf_op jit(solution)/shard_map/ppermute | solution.py:345
  39.3 17.9 %collective-permute-start.4 = (bf16[1024,256]{1,0:T(8,128)(2,1)S(1)}, bf16[1024,256]{1,0:T(8,128)(2,1)S(1)}, u32[]{:S(2)}, u32[]{:S(2)}) collective-permute-start(bf16[1024,256]{1,0:T(8,128)(2,1)S(1)} %collective-permute-done.3), channel_id=1, source_target_pairs={{16,0},{17,1},{18,2},{19,3},{20,4},{21,5},{22,6},{23,7},{24,8},{25... | collective-permute-start | bytes 1572872 | tf_op jit(solution)/shard_map/ppermute | solution.py:394
  59.9 46.4 %collective-permute-start.10 = (bf16[3072,256]{1,0:T(8,128)(2,1)}, bf16[3072,256]{1,0:T(8,128)(2,1)S(1)}, u32[]{:S(2)}, u32[]{:S(2)}) collective-permute-start(bf16[3072,256]{1,0:T(8,128)(2,1)} %get-tuple-element.85), channel_id=1, source_target_pairs={{0,2},{1,3},{2,0},{3,1},{4,6},{5,7},{6,4},{7,5},{8,10},{9,11},{10,... | collective-permute-start | bytes 4718600 | tf_op jit(solution)/shard_map/ppermute | solution.py:345
  71.6 34.7 %collective-permute-start.9 = (bf16[384,256]{1,0:T(8,128)(2,1)S(1)}, bf16[384,256]{1,0:T(8,128)(2,1)S(1)}, u32[]{:S(2)}, u32[]{:S(2)}) collective-permute-start(bf16[384,256]{1,0:T(8,128)(2,1)S(1)} %add_convert_fusion.3), channel_id=1, source_target_pairs={{0,16},{1,17},{2,18},{3,19},{4,20},{5,21},{6,22},{7,23},{8,24},{9,... | collective-permute-start | bytes 589832 | tf_op jit(solution)/shard_map/ppermute | solution.py:480
  114.4 16.4 %collective-permute-start.13 = (bf16[384,256]{1,0:T(8,128)(2,1)S(1)}, bf16[384,256]{1,0:T(8,128)(2,1)S(1)}, u32[]{:S(2)}, u32[]{:S(2)}) collective-permute-start(bf16[384,256]{1,0:T(8,128)(2,1)S(1)} %collective-permute-done.9.refs_0_), channel_id=1, source_target_pairs={{16,24},{20,28},{24,16},{28,20},{17,25},{21,29},{25,17},{29,21},{1... | collective-permute-start | bytes 589832 | tf_op jit(solution)/shard_map/ppermute | solution.py:345
  116.3 14.5 %collective-permute-start.12 = (bf16[384,256]{1,0:T(8,128)(2,1)S(1)}, bf16[384,256]{1,0:T(8,128)(2,1)S(1)}, u32[]{:S(2)}, u32[]{:S(2)}) collective-permute-start(bf16[384,256]{1,0:T(8,128)(2,1)S(1)} %collective-permute-done.9.refs_0_), channel_id=1, source_target_pairs={{16,20},{20,16},{24,28},{28,24},{17,21},{21,17},{25,29},{29,25},{1... | collective-permute-start | bytes 589832 | tf_op jit(solution)/shard_map/ppermute | solution.py:345
  133.7 21.1 %collective-permute-start.17 = (bf16[384,256]{1,0:T(8,128)(2,1)S(1)}, bf16[384,256]{1,0:T(8,128)(2,1)S(1)}, u32[]{:S(2)}, u32[]{:S(2)}) collective-permute-start(bf16[384,256]{1,0:T(8,128)(2,1)S(1)} %get-tuple-element.92), channel_id=1, source_target_pairs={{0,8},{4,12},{8,0},{12,4},{1,9},{5,13},{9,1},{13,5},{2,10},{6,14},... | collective-permute-start | bytes 589832 | tf_op jit(solution)/shard_map/ppermute | solution.py:345
  134.4 20.4 %collective-permute-start.18 = (bf16[384,256]{1,0:T(8,128)(2,1)S(1)}, bf16[384,256]{1,0:T(8,128)(2,1)S(1)}, u32[]{:S(2)}, u32[]{:S(2)}) collective-permute-start(bf16[384,256]{1,0:T(8,128)(2,1)S(1)} %get-tuple-element.93), channel_id=1, source_target_pairs={{0,12},{4,8},{8,4},{12,0},{1,13},{5,9},{9,5},{13,1},{2,14},{6,10},... | collective-permute-start | bytes 589832 | tf_op jit(solution)/shard_map/ppermute | solution.py:345
  135.1 19.7 %collective-permute-start.16 = (bf16[384,256]{1,0:T(8,128)(2,1)S(1)}, bf16[384,256]{1,0:T(8,128)(2,1)S(1)}, u32[]{:S(2)}, u32[]{:S(2)}) collective-permute-start(bf16[384,256]{1,0:T(8,128)(2,1)S(1)} %get-tuple-element.87), channel_id=1, source_target_pairs={{0,4},{4,0},{8,12},{12,8},{1,5},{5,1},{9,13},{13,9},{2,6},{6,2},{1... | collective-permute-start | bytes 589832 | tf_op jit(solution)/shard_map/ppermute | solution.py:345
  151.4 50.0 %collective-permute-start.24 = (bf16[3072,256]{1,0:T(8,128)(2,1)}, bf16[3072,256]{1,0:T(8,128)(2,1)}, u32[]{:S(2)}, u32[]{:S(2)}) collective-permute-start(bf16[3072,256]{1,0:T(8,128)(2,1)} %get-tuple-element.98), channel_id=1, source_target_pairs={{16,18},{17,19},{18,16},{19,17},{20,22},{21,23},{22,20},{23,21},{2... | collective-permute-start | bytes 4718600 | tf_op jit(solution)/shard_map/ppermute | solution.py:345
  168.4 15.6 %collective-permute-start.21 = (bf16[384,256]{1,0:T(8,128)(2,1)S(1)}, bf16[384,256]{1,0:T(8,128)(2,1)S(1)}, u32[]{:S(2)}, u32[]{:S(2)}) collective-permute-start(bf16[384,256]{1,0:T(8,128)(2,1)S(1)} %collective-permute-done.19.refs_0_), channel_id=1, source_target_pairs={{16,24},{20,28},{24,16},{28,20},{17,25},{21,29},{25,17},{29,21},{1... | collective-permute-start | bytes 589832 | tf_op jit(solution)/shard_map/ppermute | solution.py:345
  211.1 38.2 %collective-permute-start.29 = (bf16[3072,256]{1,0:T(8,128)(2,1)S(1)}, bf16[3072,256]{1,0:T(8,128)(2,1)S(1)}, u32[]{:S(2)}, u32[]{:S(2)}) collective-permute-start(bf16[3072,256]{1,0:T(8,128)(2,1)S(1)} %get-tuple-element.108), channel_id=1, source_target_pairs={{16,18},{17,19},{18,16},{19,17},{20,22},{21,23},{22,20},{23,21},{2... | collective-permute-start | bytes 4718600 | tf_op jit(solution)/shard_map/ppermute | solution.py:345
  219.6 17.6 %collective-permute-start.27 = (bf16[384,256]{1,0:T(8,128)(2,1)S(1)}, bf16[384,256]{1,0:T(8,128)(2,1)S(1)}, u32[]{:S(2)}, u32[]{:S(2)}) collective-permute-start(bf16[384,256]{1,0:T(8,128)(2,1)S(1)} %get-tuple-element.104), channel_id=1, source_target_pairs={{16,24},{20,28},{24,16},{28,20},{17,25},{21,29},{25,17},{29,21},{1... | collective-permute-start | bytes 589832 | tf_op jit(solution)/shard_map/ppermute | solution.py:345
  221.5 15.7 %collective-permute-start.28 = (bf16[384,256]{1,0:T(8,128)(2,1)S(1)}, bf16[384,256]{1,0:T(8,128)(2,1)S(1)}, u32[]{:S(2)}, u32[]{:S(2)}) collective-permute-start(bf16[384,256]{1,0:T(8,128)(2,1)S(1)} %get-tuple-element.105), channel_id=1, source_target_pairs={{16,28},{20,24},{24,20},{28,16},{17,29},{21,25},{25,21},{29,17},{1... | collective-permute-start | bytes 589832 | tf_op jit(solution)/shard_map/ppermute | solution.py:345
  225.2 16.1 %collective-permute-start.26 = (bf16[384,256]{1,0:T(8,128)(2,1)S(1)}, bf16[384,256]{1,0:T(8,128)(2,1)S(1)}, u32[]{:S(2)}, u32[]{:S(2)}) collective-permute-start(bf16[384,256]{1,0:T(8,128)(2,1)S(1)} %get-tuple-element.102), channel_id=1, source_target_pairs={{16,20},{20,16},{24,28},{28,24},{17,21},{21,17},{25,29},{29,25},{1... | collective-permute-start | bytes 589832 | tf_op jit(solution)/shard_map/ppermute | solution.py:345
  258.0 16.2 %collective-permute-start.33 = (bf16[384,256]{1,0:T(8,128)(2,1)S(1)}, bf16[384,256]{1,0:T(8,128)(2,1)S(1)}, u32[]{:S(2)}, u32[]{:S(2)}) collective-permute-start(bf16[384,256]{1,0:T(8,128)(2,1)S(1)} %fusion.refs_2_), channel_id=1, source_target_pairs={{0,12},{4,8},{8,4},{12,0},{1,13},{5,9},{9,5},{13,1},{2,14},{6,10},... | collective-permute-start | bytes 589832 | tf_op jit(solution)/shard_map/ppermute | solution.py:349
  259.8 25.8 %collective-permute-start.32 = (bf16[384,256]{1,0:T(8,128)(2,1)S(1)}, bf16[384,256]{1,0:T(8,128)(2,1)S(1)}, u32[]{:S(2)}, u32[]{:S(2)}) collective-permute-start(bf16[384,256]{1,0:T(8,128)(2,1)S(1)} %fusion.refs_2_), channel_id=1, source_target_pairs={{0,8},{4,12},{8,0},{12,4},{1,9},{5,13},{9,1},{13,5},{2,10},{6,14},... | collective-permute-start | bytes 589832 | tf_op jit(solution)/shard_map/ppermute | solution.py:349
  259.8 25.8 %collective-permute-start.31 = (bf16[384,256]{1,0:T(8,128)(2,1)S(1)}, bf16[384,256]{1,0:T(8,128)(2,1)S(1)}, u32[]{:S(2)}, u32[]{:S(2)}) collective-permute-start(bf16[384,256]{1,0:T(8,128)(2,1)S(1)} %fusion.refs_2_), channel_id=1, source_target_pairs={{0,4},{4,0},{8,12},{12,8},{1,5},{5,1},{9,13},{13,9},{2,6},{6,2},{1... | collective-permute-start | bytes 589832 | tf_op jit(solution)/shard_map/ppermute | solution.py:349
  268.0 21.8 %collective-permute-start.35 = (bf16[384,256]{1,0:T(8,128)(2,1)S(1)}, bf16[384,256]{1,0:T(8,128)(2,1)S(1)}, u32[]{:S(2)}, u32[]{:S(2)}) collective-permute-start(bf16[384,256]{1,0:T(8,128)(2,1)S(1)} %get-tuple-element.117), channel_id=1, source_target_pairs={{16,24},{20,28},{24,16},{28,20},{17,25},{21,29},{25,17},{29,21},{1... | collective-permute-start | bytes 589832 | tf_op jit(solution)/shard_map/ppermute | solution.py:345
  270.1 19.6 %collective-permute-start.36 = (bf16[384,256]{1,0:T(8,128)(2,1)S(1)}, bf16[384,256]{1,0:T(8,128)(2,1)S(1)}, u32[]{:S(2)}, u32[]{:S(2)}) collective-permute-start(bf16[384,256]{1,0:T(8,128)(2,1)S(1)} %get-tuple-element.118), channel_id=1, source_target_pairs={{16,28},{20,24},{24,20},{28,16},{17,29},{21,25},{25,21},{29,17},{1... | collective-permute-start | bytes 589832 | tf_op jit(solution)/shard_map/ppermute | solution.py:345
  274.2 17.4 %collective-permute-start.34 = (bf16[384,256]{1,0:T(8,128)(2,1)S(1)}, bf16[384,256]{1,0:T(8,128)(2,1)S(1)}, u32[]{:S(2)}, u32[]{:S(2)}) collective-permute-start(bf16[384,256]{1,0:T(8,128)(2,1)S(1)} %get-tuple-element.111), channel_id=1, source_target_pairs={{16,20},{20,16},{24,28},{28,24},{17,21},{21,17},{25,29},{29,25},{1... | collective-permute-start | bytes 589832 | tf_op jit(solution)/shard_map/ppermute | solution.py:345
  293.8 17.6 %collective-permute-start.38 = (bf16[384,256]{1,0:T(8,128)(2,1)S(1)}, bf16[384,256]{1,0:T(8,128)(2,1)S(1)}, u32[]{:S(2)}, u32[]{:S(2)}) collective-permute-start(bf16[384,256]{1,0:T(8,128)(2,1)S(1)} %fusion.1.refs_3_), channel_id=1, source_target_pairs={{0,8},{4,12},{8,0},{12,4},{1,9},{5,13},{9,1},{13,5},{2,10},{6,14},... | collective-permute-start | bytes 589832 | tf_op jit(solution)/shard_map/ppermute | solution.py:349
  295.8 15.7 %collective-permute-start.37 = (bf16[384,256]{1,0:T(8,128)(2,1)S(1)}, bf16[384,256]{1,0:T(8,128)(2,1)S(1)}, u32[]{:S(2)}, u32[]{:S(2)}) collective-permute-start(bf16[384,256]{1,0:T(8,128)(2,1)S(1)} %fusion.1.refs_3_), channel_id=1, source_target_pairs={{0,4},{4,0},{8,12},{12,8},{1,5},{5,1},{9,13},{13,9},{2,6},{6,2},{1... | collective-permute-start | bytes 589832 | tf_op jit(solution)/shard_map/ppermute | solution.py:349
  (23 other events, 186.3 us)

commit v3 on v2

--- a/solution.py
+++ b/solution.py
@@ -358,6 +358,7 @@
     starts = [unit * sum(SHARES[:k]) for k in range(len(SHARES))]
     sizes = [unit * share for share in SHARES]
     chunks = range(len(SHARES))
+    last_chunk = len(SHARES) - 1
     grad = grad_out.reshape(total, quarter)
     pre = pre_act[0].reshape(total, hid_tile)
     grads = [grad[starts[k] : starts[k] + sizes[k]] for k in chunks]
@@ -392,6 +393,11 @@
     def returned(piece):
         size = lax.axis_size("wid")
         return lax.ppermute(piece, ("section", "wid"), [(size + i, i) for i in range(size)])
+
+    def across(term, distance):
+        size = lax.axis_size("hid")
+        pairs = [(i, size + (i ^ distance)) for i in range(size)]
+        return lax.ppermute(term, ("section", "hid"), pairs)
 
     def product_in(flags, place, sources, prepare, tokens, kind):
         return product(
@@ -477,9 +483,13 @@
     def cross(k):
         *others, own = parts_out[k]
         terms[k] = scatter_hid(0, others + [steps.after(own)])
-        crossed = lax.ppermute(terms[k], "section", [(0, 1)])
-        steps.last = crossed
-        gathered[k] = [crossed] + [within(1, d, crossed, "hid") for d in range(1, PARTS)]
+        if k == 0:
+            crossed = across(terms[k], 0)
+            steps.last = crossed
+            gathered[k] = [crossed] + [within(1, d, crossed, "hid") for d in range(1, PARTS)]
+        else:
+            gathered[k] = [across(terms[k], d) for d in range(PARTS)]
+            steps.last = gathered[k][0]
 
     def up_hidden(k):
         tokens = sizes[k]
@@ -494,7 +504,7 @@
         )
         steps.last = full
         up_full[k] = full
-        up_other[k] = exchange(1, pieces, up_other[k - 1][-1] if k else None)
+        up_other[k] = exchange(1, pieces, up_other[k - 1][0] if k else None)
 
     def place(part, core):
         row = core * (PARTS // 2) + lax.rem(part, PARTS // 2)
@@ -520,23 +530,22 @@
         down_send(k)
     for k in chunks:
         down_hidden(k)
+    down_return()
     slope(0)
-    down_return()
     down_back(0)
-    out = None
-    for k in chunks:
-        if k + 1 < len(SHARES):
-            slope(k + 1)
-        cross(k)
-        if k + 1 < len(SHARES):
-            down_back(k + 1)
-        up_hidden(k)
-    for k in chunks:
-        up_back(k)
-        if k > 0:
-            out = finish(steps.after(up), out, grad, starts[k - 1], up_terms[k - 1], lasts[k - 1])
-            steps.last = out
-        gather(k)
+    slope(1)
+    cross(0)
+    down_back(1)
+    up_hidden(0)
+    cross(1)
+    up_hidden(1)
+    up_back(0)
+    gather(0)
+    up_back(1)
+    out = finish(steps.after(up), None, grad, starts[0], up_terms[0], lasts[0])
+    steps.last = out
+    gather(1)
+    k = last_chunk
     out = finish(up, out, grad, starts[k], up_terms[k], lasts[k])
     return out.reshape(1, batches, batch_tokens, quarter)
 

time: 316 us -> 305 us (0.965)
  starting transfers between devices: 81 us -> 69.3 us
    ppermute x2 -> x5, waiting for transfers between devices: 41 us -> 51.6 us  [across(): return lax.ppermute(term, ('section', 'hid'), pairs)]
    ppermute x30 -> x27, starting transfers between devices: 61.4 us -> 51.1 us  [within(): return lax.ppermute(block, ('section', axis), pairs)]
    ppermute x30 -> x27, waiting for transfers between devices: 44.2 us -> 34 us  [within(): return lax.ppermute(block, ('section', axis), pairs)]
    ppermute x1, waiting for transfers between devices: 9.02 us -> 16.6 us  [detour(): lax.ppermute(piece, ('section', 'wid'), [(i, size + (i ^ 2)) for i in ran...]
    ppermute x1, waiting for transfers between devices: 11 us -> 3.52 us  [returned(): lax.ppermute(piece, ('section', 'wid'), [(size + i, i) for i in range(siz...]
    ppermute x1, starting transfers between devices: 6.82 us -> 1.31 us  [returned(): lax.ppermute(piece, ('section', 'wid'), [(size + i, i) for i in range(siz...]
    ppermute x2 -> x5, starting transfers between devices: 2.58 us -> 6.64 us  [across(): return lax.ppermute(term, ('section', 'hid'), pairs)]
  transfers between devices with their start and end apart: 40 -> 40, of which waited for: 16 -> 15; matrix products, arithmetic and copies ran while one was open for 0% -> 0% of each run, Pallas kernels for 19% -> 17%
where the time goes in v3:
time: 305 us; the launch traced here: 304 us
  waiting for transfers between devices  131 us (43%)
  Pallas kernels  96.2 us (32%)
  starting transfers between devices  69.3 us (23%)
  local copies, waits for them, and re-layouts  6.96 us (2%)
    pallas_call x16, Pallas kernels, product(): pl.pallas_call(body, in_specs=[SMEM, ANY] + [VMEM if first is None else A...  58.5 us
    ppermute x5, waiting for transfers between devices, across(): return lax.ppermute(term, ('section', 'hid'), pairs)  51.6 us
    ppermute x27, starting transfers between devices, within(): return lax.ppermute(block, ('section', axis), pairs)  51.1 us
    ppermute x27, waiting for transfers between devices, within(): return lax.ppermute(block, ('section', axis), pairs)  34 us
    ppermute x6, waiting for transfers between devices, everywhere(): return lax.ppermute(block, axis, [(i, i ^ distance) for i in range(size)])  24.9 us
    ppermute x1, waiting for transfers between devices, detour(): lax.ppermute(piece, ('section', 'wid'), [(i, size + (i ^ 2)) for i in ran...  16.6 us
    pallas_call x1, Pallas kernels, split_rows(): pl.pallas_call(body, in_specs=[SMEM, ANY], out_specs=ANY, out_shape=jax.S...  14.5 us
    pallas_call x2, Pallas kernels, slope_of(): pl.pallas_call(body, grid_spec=pltpu.PrefetchScalarGridSpec(num_scalar_pr...  11.7 us
  transfers between devices with their start and end apart: 40, of which 15 were waited for; matrix products, arithmetic and copies ran while one was open for 0% of the time, Pallas kernels for 17%

profile of v3, /device:TPU:2, one launch (start us, length us, event | category | flops | bytes accessed | tf_op | source)
XLA Modules:
  0.0 304.2 jit_solution(4735788370396923300)
XLA Ops:
  0.1 14.5 %shard_map.46 = bf16[2,3072,1536]{2,1,0:T(8,128)(2,1)} custom-call(s32[3]{0:T(128)S(1)} %get-tuple-element.112.s, bf16[6144,1536]{1,0:T(8,128)(2,1)} %bitcast.26), custom_call_target="tpu_custom_call" | custom-call | flops 1179648 | bytes 9216 | tf_op jit(solution)/shard_map/pallas_call | solution.py:204
  22.8 16.6 %collective-permute-done.3 = bf16[1024,256]{1,0:T(8,128)(2,1)S(1)} collective-permute-done((bf16[1024,256]{1,0:T(8,128)(2,1)S(1)}, bf16[1024,256]{1,0:T(8,128)(2,1)S(1)}, u32[]{:S(2)}, u32[]{:S(2)}) %collective-permute-start.3) | collective-permute-done | bytes 524320 | tf_op jit(solution)/shard_map/ppermute | solution.py:391
  40.6 5.9 %shard_map.51.slope_ref.refs_1_ = f32[3072,256]{1,0:T(8,128)S(1)} custom-call(s32[3]{0:T(128)S(1)} %get-tuple-element.83.s, f32[512,6144]{1,0:T(8,128)} %bitcast.35), custom_call_target="tpu_custom_call" | custom-call | flops 192 | bytes 1536 | tf_op jit(solution)/shard_map/pallas_call | solution.py:230
  58.4 5.9 %shard_map.55.slope_ref.refs_1_ = f32[3072,256]{1,0:T(8,128)S(1)} custom-call(s32[3]{0:T(128)S(1)} %get-tuple-element.83.s, f32[512,6144]{1,0:T(8,128)} %bitcast.36), custom_call_target="tpu_custom_call" | custom-call | flops 192 | bytes 1536 | tf_op jit(solution)/shard_map/pallas_call | solution.py:230
  67.4 33.8 %collective-permute-done.9.refs_0_ = bf16[384,256]{1,0:T(8,128)(2,1)S(1)} collective-permute-done((bf16[384,256]{1,0:T(8,128)(2,1)S(1)}, bf16[384,256]{1,0:T(8,128)(2,1)S(1)}, u32[]{:S(2)}, u32[]{:S(2)}) %collective-permute-start.9) | collective-permute-done | bytes 196640 | tf_op jit(solution)/shard_map/ppermute | solution.py:400
  103.9 5.4 %collective-permute-start.14 = (bf16[384,256]{1,0:T(8,128)(2,1)S(1)}, bf16[384,256]{1,0:T(8,128)(2,1)S(1)}, u32[]{:S(2)}, u32[]{:S(2)}) collective-permute-start(bf16[384,256]{1,0:T(8,128)(2,1)S(1)} %collective-permute-done.9.refs_0_), channel_id=1, source_target_pairs={{16,28},{20,24},{24,20},{28,16},{17,29},{21,25},{25,21},{29,17},{1... | collective-permute-start | bytes 589832 | tf_op jit(solution)/shard_map/ppermute | solution.py:345
  115.4 10.2 %collective-permute-done.13.refs_2_ = bf16[384,256]{1,0:T(8,128)(2,1)S(1)} collective-permute-done((bf16[384,256]{1,0:T(8,128)(2,1)S(1)}, bf16[384,256]{1,0:T(8,128)(2,1)S(1)}, u32[]{:S(2)}, u32[]{:S(2)}) %collective-permute-start.13) | collective-permute-done | bytes 196640 | tf_op jit(solution)/shard_map/ppermute | solution.py:345
  128.6 5.6 %shard_map.60.refs_1_ = f32[3072,256]{1,0:T(8,128)S(1)} custom-call(s32[3]{0:T(128)S(1)} %get-tuple-element.112.s, bf16[6144,1536]{1,0:T(8,128)(2,1)} %bitcast.31, bf16[1536,256]{1,0:T(8,128)(2,1)S(1)} %get-tuple-element.89.refs_0_), custom_call_target="tpu_custom_call" | custom-call | flops 589824 | bytes 2304 | tf_op jit(solution)/shard_map/pallas_call | solution.py:104
  136.0 8.2 %shard_map.61 = (f32[3072,256]{1,0:T(8,128)S(1)}, bf16[3072,256]{1,0:T(8,128)(2,1)}) custom-call(s32[3]{0:T(128)S(1)} %get-tuple-element.112.s, bf16[6144,1536]{1,0:T(8,128)(2,1)} %bitcast.32, bf16[1536,256]{1,0:T(8,128)(2,1)S(1)} %collective-permute-done.15.refs_0_, f32[3072,256]{1,0:T(8,128)} %copy-done.4), custom_call_target="tpu_custom_call" | custom-call | flops 589824 | bytes 2304 | tf_op jit(solution)/shard_map/pallas_call | solution.py:104
  154.8 12.0 %collective-permute-done.19.refs_0_ = bf16[384,256]{1,0:T(8,128)(2,1)S(1)} collective-permute-done((bf16[384,256]{1,0:T(8,128)(2,1)S(1)}, bf16[384,256]{1,0:T(8,128)(2,1)S(1)}, u32[]{:S(2)}, u32[]{:S(2)}) %collective-permute-start.19) | collective-permute-done | bytes 196640 | tf_op jit(solution)/shard_map/ppermute | solution.py:400
  166.8 5.9 %collective-permute-done.21.refs_2_ = bf16[384,256]{1,0:T(8,128)(2,1)S(1)} collective-permute-done((bf16[384,256]{1,0:T(8,128)(2,1)S(1)}, bf16[384,256]{1,0:T(8,128)(2,1)S(1)}, u32[]{:S(2)}, u32[]{:S(2)}) %collective-permute-start.21) | collective-permute-done | bytes 196640 | tf_op jit(solution)/shard_map/ppermute | solution.py:400
  175.6 5.6 %shard_map.63.refs_1_ = f32[3072,256]{1,0:T(8,128)S(1)} custom-call(s32[3]{0:T(128)S(1)} %get-tuple-element.112.s, bf16[6144,1536]{1,0:T(8,128)(2,1)} %bitcast.33, bf16[1536,256]{1,0:T(8,128)(2,1)S(1)} %get-tuple-element.95.refs_0_), custom_call_target="tpu_custom_call" | custom-call | flops 589824 | bytes 2304 | tf_op jit(solution)/shard_map/pallas_call | solution.py:104
  183.0 7.1 %shard_map.64 = (f32[3072,256]{1,0:T(8,128)S(1)}, bf16[3072,256]{1,0:T(8,128)(2,1)S(1)}) custom-call(s32[3]{0:T(128)S(1)} %get-tuple-element.112.s, bf16[6144,1536]{1,0:T(8,128)(2,1)} %bitcast.34, bf16[1536,256]{1,0:T(8,128)(2,1)S(1)} %collective-permute-done.23.refs_0_, f32[3072,256]{1,0:T(8,128)} %copy-done.3), custom_call_target="tpu_custom_call" | custom-call | flops 589824 | bytes 2304 | tf_op jit(solution)/shard_map/pallas_call | solution.py:104
  190.1 7.3 %shard_map.65 = (f32[1536,256]{1,0:T(8,128)S(1)}, bf16[3072,256]{1,0:T(8,128)(2,1)S(1)}) custom-call(s32[3]{0:T(128)S(1)} %get-tuple-element.112.s, bf16[1536,6144]{1,0:T(8,128)(2,1)} %bitcast.22, f32[3072,256]{1,0:T(8,128)S(1)} %get-tuple-element.90.refs_0_, f32[3072,256]{1,0:T(8,128)} %copy-done.2, bf16[3072,256]{1,0:T(8,128)(2,1)} %collective-permute-done.24.refs_2_), custom_call_target="tpu_custom_call" | custom-call | flops 589824 | bytes 2304 | tf_op jit(solution)/shard_map/pallas_call | solution.py:104
  202.8 5.5 %shard_map.66 = (bf16[384,256]{1,0:T(8,128)(2,1)S(1)}, bf16[384,256]{1,0:T(8,128)(2,1)S(1)}, bf16[384,256]{1,0:T(8,128)(2,1)S(1)}, f32[384,256]{1,0:T(8,128)S(1)}) custom-call(s32[3]{0:T(128)S(1)} %get-tuple-element.112.s, bf16[1536,6144]{1,0:T(8,128)(2,1)} %bitcast.23, bf16[3072,256]{1,0:T(8,128)(2,1)S(1)} %get-tuple-element.99.refs_0_, ...), custom_call_target="tpu_custom_call" | custom-call | flops 589824 | bytes 2304 | tf_op jit(solution)/shard_map/pallas_call | solution.py:104
  210.7 4.3 %collective-permute-start.28 = (bf16[384,256]{1,0:T(8,128)(2,1)S(1)}, bf16[384,256]{1,0:T(8,128)(2,1)S(1)}, u32[]{:S(2)}, u32[]{:S(2)}) collective-permute-start(bf16[384,256]{1,0:T(8,128)(2,1)S(1)} %get-tuple-element.105), channel_id=1, source_target_pairs={{16,28},{20,24},{24,20},{28,16},{17,29},{21,25},{25,21},{29,17},{1... | collective-permute-start | bytes 589832 | tf_op jit(solution)/shard_map/ppermute | solution.py:345
  217.5 9.1 %collective-permute-done.27 = bf16[384,256]{1,0:T(8,128)(2,1)S(1)} collective-permute-done((bf16[384,256]{1,0:T(8,128)(2,1)S(1)}, bf16[384,256]{1,0:T(8,128)(2,1)S(1)}, u32[]{:S(2)}, u32[]{:S(2)}) %collective-permute-start.27) | collective-permute-done | bytes 196640 | tf_op jit(solution)/shard_map/ppermute | solution.py:345
  226.7 4.1 %collective-permute-done.26 = bf16[384,256]{1,0:T(8,128)(2,1)S(1)} collective-permute-done((bf16[384,256]{1,0:T(8,128)(2,1)S(1)}, bf16[384,256]{1,0:T(8,128)(2,1)S(1)}, u32[]{:S(2)}, u32[]{:S(2)}) %collective-permute-start.26) | collective-permute-done | bytes 196640 | tf_op jit(solution)/shard_map/ppermute | solution.py:345
  230.9 7.1 %collective-permute-done.29.refs_2_ = bf16[3072,256]{1,0:T(8,128)(2,1)S(1)} collective-permute-done((bf16[3072,256]{1,0:T(8,128)(2,1)S(1)}, bf16[3072,256]{1,0:T(8,128)(2,1)S(1)}, u32[]{:S(2)}, u32[]{:S(2)}) %collective-permute-start.29) | collective-permute-done | bytes 1572896 | tf_op jit(solution)/shard_map/ppermute | solution.py:345
  238.0 6.8 %shard_map.67 = (f32[1536,256]{1,0:T(8,128)S(1)}, bf16[3072,256]{1,0:T(8,128)(2,1)S(1)}) custom-call(s32[3]{0:T(128)S(1)} %get-tuple-element.112.s, bf16[1536,6144]{1,0:T(8,128)(2,1)} %bitcast.24, f32[3072,256]{1,0:T(8,128)S(1)} %get-tuple-element.96.refs_0_, f32[3072,256]{1,0:T(8,128)} %copy-done.1, bf16[3072,256]{1,0:T(8,128)(2,1)S(1)} %collective-permute-done.29.refs_2_), custom_call_target="tpu_custom_call" | custom-call | flops 589824 | bytes 2304 | tf_op jit(solution)/shard_map/pallas_call | solution.py:104
  251.2 5.5 %shard_map.68 = (bf16[384,256]{1,0:T(8,128)(2,1)S(1)}, bf16[384,256]{1,0:T(8,128)(2,1)S(1)}, bf16[384,256]{1,0:T(8,128)(2,1)S(1)}, f32[384,256]{1,0:T(8,128)S(1)}) custom-call(s32[3]{0:T(128)S(1)} %get-tuple-element.112.s, bf16[1536,6144]{1,0:T(8,128)(2,1)} %bitcast.25, bf16[3072,256]{1,0:T(8,128)(2,1)S(1)} %get-tuple-element.109.refs_0_, ...), custom_call_target="tpu_custom_call" | custom-call | flops 589824 | bytes 2304 | tf_op jit(solution)/shard_map/pallas_call | solution.py:104
  265.9 9.6 %collective-permute-done.32.refs_4_ = bf16[384,256]{1,0:T(8,128)(2,1)S(1)} collective-permute-done((bf16[384,256]{1,0:T(8,128)(2,1)S(1)}, bf16[384,256]{1,0:T(8,128)(2,1)S(1)}, u32[]{:S(2)}, u32[]{:S(2)}) %collective-permute-start.32) | collective-permute-done | bytes 196640 | tf_op jit(solution)/shard_map/ppermute | solution.py:349
  286.1 5.1 %collective-permute-done.39.refs_6_ = bf16[384,256]{1,0:T(8,128)(2,1)S(1)} collective-permute-done((bf16[384,256]{1,0:T(8,128)(2,1)S(1)}, bf16[384,256]{1,0:T(8,128)(2,1)S(1)}, u32[]{:S(2)}, u32[]{:S(2)}) %collective-permute-start.39) | collective-permute-done | bytes 196640 | tf_op jit(solution)/shard_map/ppermute | solution.py:349
  291.2 10.2 %collective-permute-done.38.refs_5_ = bf16[384,256]{1,0:T(8,128)(2,1)S(1)} collective-permute-done((bf16[384,256]{1,0:T(8,128)(2,1)S(1)}, bf16[384,256]{1,0:T(8,128)(2,1)S(1)}, u32[]{:S(2)}, u32[]{:S(2)}) %collective-permute-start.38) | collective-permute-done | bytes 196640 | tf_op jit(solution)/shard_map/ppermute | solution.py:349
  (101 shorter events, 92.4 us)
Async XLA Ops:
  19.0 20.3 %collective-permute-start.3 = (bf16[1024,256]{1,0:T(8,128)(2,1)S(1)}, bf16[1024,256]{1,0:T(8,128)(2,1)S(1)}, u32[]{:S(2)}, u32[]{:S(2)}) collective-permute-start(bf16[1024,256]{1,0:T(8,128)(2,1)S(1)} %get-tuple-element.75), channel_id=1, source_target_pairs={{0,18},{1,19},{2,16},{3,17},{4,22},{5,23},{6,20},{7,21},{8,26},{9,... | collective-permute-start | bytes 1572872 | tf_op jit(solution)/shard_map/ppermute | solution.py:391
  20.3 27.9 %collective-permute-start.2 = (bf16[2048,256]{1,0:T(8,128)(2,1)}, bf16[2048,256]{1,0:T(8,128)(2,1)S(1)}, u32[]{:S(2)}, u32[]{:S(2)}) collective-permute-start(bf16[2048,256]{1,0:T(8,128)(2,1)} %get-tuple-element.74), channel_id=1, source_target_pairs={{0,2},{1,3},{2,0},{3,1},{4,6},{5,7},{6,4},{7,5},{8,10},{9,11},{10,... | collective-permute-start | bytes 3145736 | tf_op jit(solution)/shard_map/ppermute | solution.py:345
  39.3 12.4 %collective-permute-start.4 = (bf16[1024,256]{1,0:T(8,128)(2,1)S(1)}, bf16[1024,256]{1,0:T(8,128)(2,1)S(1)}, u32[]{:S(2)}, u32[]{:S(2)}) collective-permute-start(bf16[1024,256]{1,0:T(8,128)(2,1)S(1)} %collective-permute-done.3), channel_id=1, source_target_pairs={{16,0},{17,1},{18,2},{19,3},{20,4},{21,5},{22,6},{23,7},{24,8},{25... | collective-permute-start | bytes 1572872 | tf_op jit(solution)/shard_map/ppermute | solution.py:395
  54.4 46.8 %collective-permute-start.10 = (bf16[3072,256]{1,0:T(8,128)(2,1)}, bf16[3072,256]{1,0:T(8,128)(2,1)S(1)}, u32[]{:S(2)}, u32[]{:S(2)}) collective-permute-start(bf16[3072,256]{1,0:T(8,128)(2,1)} %get-tuple-element.85), channel_id=1, source_target_pairs={{0,2},{1,3},{2,0},{3,1},{4,6},{5,7},{6,4},{7,5},{8,10},{9,11},{10,... | collective-permute-start | bytes 4718600 | tf_op jit(solution)/shard_map/ppermute | solution.py:345
  66.1 35.1 %collective-permute-start.9 = (bf16[384,256]{1,0:T(8,128)(2,1)S(1)}, bf16[384,256]{1,0:T(8,128)(2,1)S(1)}, u32[]{:S(2)}, u32[]{:S(2)}) collective-permute-start(bf16[384,256]{1,0:T(8,128)(2,1)S(1)} %add_convert_fusion.3), channel_id=1, source_target_pairs={{0,16},{4,20},{8,24},{12,28},{1,17},{5,21},{9,25},{13,29},{2,18},{... | collective-permute-start | bytes 589832 | tf_op jit(solution)/shard_map/ppermute | solution.py:400
  109.3 16.4 %collective-permute-start.13 = (bf16[384,256]{1,0:T(8,128)(2,1)S(1)}, bf16[384,256]{1,0:T(8,128)(2,1)S(1)}, u32[]{:S(2)}, u32[]{:S(2)}) collective-permute-start(bf16[384,256]{1,0:T(8,128)(2,1)S(1)} %collective-permute-done.9.refs_0_), channel_id=1, source_target_pairs={{16,24},{20,28},{24,16},{28,20},{17,25},{21,29},{25,17},{29,21},{1... | collective-permute-start | bytes 589832 | tf_op jit(solution)/shard_map/ppermute | solution.py:345
  111.2 14.5 %collective-permute-start.12 = (bf16[384,256]{1,0:T(8,128)(2,1)S(1)}, bf16[384,256]{1,0:T(8,128)(2,1)S(1)}, u32[]{:S(2)}, u32[]{:S(2)}) collective-permute-start(bf16[384,256]{1,0:T(8,128)(2,1)S(1)} %collective-permute-done.9.refs_0_), channel_id=1, source_target_pairs={{16,20},{20,16},{24,28},{28,24},{17,21},{21,17},{25,29},{29,25},{1... | collective-permute-start | bytes 589832 | tf_op jit(solution)/shard_map/ppermute | solution.py:345
  144.2 45.9 %collective-permute-start.24 = (bf16[3072,256]{1,0:T(8,128)(2,1)}, bf16[3072,256]{1,0:T(8,128)(2,1)}, u32[]{:S(2)}, u32[]{:S(2)}) collective-permute-start(bf16[3072,256]{1,0:T(8,128)(2,1)} %get-tuple-element.98), channel_id=1, source_target_pairs={{16,18},{17,19},{18,16},{19,17},{20,22},{21,23},{22,20},{23,21},{2... | collective-permute-start | bytes 4718600 | tf_op jit(solution)/shard_map/ppermute | solution.py:345
  149.5 17.3 %collective-permute-start.19 = (bf16[384,256]{1,0:T(8,128)(2,1)S(1)}, bf16[384,256]{1,0:T(8,128)(2,1)S(1)}, u32[]{:S(2)}, u32[]{:S(2)}) collective-permute-start(bf16[384,256]{1,0:T(8,128)(2,1)S(1)} %add_convert_fusion.2), channel_id=1, source_target_pairs={{0,16},{4,20},{8,24},{12,28},{1,17},{5,21},{9,25},{13,29},{2,18},{... | collective-permute-start | bytes 589832 | tf_op jit(solution)/shard_map/ppermute | solution.py:400
  150.8 16.1 %collective-permute-start.22 = (bf16[384,256]{1,0:T(8,128)(2,1)S(1)}, bf16[384,256]{1,0:T(8,128)(2,1)S(1)}, u32[]{:S(2)}, u32[]{:S(2)}) collective-permute-start(bf16[384,256]{1,0:T(8,128)(2,1)S(1)} %add_convert_fusion.2), channel_id=1, source_target_pairs={{0,28},{4,24},{8,20},{12,16},{1,29},{5,25},{9,21},{13,17},{2,30},{... | collective-permute-start | bytes 589832 | tf_op jit(solution)/shard_map/ppermute | solution.py:400
  152.1 20.6 %collective-permute-start.21 = (bf16[384,256]{1,0:T(8,128)(2,1)S(1)}, bf16[384,256]{1,0:T(8,128)(2,1)S(1)}, u32[]{:S(2)}, u32[]{:S(2)}) collective-permute-start(bf16[384,256]{1,0:T(8,128)(2,1)S(1)} %add_convert_fusion.2), channel_id=1, source_target_pairs={{0,24},{4,28},{8,16},{12,20},{1,25},{5,29},{9,17},{13,21},{2,26},{... | collective-permute-start | bytes 589832 | tf_op jit(solution)/shard_map/ppermute | solution.py:400
  153.4 19.3 %collective-permute-start.20 = (bf16[384,256]{1,0:T(8,128)(2,1)S(1)}, bf16[384,256]{1,0:T(8,128)(2,1)S(1)}, u32[]{:S(2)}, u32[]{:S(2)}) collective-permute-start(bf16[384,256]{1,0:T(8,128)(2,1)S(1)} %add_convert_fusion.2), channel_id=1, source_target_pairs={{0,20},{4,16},{8,28},{12,24},{1,21},{5,17},{9,29},{13,25},{2,22},{... | collective-permute-start | bytes 589832 | tf_op jit(solution)/shard_map/ppermute | solution.py:400
  199.8 38.2 %collective-permute-start.29 = (bf16[3072,256]{1,0:T(8,128)(2,1)S(1)}, bf16[3072,256]{1,0:T(8,128)(2,1)S(1)}, u32[]{:S(2)}, u32[]{:S(2)}) collective-permute-start(bf16[3072,256]{1,0:T(8,128)(2,1)S(1)} %get-tuple-element.108), channel_id=1, source_target_pairs={{16,18},{17,19},{18,16},{19,17},{20,22},{21,23},{22,20},{23,21},{2... | collective-permute-start | bytes 4718600 | tf_op jit(solution)/shard_map/ppermute | solution.py:345
  208.3 18.4 %collective-permute-start.27 = (bf16[384,256]{1,0:T(8,128)(2,1)S(1)}, bf16[384,256]{1,0:T(8,128)(2,1)S(1)}, u32[]{:S(2)}, u32[]{:S(2)}) collective-permute-start(bf16[384,256]{1,0:T(8,128)(2,1)S(1)} %get-tuple-element.104), channel_id=1, source_target_pairs={{16,24},{20,28},{24,16},{28,20},{17,25},{21,29},{25,17},{29,21},{1... | collective-permute-start | bytes 589832 | tf_op jit(solution)/shard_map/ppermute | solution.py:345
  210.7 16.0 %collective-permute-start.28 = (bf16[384,256]{1,0:T(8,128)(2,1)S(1)}, bf16[384,256]{1,0:T(8,128)(2,1)S(1)}, u32[]{:S(2)}, u32[]{:S(2)}) collective-permute-start(bf16[384,256]{1,0:T(8,128)(2,1)S(1)} %get-tuple-element.105), channel_id=1, source_target_pairs={{16,28},{20,24},{24,20},{28,16},{17,29},{21,25},{25,21},{29,17},{1... | collective-permute-start | bytes 589832 | tf_op jit(solution)/shard_map/ppermute | solution.py:345
  214.9 15.8 %collective-permute-start.26 = (bf16[384,256]{1,0:T(8,128)(2,1)S(1)}, bf16[384,256]{1,0:T(8,128)(2,1)S(1)}, u32[]{:S(2)}, u32[]{:S(2)}) collective-permute-start(bf16[384,256]{1,0:T(8,128)(2,1)S(1)} %get-tuple-element.102), channel_id=1, source_target_pairs={{16,20},{20,16},{24,28},{28,24},{17,21},{21,17},{25,29},{29,25},{1... | collective-permute-start | bytes 589832 | tf_op jit(solution)/shard_map/ppermute | solution.py:345
  246.7 16.2 %collective-permute-start.33 = (bf16[384,256]{1,0:T(8,128)(2,1)S(1)}, bf16[384,256]{1,0:T(8,128)(2,1)S(1)}, u32[]{:S(2)}, u32[]{:S(2)}) collective-permute-start(bf16[384,256]{1,0:T(8,128)(2,1)S(1)} %fusion.refs_2_), channel_id=1, source_target_pairs={{0,12},{4,8},{8,4},{12,0},{1,13},{5,9},{9,5},{13,1},{2,14},{6,10},... | collective-permute-start | bytes 589832 | tf_op jit(solution)/shard_map/ppermute | solution.py:349
  248.5 27.0 %collective-permute-start.32 = (bf16[384,256]{1,0:T(8,128)(2,1)S(1)}, bf16[384,256]{1,0:T(8,128)(2,1)S(1)}, u32[]{:S(2)}, u32[]{:S(2)}) collective-permute-start(bf16[384,256]{1,0:T(8,128)(2,1)S(1)} %fusion.refs_2_), channel_id=1, source_target_pairs={{0,8},{4,12},{8,0},{12,4},{1,9},{5,13},{9,1},{13,5},{2,10},{6,14},... | collective-permute-start | bytes 589832 | tf_op jit(solution)/shard_map/ppermute | solution.py:349
  248.7 26.8 %collective-permute-start.31 = (bf16[384,256]{1,0:T(8,128)(2,1)S(1)}, bf16[384,256]{1,0:T(8,128)(2,1)S(1)}, u32[]{:S(2)}, u32[]{:S(2)}) collective-permute-start(bf16[384,256]{1,0:T(8,128)(2,1)S(1)} %fusion.refs_2_), channel_id=1, source_target_pairs={{0,4},{4,0},{8,12},{12,8},{1,5},{5,1},{9,13},{13,9},{2,6},{6,2},{1... | collective-permute-start | bytes 589832 | tf_op jit(solution)/shard_map/ppermute | solution.py:349
  256.7 23.0 %collective-permute-start.35 = (bf16[384,256]{1,0:T(8,128)(2,1)S(1)}, bf16[384,256]{1,0:T(8,128)(2,1)S(1)}, u32[]{:S(2)}, u32[]{:S(2)}) collective-permute-start(bf16[384,256]{1,0:T(8,128)(2,1)S(1)} %get-tuple-element.117), channel_id=1, source_target_pairs={{16,24},{20,28},{24,16},{28,20},{17,25},{21,29},{25,17},{29,21},{1... | collective-permute-start | bytes 589832 | tf_op jit(solution)/shard_map/ppermute | solution.py:345
  258.9 20.8 %collective-permute-start.36 = (bf16[384,256]{1,0:T(8,128)(2,1)S(1)}, bf16[384,256]{1,0:T(8,128)(2,1)S(1)}, u32[]{:S(2)}, u32[]{:S(2)}) collective-permute-start(bf16[384,256]{1,0:T(8,128)(2,1)S(1)} %get-tuple-element.118), channel_id=1, source_target_pairs={{16,28},{20,24},{24,20},{28,16},{17,29},{21,25},{25,21},{29,17},{1... | collective-permute-start | bytes 589832 | tf_op jit(solution)/shard_map/ppermute | solution.py:345
  262.9 18.6 %collective-permute-start.34 = (bf16[384,256]{1,0:T(8,128)(2,1)S(1)}, bf16[384,256]{1,0:T(8,128)(2,1)S(1)}, u32[]{:S(2)}, u32[]{:S(2)}) collective-permute-start(bf16[384,256]{1,0:T(8,128)(2,1)S(1)} %get-tuple-element.111), channel_id=1, source_target_pairs={{16,20},{20,16},{24,28},{28,24},{17,21},{21,17},{25,29},{29,25},{1... | collective-permute-start | bytes 589832 | tf_op jit(solution)/shard_map/ppermute | solution.py:345
  283.2 18.3 %collective-permute-start.38 = (bf16[384,256]{1,0:T(8,128)(2,1)S(1)}, bf16[384,256]{1,0:T(8,128)(2,1)S(1)}, u32[]{:S(2)}, u32[]{:S(2)}) collective-permute-start(bf16[384,256]{1,0:T(8,128)(2,1)S(1)} %fusion.1.refs_3_), channel_id=1, source_target_pairs={{0,8},{4,12},{8,0},{12,4},{1,9},{5,13},{9,1},{13,5},{2,10},{6,14},... | collective-permute-start | bytes 589832 | tf_op jit(solution)/shard_map/ppermute | solution.py:349
  285.7 15.7 %collective-permute-start.37 = (bf16[384,256]{1,0:T(8,128)(2,1)S(1)}, bf16[384,256]{1,0:T(8,128)(2,1)S(1)}, u32[]{:S(2)}, u32[]{:S(2)}) collective-permute-start(bf16[384,256]{1,0:T(8,128)(2,1)S(1)} %fusion.1.refs_3_), channel_id=1, source_target_pairs={{0,4},{4,0},{8,12},{12,8},{1,5},{5,1},{9,13},{13,9},{2,6},{6,2},{1... | collective-permute-start | bytes 589832 | tf_op jit(solution)/shard_map/ppermute | solution.py:349
  (23 other events, 154.9 us)

commit v4 on v3

--- a/solution.py
+++ b/solution.py
@@ -122,6 +122,61 @@
     )(flags, mat, *sources, *([] if base is None else [base]))
 
 
+def pair_product(flags, mat, rows, own, other):
+    _, height, depth = mat.shape
+    tokens = own.shape[1]
+    steps = height // rows
+    slots = min(3, steps)
+
+    def body(s, mat_ref, own_ref, other_ref, full_ref, low_ref, buf, sem):
+        def fetch(i):
+            piece = mat_ref.at[:, pl.ds(pl.multiple_of(i * rows, 16), rows)]
+            slot = lax.rem(i, slots)
+            return pltpu.make_async_copy(piece, buf.at[slot], sem.at[slot])
+
+        @pl.when(s[0] == 1)
+        def _():
+            for i in range(slots):
+                fetch(i).start()
+
+            @pl.loop(0, steps)
+            def _(i):
+                fetch(i).wait()
+                slot = lax.rem(i, slots)
+                got = jnp.dot(buf[slot, s[1]], own_ref[...], preferred_element_type=F32)
+                got = got + jnp.dot(
+                    buf[slot, 1 - s[1]], other_ref[...], preferred_element_type=F32
+                )
+
+                @pl.when(i + slots < steps)
+                def _():
+                    fetch(i + slots).start()
+
+                at = pl.ds(pl.multiple_of(i * rows, 16), rows)
+                full_ref[at] = got
+                low_ref[at] = got.astype(LOW)
+
+    return pl.pallas_call(
+        body,
+        in_specs=[SMEM, ANY, VMEM, VMEM],
+        out_specs=[VMEM, VMEM],
+        out_shape=[
+            jax.ShapeDtypeStruct((height, tokens), F32),
+            jax.ShapeDtypeStruct((height, tokens), LOW),
+        ],
+        scratch_shapes=[
+            pltpu.VMEM((slots, 2, rows, depth), LOW),
+            pltpu.SemaphoreType.DMA((slots,)),
+        ],
+        compiler_params=params(),
+        cost_estimate=pl.CostEstimate(
+            flops=4 * tokens * height * depth // WEIGHT,
+            bytes_accessed=4 * height * depth // WEIGHT,
+            transcendentals=0,
+        ),
+    )(flags, mat, own, other)
+
+
 def turned(right_ref, grad_ref):
     right_ref[...] = grad_ref[...].T.astype(LOW)
 
@@ -217,7 +272,7 @@
             flops=2 * rows * step * cols // WEIGHT, bytes_accessed=4 * rows * cols // WEIGHT, transcendentals=0
         ),
     )(flags, mat)
-    return out.reshape(rows, cols)
+    return out
 
 
 def slope_of(flags, pre, start, tokens, half):
@@ -415,9 +470,10 @@
             base, lambda i, s: part_of(i, s) * part_rows, True,
         )
 
-    def scatter_hid(active, parts):
-        *others, own = parts
-        got = [within(active, d + 1, part, "hid") for d, part in enumerate(others)]
+    def send_parts(active, parts):
+        return [within(active, d + 1, part, "hid") for d, part in enumerate(parts[:-1])]
+
+    def sum_hid(active, own, got):
         for part in got:
             own = own + part.astype(F32)
         distance = PARTS
@@ -438,7 +494,7 @@
     steps = Steps()
     steps.last = split_out
     hidden_full, hidden_other, slopes, parts_out, terms, gathered = {}, {}, {}, {}, {}, {}
-    lows, core_got = {}, {}
+    lows, core_got, parts_got = {}, {}, {}
     up_full, up_other, up_parts, up_terms, lasts = {}, {}, {}, {}, {}
 
     def down_send(k):
@@ -478,11 +534,11 @@
         parts_out[k] = product_parts(
             down, lambda i, s: (i * part_rows, (1 - s[1]) * half), swapped, tokens, partial
         )
+        parts_got[k] = send_parts(0, parts_out[k])
         steps.last = parts_out[k][0]
 
     def cross(k):
-        *others, own = parts_out[k]
-        terms[k] = scatter_hid(0, others + [steps.after(own)])
+        terms[k] = sum_hid(0, steps.after(parts_out[k][-1]), parts_got[k])
         if k == 0:
             crossed = across(terms[k], 0)
             steps.last = crossed
@@ -495,16 +551,13 @@
         tokens = sizes[k]
         low, up_terms[k] = join(steps.after(up), grads[k], gathered[k])
         low_other = within(1, 1, low)
-        (partial,) = product_out(
-            up, split_out, lambda s: s[1] * half, [low], None, tokens, [(half, 0, F32)]
-        )
-        full, *pieces = product_out(
-            up, split_out, lambda s: (1 - s[1]) * half, [low_other], None, tokens,
-            in_pieces(1), partial,
-        )
+        flags = up
+        if k + 1 in parts_got:
+            flags = lax.optimization_barrier((up, *parts_got[k + 1]))[0]
+        full, low_grad = pair_product(flags, split_out, hid_rows, low, low_other)
         steps.last = full
         up_full[k] = full
-        up_other[k] = exchange(1, pieces, up_other[k - 1][0] if k else None)
+        up_other[k] = exchange(1, [low_grad], up_other[k - 1][0] if k else None)
 
     def place(part, core):
         row = core * (PARTS // 2) + lax.rem(part, PARTS // 2)
@@ -521,10 +574,11 @@
         steps.last = up_parts[k][0]
 
     def gather(k):
-        *others, own = up_parts[k]
-        last = jnp.where(is_up, scatter_hid(1, others + [steps.after(own)]), terms[k])
+        own = steps.after(up_parts[k][-1])
+        last = jnp.where(is_up, sum_hid(1, own, send_parts(1, up_parts[k])), terms[k])
         steps.last = last
         lasts[k] = [last] + [everywhere(d, last) for d in range(1, PARTS)]
+        steps.last = lasts[k][1]
 
     for k in chunks:
         down_send(k)

time: 305 us -> 299 us (0.980)
  Pallas kernels: 96.2 us -> 86.6 us
  waiting for transfers between devices: 131 us -> 139 us
  starting transfers between devices: 69.3 us -> 66 us
    pallas_call x16 -> x12, Pallas kernels: 58.5 us -> 31.9 us  [product(): pl.pallas_call(body, in_specs=[SMEM, ANY] + [VMEM if first is None else A...]
    pallas_call x0 -> x2, Pallas kernels: none -> 16.8 us  [pair_product(): pl.pallas_call(body, in_specs=[SMEM, ANY, VMEM, VMEM], out_specs=[VMEM, V...]
    ppermute x6, waiting for transfers between devices: 24.9 us -> 30 us  [everywhere(): return lax.ppermute(block, axis, [(i, i ^ distance) for i in range(size)])]
    ppermute x6, starting transfers between devices: 8.91 us -> 5.39 us  [everywhere(): return lax.ppermute(block, axis, [(i, i ^ distance) for i in range(size)])]
    ppermute x5, waiting for transfers between devices: 51.6 us -> 55.1 us  [across(): return lax.ppermute(term, ('section', 'hid'), pairs)]
    unnamed x14 -> x10, local copies, waits for them, and re-layouts: 6.75 us -> 4.28 us
  transfers between devices with their start and end apart: 40 -> 40, of which waited for: 15 -> 19; matrix products, arithmetic and copies ran while one was open for 0% -> 0% of each run, Pallas kernels for 17% -> 14%
where the time goes in v4:
time: 299 us; the launch traced here: 298 us
  waiting for transfers between devices  139 us (46%)
  Pallas kernels  86.6 us (29%)
  starting transfers between devices  66 us (22%)
  local copies, waits for them, and re-layouts  4.49 us (2%)
    ppermute x5, waiting for transfers between devices, across(): return lax.ppermute(term, ('section', 'hid'), pairs)  55.1 us
    ppermute x27, starting transfers between devices, within(): return lax.ppermute(block, ('section', axis), pairs)  51.5 us
    ppermute x27, waiting for transfers between devices, within(): return lax.ppermute(block, ('section', axis), pairs)  34.2 us
    pallas_call x12, Pallas kernels, product(): pl.pallas_call(body, in_specs=[SMEM, ANY] + [VMEM if first is None else A...  31.9 us
    ppermute x6, waiting for transfers between devices, everywhere(): return lax.ppermute(block, axis, [(i, i ^ distance) for i in range(size)])  30 us
    pallas_call x2, Pallas kernels, pair_product(): pl.pallas_call(body, in_specs=[SMEM, ANY, VMEM, VMEM], out_specs=[VMEM, V...  16.8 us
    ppermute x1, waiting for transfers between devices, detour(): lax.ppermute(piece, ('section', 'wid'), [(i, size + (i ^ 2)) for i in ran...  16.6 us
    pallas_call x1, Pallas kernels, split_rows(): pl.pallas_call(body, in_specs=[SMEM, ANY], out_specs=ANY, out_shape=jax.S...  14.5 us
  transfers between devices with their start and end apart: 40, of which 19 were waited for; matrix products, arithmetic and copies ran while one was open for 0% of the time, Pallas kernels for 14%

profile of v4, /device:TPU:2, one launch (start us, length us, event | category | flops | bytes accessed | tf_op | source)
XLA Modules:
  0.0 297.6 jit_solution(3443595953945359272)
XLA Ops:
  0.1 14.5 %shard_map.46.mat_ref = bf16[2,3072,1536]{2,1,0:T(8,128)(2,1)} custom-call(s32[3]{0:T(128)S(1)} %get-tuple-element.114.s, bf16[6144,1536]{1,0:T(8,128)(2,1)} %bitcast.25), custom_call_target="tpu_custom_call" | custom-call | flops 1179648 | bytes 9216 | tf_op jit(solution)/shard_map/pallas_call | solution.py:259
  22.8 16.6 %collective-permute-done.3 = bf16[1024,256]{1,0:T(8,128)(2,1)S(1)} collective-permute-done((bf16[1024,256]{1,0:T(8,128)(2,1)S(1)}, bf16[1024,256]{1,0:T(8,128)(2,1)S(1)}, u32[]{:S(2)}, u32[]{:S(2)}) %collective-permute-start.3) | collective-permute-done | bytes 524320 | tf_op jit(solution)/shard_map/ppermute | solution.py:446
  40.6 5.9 %shard_map.51.slope_ref.refs_1_ = f32[3072,256]{1,0:T(8,128)S(1)} custom-call(s32[3]{0:T(128)S(1)} %get-tuple-element.84.s, f32[512,6144]{1,0:T(8,128)} %bitcast.30), custom_call_target="tpu_custom_call" | custom-call | flops 192 | bytes 1536 | tf_op jit(solution)/shard_map/pallas_call | solution.py:285
  58.4 5.9 %shard_map.55.slope_ref.refs_1_ = f32[3072,256]{1,0:T(8,128)S(1)} custom-call(s32[3]{0:T(128)S(1)} %get-tuple-element.84.s, f32[512,6144]{1,0:T(8,128)} %bitcast.31), custom_call_target="tpu_custom_call" | custom-call | flops 192 | bytes 1536 | tf_op jit(solution)/shard_map/pallas_call | solution.py:285
  67.4 33.8 %collective-permute-done.9.refs_0_ = bf16[384,256]{1,0:T(8,128)(2,1)S(1)} collective-permute-done((bf16[384,256]{1,0:T(8,128)(2,1)S(1)}, bf16[384,256]{1,0:T(8,128)(2,1)S(1)}, u32[]{:S(2)}, u32[]{:S(2)}) %collective-permute-start.9) | collective-permute-done | bytes 196640 | tf_op jit(solution)/shard_map/ppermute | solution.py:455
  103.9 5.4 %collective-permute-start.17 = (bf16[384,256]{1,0:T(8,128)(2,1)S(1)}, bf16[384,256]{1,0:T(8,128)(2,1)S(1)}, u32[]{:S(2)}, u32[]{:S(2)}) collective-permute-start(bf16[384,256]{1,0:T(8,128)(2,1)S(1)} %collective-permute-done.9.refs_0_), channel_id=1, source_target_pairs={{16,28},{20,24},{24,20},{28,16},{17,29},{21,25},{25,21},{29,17},{1... | collective-permute-start | bytes 589832 | tf_op jit(solution)/shard_map/ppermute | solution.py:400
  115.4 10.2 %collective-permute-done.16.refs_2_ = bf16[384,256]{1,0:T(8,128)(2,1)S(1)} collective-permute-done((bf16[384,256]{1,0:T(8,128)(2,1)S(1)}, bf16[384,256]{1,0:T(8,128)(2,1)S(1)}, u32[]{:S(2)}, u32[]{:S(2)}) %collective-permute-start.16) | collective-permute-done | bytes 196640 | tf_op jit(solution)/shard_map/ppermute | solution.py:400
  130.9 8.4 %shard_map.60 = (f32[3072,256]{1,0:T(8,128)S(1)}, bf16[3072,256]{1,0:T(8,128)(2,1)S(1)}) custom-call(s32[3]{0:T(128)S(1)} %get-tuple-element.114.s, bf16[2,3072,1536]{2,1,0:T(8,128)(2,1)} %shard_map.46.mat_ref, bf16[1536,256]{1,0:T(8,128)(2,1)S(1)} %get-tuple-element.93.own_ref, bf16[1536,256]{1,0:T(8,128)(2,1)S(1)} %collective-permute-done.18.other_ref), custom_call_target="tpu_custom_call" | custom-call | flops 1179648 | bytes 4608 | tf_op jit(solution)/shard_map/pallas_call | solution.py:159
  151.3 5.0 %collective-permute-done.22.refs_3_ = bf16[384,256]{1,0:T(8,128)(2,1)S(1)} collective-permute-done((bf16[384,256]{1,0:T(8,128)(2,1)S(1)}, bf16[384,256]{1,0:T(8,128)(2,1)S(1)}, u32[]{:S(2)}, u32[]{:S(2)}) %collective-permute-start.22) | collective-permute-done | bytes 196640 | tf_op jit(solution)/shard_map/ppermute | solution.py:455
  156.3 12.7 %collective-permute-done.21.refs_2_ = bf16[384,256]{1,0:T(8,128)(2,1)S(1)} collective-permute-done((bf16[384,256]{1,0:T(8,128)(2,1)S(1)}, bf16[384,256]{1,0:T(8,128)(2,1)S(1)}, u32[]{:S(2)}, u32[]{:S(2)}) %collective-permute-start.21) | collective-permute-done | bytes 196640 | tf_op jit(solution)/shard_map/ppermute | solution.py:455
  175.3 8.4 %shard_map.62 = (f32[3072,256]{1,0:T(8,128)S(1)}, bf16[3072,256]{1,0:T(8,128)(2,1)S(1)}) custom-call(s32[3]{0:T(128)S(1)} %get-tuple-element.114.s, bf16[2,3072,1536]{2,1,0:T(8,128)(2,1)} %shard_map.46.mat_ref, bf16[1536,256]{1,0:T(8,128)(2,1)S(1)} %get-tuple-element.97.own_ref, bf16[1536,256]{1,0:T(8,128)(2,1)S(1)} %collective-permute-done.23.other_ref), custom_call_target="tpu_custom_call" | custom-call | flops 1179648 | bytes 4608 | tf_op jit(solution)/shard_map/pallas_call | solution.py:159
  183.7 7.3 %shard_map.63 = (f32[1536,256]{1,0:T(8,128)S(1)}, bf16[3072,256]{1,0:T(8,128)(2,1)S(1)}) custom-call(s32[3]{0:T(128)S(1)} %get-tuple-element.114.s, bf16[1536,6144]{1,0:T(8,128)(2,1)} %bitcast.21, f32[3072,256]{1,0:T(8,128)S(1)} %get-tuple-element.94.refs_0_, f32[3072,256]{1,0:T(8,128)} %copy-done.2, bf16[3072,256]{1,0:T(8,128)(2,1)} %collective-permute-done.24.refs_2_), custom_call_target="tpu_custom_call" | custom-call | flops 589824 | bytes 2304 | tf_op jit(solution)/shard_map/pallas_call | solution.py:104
  196.6 5.5 %shard_map.64 = (bf16[384,256]{1,0:T(8,128)(2,1)S(1)}, bf16[384,256]{1,0:T(8,128)(2,1)S(1)}, bf16[384,256]{1,0:T(8,128)(2,1)S(1)}, f32[384,256]{1,0:T(8,128)S(1)}) custom-call(s32[3]{0:T(128)S(1)} %get-tuple-element.114.s, bf16[1536,6144]{1,0:T(8,128)(2,1)} %bitcast.22, bf16[3072,256]{1,0:T(8,128)(2,1)S(1)} %get-tuple-element.101.refs_0_, ...), custom_call_target="tpu_custom_call" | custom-call | flops 589824 | bytes 2304 | tf_op jit(solution)/shard_map/pallas_call | solution.py:104
  206.7 4.6 %collective-permute-start.26 = (bf16[384,256]{1,0:T(8,128)(2,1)S(1)}, bf16[384,256]{1,0:T(8,128)(2,1)S(1)}, u32[]{:S(2)}, u32[]{:S(2)}) collective-permute-start(bf16[384,256]{1,0:T(8,128)(2,1)S(1)} %get-tuple-element.104), channel_id=1, source_target_pairs={{16,20},{20,16},{24,28},{28,24},{17,21},{21,17},{25,29},{29,25},{1... | collective-permute-start | bytes 589832 | tf_op jit(solution)/shard_map/ppermute | solution.py:400
  211.3 7.0 %collective-permute-done.27 = bf16[384,256]{1,0:T(8,128)(2,1)S(1)} collective-permute-done((bf16[384,256]{1,0:T(8,128)(2,1)S(1)}, bf16[384,256]{1,0:T(8,128)(2,1)S(1)}, u32[]{:S(2)}, u32[]{:S(2)}) %collective-permute-start.27) | collective-permute-done | bytes 196640 | tf_op jit(solution)/shard_map/ppermute | solution.py:400
  218.3 4.1 %collective-permute-done.26 = bf16[384,256]{1,0:T(8,128)(2,1)S(1)} collective-permute-done((bf16[384,256]{1,0:T(8,128)(2,1)S(1)}, bf16[384,256]{1,0:T(8,128)(2,1)S(1)}, u32[]{:S(2)}, u32[]{:S(2)}) %collective-permute-start.26) | collective-permute-done | bytes 196640 | tf_op jit(solution)/shard_map/ppermute | solution.py:400
  223.2 6.2 %collective-permute-done.29.refs_3_ = bf16[384,256]{1,0:T(8,128)(2,1)S(1)} collective-permute-done((bf16[384,256]{1,0:T(8,128)(2,1)S(1)}, bf16[384,256]{1,0:T(8,128)(2,1)S(1)}, u32[]{:S(2)}, u32[]{:S(2)}) %collective-permute-start.29) | collective-permute-done | bytes 196640 | tf_op jit(solution)/shard_map/ppermute | solution.py:404
  231.6 6.8 %shard_map.65 = (f32[1536,256]{1,0:T(8,128)S(1)}, bf16[3072,256]{1,0:T(8,128)(2,1)S(1)}) custom-call(s32[3]{0:T(128)S(1)} %get-tuple-element.114.s, bf16[1536,6144]{1,0:T(8,128)(2,1)} %bitcast.23, f32[3072,256]{1,0:T(8,128)S(1)} %get-tuple-element.98.refs_0_, f32[3072,256]{1,0:T(8,128)} %copy-done.1, bf16[3072,256]{1,0:T(8,128)(2,1)S(1)} %collective-permute-done.30.refs_2_), custom_call_target="tpu_custom_call" | custom-call | flops 589824 | bytes 2304 | tf_op jit(solution)/shard_map/pallas_call | solution.py:104
  243.7 5.5 %shard_map.66 = (bf16[384,256]{1,0:T(8,128)(2,1)S(1)}, bf16[384,256]{1,0:T(8,128)(2,1)S(1)}, bf16[384,256]{1,0:T(8,128)(2,1)S(1)}, f32[384,256]{1,0:T(8,128)S(1)}) custom-call(s32[3]{0:T(128)S(1)} %get-tuple-element.114.s, bf16[1536,6144]{1,0:T(8,128)(2,1)} %bitcast.24, bf16[3072,256]{1,0:T(8,128)(2,1)S(1)} %get-tuple-element.111.refs_0_, ...), custom_call_target="tpu_custom_call" | custom-call | flops 589824 | bytes 2304 | tf_op jit(solution)/shard_map/pallas_call | solution.py:104
  251.2 5.3 %collective-permute-start.36 = (bf16[384,256]{1,0:T(8,128)(2,1)S(1)}, bf16[384,256]{1,0:T(8,128)(2,1)S(1)}, u32[]{:S(2)}, u32[]{:S(2)}) collective-permute-start(bf16[384,256]{1,0:T(8,128)(2,1)S(1)} %get-tuple-element.120), channel_id=1, source_target_pairs={{16,28},{20,24},{24,20},{28,16},{17,29},{21,25},{25,21},{29,17},{1... | collective-permute-start | bytes 589832 | tf_op jit(solution)/shard_map/ppermute | solution.py:400
  258.5 9.0 %collective-permute-done.32.refs_4_ = bf16[384,256]{1,0:T(8,128)(2,1)S(1)} collective-permute-done((bf16[384,256]{1,0:T(8,128)(2,1)S(1)}, bf16[384,256]{1,0:T(8,128)(2,1)S(1)}, u32[]{:S(2)}, u32[]{:S(2)}) %collective-permute-start.32) | collective-permute-done | bytes 196640 | tf_op jit(solution)/shard_map/ppermute | solution.py:404
  271.6 3.8 %collective-permute-done.34 = bf16[384,256]{1,0:T(8,128)(2,1)S(1)} collective-permute-done((bf16[384,256]{1,0:T(8,128)(2,1)S(1)}, bf16[384,256]{1,0:T(8,128)(2,1)S(1)}, u32[]{:S(2)}, u32[]{:S(2)}) %collective-permute-start.34) | collective-permute-done | bytes 196640 | tf_op jit(solution)/shard_map/ppermute | solution.py:400
  280.0 5.3 %collective-permute-done.39.refs_6_ = bf16[384,256]{1,0:T(8,128)(2,1)S(1)} collective-permute-done((bf16[384,256]{1,0:T(8,128)(2,1)S(1)}, bf16[384,256]{1,0:T(8,128)(2,1)S(1)}, u32[]{:S(2)}, u32[]{:S(2)}) %collective-permute-start.39) | collective-permute-done | bytes 196640 | tf_op jit(solution)/shard_map/ppermute | solution.py:404
  285.3 9.5 %collective-permute-done.38.refs_5_ = bf16[384,256]{1,0:T(8,128)(2,1)S(1)} collective-permute-done((bf16[384,256]{1,0:T(8,128)(2,1)S(1)}, bf16[384,256]{1,0:T(8,128)(2,1)S(1)}, u32[]{:S(2)}, u32[]{:S(2)}) %collective-permute-start.38) | collective-permute-done | bytes 196640 | tf_op jit(solution)/shard_map/ppermute | solution.py:404
  (95 shorter events, 90.4 us)
Async XLA Ops:
  19.0 20.4 %collective-permute-start.3 = (bf16[1024,256]{1,0:T(8,128)(2,1)S(1)}, bf16[1024,256]{1,0:T(8,128)(2,1)S(1)}, u32[]{:S(2)}, u32[]{:S(2)}) collective-permute-start(bf16[1024,256]{1,0:T(8,128)(2,1)S(1)} %get-tuple-element.76), channel_id=1, source_target_pairs={{0,18},{1,19},{2,16},{3,17},{4,22},{5,23},{6,20},{7,21},{8,26},{9,... | collective-permute-start | bytes 1572872 | tf_op jit(solution)/shard_map/ppermute | solution.py:446
  20.3 27.9 %collective-permute-start.2 = (bf16[2048,256]{1,0:T(8,128)(2,1)}, bf16[2048,256]{1,0:T(8,128)(2,1)S(1)}, u32[]{:S(2)}, u32[]{:S(2)}) collective-permute-start(bf16[2048,256]{1,0:T(8,128)(2,1)} %get-tuple-element.75), channel_id=1, source_target_pairs={{0,2},{1,3},{2,0},{3,1},{4,6},{5,7},{6,4},{7,5},{8,10},{9,11},{10,... | collective-permute-start | bytes 3145736 | tf_op jit(solution)/shard_map/ppermute | solution.py:400
  39.3 12.4 %collective-permute-start.4 = (bf16[1024,256]{1,0:T(8,128)(2,1)S(1)}, bf16[1024,256]{1,0:T(8,128)(2,1)S(1)}, u32[]{:S(2)}, u32[]{:S(2)}) collective-permute-start(bf16[1024,256]{1,0:T(8,128)(2,1)S(1)} %collective-permute-done.3), channel_id=1, source_target_pairs={{16,0},{17,1},{18,2},{19,3},{20,4},{21,5},{22,6},{23,7},{24,8},{25... | collective-permute-start | bytes 1572872 | tf_op jit(solution)/shard_map/ppermute | solution.py:450
  54.4 46.8 %collective-permute-start.10 = (bf16[3072,256]{1,0:T(8,128)(2,1)}, bf16[3072,256]{1,0:T(8,128)(2,1)S(1)}, u32[]{:S(2)}, u32[]{:S(2)}) collective-permute-start(bf16[3072,256]{1,0:T(8,128)(2,1)} %get-tuple-element.86), channel_id=1, source_target_pairs={{0,2},{1,3},{2,0},{3,1},{4,6},{5,7},{6,4},{7,5},{8,10},{9,11},{10,... | collective-permute-start | bytes 4718600 | tf_op jit(solution)/shard_map/ppermute | solution.py:400
  66.1 35.1 %collective-permute-start.9 = (bf16[384,256]{1,0:T(8,128)(2,1)S(1)}, bf16[384,256]{1,0:T(8,128)(2,1)S(1)}, u32[]{:S(2)}, u32[]{:S(2)}) collective-permute-start(bf16[384,256]{1,0:T(8,128)(2,1)S(1)} %add_convert_fusion.3), channel_id=1, source_target_pairs={{0,16},{4,20},{8,24},{12,28},{1,17},{5,21},{9,25},{13,29},{2,18},{... | collective-permute-start | bytes 589832 | tf_op jit(solution)/shard_map/ppermute | solution.py:455
  103.1 11.7 %collective-permute-start.11 = (bf16[3072,256]{1,0:T(8,128)(2,1)S(1)}, bf16[3072,256]{1,0:T(8,128)(2,1)S(1)}, u32[]{:S(2)}, u32[]{:S(2)}) collective-permute-start(bf16[3072,256]{1,0:T(8,128)(2,1)S(1)} %shard_map.56.refs_0_), channel_id=1, source_target_pairs={{0,1},{1,0},{2,3},{3,2},{4,5},{5,4},{6,7},{7,6},{8,9},{9,8},{10,11... | collective-permute-start | bytes 4718600 | tf_op jit(solution)/shard_map/ppermute | solution.py:400
  103.9 11.6 %collective-permute-start.17 = (bf16[384,256]{1,0:T(8,128)(2,1)S(1)}, bf16[384,256]{1,0:T(8,128)(2,1)S(1)}, u32[]{:S(2)}, u32[]{:S(2)}) collective-permute-start(bf16[384,256]{1,0:T(8,128)(2,1)S(1)} %collective-permute-done.9.refs_0_), channel_id=1, source_target_pairs={{16,28},{20,24},{24,20},{28,16},{17,29},{21,25},{25,21},{29,17},{1... | collective-permute-start | bytes 589832 | tf_op jit(solution)/shard_map/ppermute | solution.py:400
  109.3 16.4 %collective-permute-start.16 = (bf16[384,256]{1,0:T(8,128)(2,1)S(1)}, bf16[384,256]{1,0:T(8,128)(2,1)S(1)}, u32[]{:S(2)}, u32[]{:S(2)}) collective-permute-start(bf16[384,256]{1,0:T(8,128)(2,1)S(1)} %collective-permute-done.9.refs_0_), channel_id=1, source_target_pairs={{16,24},{20,28},{24,16},{28,20},{17,25},{21,29},{25,17},{29,21},{1... | collective-permute-start | bytes 589832 | tf_op jit(solution)/shard_map/ppermute | solution.py:400
  111.2 14.5 %collective-permute-start.15 = (bf16[384,256]{1,0:T(8,128)(2,1)S(1)}, bf16[384,256]{1,0:T(8,128)(2,1)S(1)}, u32[]{:S(2)}, u32[]{:S(2)}) collective-permute-start(bf16[384,256]{1,0:T(8,128)(2,1)S(1)} %collective-permute-done.9.refs_0_), channel_id=1, source_target_pairs={{16,20},{20,16},{24,28},{28,24},{17,21},{21,17},{25,29},{29,25},{1... | collective-permute-start | bytes 589832 | tf_op jit(solution)/shard_map/ppermute | solution.py:400
  139.3 44.4 %collective-permute-start.24 = (bf16[3072,256]{1,0:T(8,128)(2,1)S(1)}, bf16[3072,256]{1,0:T(8,128)(2,1)}, u32[]{:S(2)}, u32[]{:S(2)}) collective-permute-start(bf16[3072,256]{1,0:T(8,128)(2,1)S(1)} %get-tuple-element.100), channel_id=1, source_target_pairs={{16,18},{17,19},{18,16},{19,17},{20,22},{21,23},{22,20},{23,21},{2... | collective-permute-start | bytes 4718600 | tf_op jit(solution)/shard_map/ppermute | solution.py:400
  143.8 12.5 %collective-permute-start.22 = (bf16[384,256]{1,0:T(8,128)(2,1)S(1)}, bf16[384,256]{1,0:T(8,128)(2,1)S(1)}, u32[]{:S(2)}, u32[]{:S(2)}) collective-permute-start(bf16[384,256]{1,0:T(8,128)(2,1)S(1)} %add_convert_fusion.2), channel_id=1, source_target_pairs={{0,28},{4,24},{8,20},{12,16},{1,29},{5,25},{9,21},{13,17},{2,30},{... | collective-permute-start | bytes 589832 | tf_op jit(solution)/shard_map/ppermute | solution.py:455
  145.1 23.9 %collective-permute-start.21 = (bf16[384,256]{1,0:T(8,128)(2,1)S(1)}, bf16[384,256]{1,0:T(8,128)(2,1)S(1)}, u32[]{:S(2)}, u32[]{:S(2)}) collective-permute-start(bf16[384,256]{1,0:T(8,128)(2,1)S(1)} %add_convert_fusion.2), channel_id=1, source_target_pairs={{0,24},{4,28},{8,16},{12,20},{1,25},{5,29},{9,17},{13,21},{2,26},{... | collective-permute-start | bytes 589832 | tf_op jit(solution)/shard_map/ppermute | solution.py:455
  146.4 22.6 %collective-permute-start.20 = (bf16[384,256]{1,0:T(8,128)(2,1)S(1)}, bf16[384,256]{1,0:T(8,128)(2,1)S(1)}, u32[]{:S(2)}, u32[]{:S(2)}) collective-permute-start(bf16[384,256]{1,0:T(8,128)(2,1)S(1)} %add_convert_fusion.2), channel_id=1, source_target_pairs={{0,20},{4,16},{8,28},{12,24},{1,21},{5,17},{9,29},{13,25},{2,22},{... | collective-permute-start | bytes 589832 | tf_op jit(solution)/shard_map/ppermute | solution.py:455
  193.0 38.6 %collective-permute-start.30 = (bf16[3072,256]{1,0:T(8,128)(2,1)S(1)}, bf16[3072,256]{1,0:T(8,128)(2,1)S(1)}, u32[]{:S(2)}, u32[]{:S(2)}) collective-permute-start(bf16[3072,256]{1,0:T(8,128)(2,1)S(1)} %get-tuple-element.110), channel_id=1, source_target_pairs={{16,18},{17,19},{18,16},{19,17},{20,22},{21,23},{22,20},{23,21},{2... | collective-permute-start | bytes 4718600 | tf_op jit(solution)/shard_map/ppermute | solution.py:400
  202.1 16.2 %collective-permute-start.27 = (bf16[384,256]{1,0:T(8,128)(2,1)S(1)}, bf16[384,256]{1,0:T(8,128)(2,1)S(1)}, u32[]{:S(2)}, u32[]{:S(2)}) collective-permute-start(bf16[384,256]{1,0:T(8,128)(2,1)S(1)} %get-tuple-element.106), channel_id=1, source_target_pairs={{16,24},{20,28},{24,16},{28,20},{17,25},{21,29},{25,17},{29,21},{1... | collective-permute-start | bytes 589832 | tf_op jit(solution)/shard_map/ppermute | solution.py:400
  204.0 14.3 %collective-permute-start.28 = (bf16[384,256]{1,0:T(8,128)(2,1)S(1)}, bf16[384,256]{1,0:T(8,128)(2,1)S(1)}, u32[]{:S(2)}, u32[]{:S(2)}) collective-permute-start(bf16[384,256]{1,0:T(8,128)(2,1)S(1)} %get-tuple-element.107), channel_id=1, source_target_pairs={{16,28},{20,24},{24,20},{28,16},{17,29},{21,25},{25,21},{29,17},{1... | collective-permute-start | bytes 589832 | tf_op jit(solution)/shard_map/ppermute | solution.py:400
  206.7 15.6 %collective-permute-start.26 = (bf16[384,256]{1,0:T(8,128)(2,1)S(1)}, bf16[384,256]{1,0:T(8,128)(2,1)S(1)}, u32[]{:S(2)}, u32[]{:S(2)}) collective-permute-start(bf16[384,256]{1,0:T(8,128)(2,1)S(1)} %get-tuple-element.104), channel_id=1, source_target_pairs={{16,20},{20,16},{24,28},{28,24},{17,21},{21,17},{25,29},{29,25},{1... | collective-permute-start | bytes 589832 | tf_op jit(solution)/shard_map/ppermute | solution.py:400
  240.4 18.1 %collective-permute-start.33 = (bf16[384,256]{1,0:T(8,128)(2,1)S(1)}, bf16[384,256]{1,0:T(8,128)(2,1)S(1)}, u32[]{:S(2)}, u32[]{:S(2)}) collective-permute-start(bf16[384,256]{1,0:T(8,128)(2,1)S(1)} %fusion.refs_2_), channel_id=1, source_target_pairs={{0,12},{4,8},{8,4},{12,0},{1,13},{5,9},{9,5},{13,1},{2,14},{6,10},... | collective-permute-start | bytes 589832 | tf_op jit(solution)/shard_map/ppermute | solution.py:404
  240.4 27.0 %collective-permute-start.32 = (bf16[384,256]{1,0:T(8,128)(2,1)S(1)}, bf16[384,256]{1,0:T(8,128)(2,1)S(1)}, u32[]{:S(2)}, u32[]{:S(2)}) collective-permute-start(bf16[384,256]{1,0:T(8,128)(2,1)S(1)} %fusion.refs_2_), channel_id=1, source_target_pairs={{0,8},{4,12},{8,0},{12,4},{1,9},{5,13},{9,1},{13,5},{2,10},{6,14},... | collective-permute-start | bytes 589832 | tf_op jit(solution)/shard_map/ppermute | solution.py:404
  249.2 22.4 %collective-permute-start.35 = (bf16[384,256]{1,0:T(8,128)(2,1)S(1)}, bf16[384,256]{1,0:T(8,128)(2,1)S(1)}, u32[]{:S(2)}, u32[]{:S(2)}) collective-permute-start(bf16[384,256]{1,0:T(8,128)(2,1)S(1)} %get-tuple-element.119), channel_id=1, source_target_pairs={{16,24},{20,28},{24,16},{28,20},{17,25},{21,29},{25,17},{29,21},{1... | collective-permute-start | bytes 589832 | tf_op jit(solution)/shard_map/ppermute | solution.py:400
  251.2 20.5 %collective-permute-start.36 = (bf16[384,256]{1,0:T(8,128)(2,1)S(1)}, bf16[384,256]{1,0:T(8,128)(2,1)S(1)}, u32[]{:S(2)}, u32[]{:S(2)}) collective-permute-start(bf16[384,256]{1,0:T(8,128)(2,1)S(1)} %get-tuple-element.120), channel_id=1, source_target_pairs={{16,28},{20,24},{24,20},{28,16},{17,29},{21,25},{25,21},{29,17},{1... | collective-permute-start | bytes 589832 | tf_op jit(solution)/shard_map/ppermute | solution.py:400
  256.5 18.9 %collective-permute-start.34 = (bf16[384,256]{1,0:T(8,128)(2,1)S(1)}, bf16[384,256]{1,0:T(8,128)(2,1)S(1)}, u32[]{:S(2)}, u32[]{:S(2)}) collective-permute-start(bf16[384,256]{1,0:T(8,128)(2,1)S(1)} %get-tuple-element.113), channel_id=1, source_target_pairs={{16,20},{20,16},{24,28},{28,24},{17,21},{21,17},{25,29},{29,25},{1... | collective-permute-start | bytes 589832 | tf_op jit(solution)/shard_map/ppermute | solution.py:400
  276.8 18.0 %collective-permute-start.38 = (bf16[384,256]{1,0:T(8,128)(2,1)S(1)}, bf16[384,256]{1,0:T(8,128)(2,1)S(1)}, u32[]{:S(2)}, u32[]{:S(2)}) collective-permute-start(bf16[384,256]{1,0:T(8,128)(2,1)S(1)} %fusion.1.refs_3_), channel_id=1, source_target_pairs={{0,8},{4,12},{8,0},{12,4},{1,9},{5,13},{9,1},{13,5},{2,10},{6,14},... | collective-permute-start | bytes 589832 | tf_op jit(solution)/shard_map/ppermute | solution.py:404
  277.7 17.1 %collective-permute-start.37 = (bf16[384,256]{1,0:T(8,128)(2,1)S(1)}, bf16[384,256]{1,0:T(8,128)(2,1)S(1)}, u32[]{:S(2)}, u32[]{:S(2)}) collective-permute-start(bf16[384,256]{1,0:T(8,128)(2,1)S(1)} %fusion.1.refs_3_), channel_id=1, source_target_pairs={{0,4},{4,0},{8,12},{12,8},{1,5},{5,1},{9,13},{13,9},{2,6},{6,2},{1... | collective-permute-start | bytes 589832 | tf_op jit(solution)/shard_map/ppermute | solution.py:404
  (21 other events, 127.7 us)

commit v5 on v4

--- a/solution.py
+++ b/solution.py
@@ -177,6 +177,67 @@
     )(flags, mat, own, other)
 
 
+def back_pair(flags, mat, parts, own, other):
+    half, tokens = own.shape
+    rows = mat.shape[0] // parts
+    slots = 3
+
+    def body(s, mat_ref, own_ref, other_ref, *refs):
+        out_refs, (buf, sem) = refs[:parts], refs[parts:]
+
+        def fetch(i, core):
+            row = lax.bitwise_xor(s[2], lax.rem(i + 1, parts)) * rows
+            piece = mat_ref.at[pl.ds(pl.multiple_of(row, 16), rows), core * half : (core + 1) * half]
+            slot = lax.rem(i, slots)
+            return pltpu.make_async_copy(piece, buf.at[slot, core], sem.at[slot, core])
+
+        def both(i, act):
+            for core in range(2):
+                act(fetch(i, core))
+
+        @pl.when(s[0] == 1)
+        def _():
+            for i in range(slots):
+                both(i, lambda copy: copy.start())
+
+            @pl.loop(0, parts)
+            def _(i):
+                both(i, lambda copy: copy.wait())
+                slot = lax.rem(i, slots)
+                got = jnp.dot(buf[slot, s[1]], own_ref[...], preferred_element_type=F32)
+                got = got + jnp.dot(
+                    buf[slot, 1 - s[1]], other_ref[...], preferred_element_type=F32
+                )
+
+                @pl.when(i + slots < parts)
+                def _():
+                    both(i + slots, lambda copy: copy.start())
+
+                for which, ref in enumerate(out_refs):
+
+                    @pl.when(i == which)
+                    def _(ref=ref):
+                        ref[...] = got.astype(ref.dtype)
+
+    return pl.pallas_call(
+        body,
+        in_specs=[SMEM, ANY, VMEM, VMEM],
+        out_specs=[VMEM] * parts,
+        out_shape=[jax.ShapeDtypeStruct((rows, tokens), LOW)] * (parts - 1)
+        + [jax.ShapeDtypeStruct((rows, tokens), F32)],
+        scratch_shapes=[
+            pltpu.VMEM((slots, 2, rows, half), LOW),
+            pltpu.SemaphoreType.DMA((slots, 2)),
+        ],
+        compiler_params=params(),
+        cost_estimate=pl.CostEstimate(
+            flops=4 * tokens * rows * parts * half // WEIGHT,
+            bytes_accessed=4 * rows * parts * half // WEIGHT,
+            transcendentals=0,
+        ),
+    )(flags, mat, own, other)
+
+
 def turned(right_ref, grad_ref):
     right_ref[...] = grad_ref[...].T.astype(LOW)
 
@@ -528,12 +589,7 @@
         tokens = sizes[k]
         right = hidden(steps.after(down), hidden_full[k], slopes[k], hidden_other[k])
         swapped = within(0, 1, right)
-        (partial,) = product_in(
-            down, lambda i, s: (i * part_rows, s[1] * half), [right], None, tokens, F32
-        )
-        parts_out[k] = product_parts(
-            down, lambda i, s: (i * part_rows, (1 - s[1]) * half), swapped, tokens, partial
-        )
+        parts_out[k] = back_pair(down, mat_in, PARTS, right, swapped)
         parts_got[k] = send_parts(0, parts_out[k])
         steps.last = parts_out[k][0]
 

time: 299 us -> 296 us (0.990)
    ppermute x5, waiting for transfers between devices: 55.1 us -> 51.8 us  [across(): return lax.ppermute(term, ('section', 'hid'), pairs)]
    pallas_call x12 -> x8, Pallas kernels: 31.9 us -> 29.6 us  [product(): pl.pallas_call(body, in_specs=[SMEM, ANY] + [VMEM if first is None else A...]
where the time goes in v5:
time: 296 us; the launch traced here: 294 us
  waiting for transfers between devices  138 us (47%)
  Pallas kernels  85.5 us (29%)
  starting transfers between devices  65.6 us (22%)
  local copies, waits for them, and re-layouts  4.49 us (2%)
    ppermute x5, waiting for transfers between devices, across(): return lax.ppermute(term, ('section', 'hid'), pairs)  51.8 us
    ppermute x27, starting transfers between devices, within(): return lax.ppermute(block, ('section', axis), pairs)  50.1 us
    ppermute x27, waiting for transfers between devices, within(): return lax.ppermute(block, ('section', axis), pairs)  34.5 us
    ppermute x6, waiting for transfers between devices, everywhere(): return lax.ppermute(block, axis, [(i, i ^ distance) for i in range(size)])  31.3 us
    pallas_call x8, Pallas kernels, product(): pl.pallas_call(body, in_specs=[SMEM, ANY] + [VMEM if first is None else A...  29.6 us
    pallas_call x2, Pallas kernels, pair_product(): pl.pallas_call(body, in_specs=[SMEM, ANY, VMEM, VMEM], out_specs=[VMEM, V...  16.8 us
    ppermute x1, waiting for transfers between devices, detour(): lax.ppermute(piece, ('section', 'wid'), [(i, size + (i ^ 2)) for i in ran...  16.6 us
    pallas_call x1, Pallas kernels, split_rows(): pl.pallas_call(body, in_specs=[SMEM, ANY], out_specs=ANY, out_shape=jax.S...  14.5 us
  transfers between devices with their start and end apart: 40, of which 19 were waited for; matrix products, arithmetic and copies ran while one was open for 0% of the time, Pallas kernels for 14%

profile of v5, /device:TPU:2, one launch (start us, length us, event | category | flops | bytes accessed | tf_op | source)
XLA Modules:
  0.0 294.4 jit_solution(358512888579758452)
XLA Ops:
  0.1 14.5 %shard_map.46.mat_ref = bf16[2,3072,1536]{2,1,0:T(8,128)(2,1)} custom-call(s32[3]{0:T(128)S(1)} %get-tuple-element.114.s, bf16[6144,1536]{1,0:T(8,128)(2,1)} %bitcast.23), custom_call_target="tpu_custom_call" | custom-call | flops 1179648 | bytes 9216 | tf_op jit(solution)/shard_map/pallas_call | solution.py:320
  22.8 16.6 %collective-permute-done.3 = bf16[1024,256]{1,0:T(8,128)(2,1)S(1)} collective-permute-done((bf16[1024,256]{1,0:T(8,128)(2,1)S(1)}, bf16[1024,256]{1,0:T(8,128)(2,1)S(1)}, u32[]{:S(2)}, u32[]{:S(2)}) %collective-permute-start.3) | collective-permute-done | bytes 524320 | tf_op jit(solution)/shard_map/ppermute | solution.py:507
  40.6 5.9 %shard_map.51.slope_ref.refs_1_ = f32[3072,256]{1,0:T(8,128)S(1)} custom-call(s32[3]{0:T(128)S(1)} %get-tuple-element.84.s, f32[512,6144]{1,0:T(8,128)} %bitcast.28), custom_call_target="tpu_custom_call" | custom-call | flops 192 | bytes 1536 | tf_op jit(solution)/shard_map/pallas_call | solution.py:346
  48.2 3.5 %collective-permute-done.4.refs_1_ = bf16[1024,256]{1,0:T(8,128)(2,1)S(1)} collective-permute-done((bf16[1024,256]{1,0:T(8,128)(2,1)S(1)}, bf16[1024,256]{1,0:T(8,128)(2,1)S(1)}, u32[]{:S(2)}, u32[]{:S(2)}) %collective-permute-start.4) | collective-permute-done | bytes 524320 | tf_op jit(solution)/shard_map/ppermute | solution.py:511
  57.8 5.9 %shard_map.54.slope_ref.refs_1_ = f32[3072,256]{1,0:T(8,128)S(1)} custom-call(s32[3]{0:T(128)S(1)} %get-tuple-element.84.s, f32[512,6144]{1,0:T(8,128)} %bitcast.29), custom_call_target="tpu_custom_call" | custom-call | flops 192 | bytes 1536 | tf_op jit(solution)/shard_map/pallas_call | solution.py:346
  66.8 32.6 %collective-permute-done.9.refs_0_ = bf16[384,256]{1,0:T(8,128)(2,1)S(1)} collective-permute-done((bf16[384,256]{1,0:T(8,128)(2,1)S(1)}, bf16[384,256]{1,0:T(8,128)(2,1)S(1)}, u32[]{:S(2)}, u32[]{:S(2)}) %collective-permute-start.9) | collective-permute-done | bytes 196640 | tf_op jit(solution)/shard_map/ppermute | solution.py:516
  102.1 5.4 %collective-permute-start.17 = (bf16[384,256]{1,0:T(8,128)(2,1)S(1)}, bf16[384,256]{1,0:T(8,128)(2,1)S(1)}, u32[]{:S(2)}, u32[]{:S(2)}) collective-permute-start(bf16[384,256]{1,0:T(8,128)(2,1)S(1)} %collective-permute-done.9.refs_0_), channel_id=1, source_target_pairs={{16,28},{20,24},{24,20},{28,16},{17,29},{21,25},{25,21},{29,17},{1... | collective-permute-start | bytes 589832 | tf_op jit(solution)/shard_map/ppermute | solution.py:461
  113.1 10.8 %collective-permute-done.16.refs_2_ = bf16[384,256]{1,0:T(8,128)(2,1)S(1)} collective-permute-done((bf16[384,256]{1,0:T(8,128)(2,1)S(1)}, bf16[384,256]{1,0:T(8,128)(2,1)S(1)}, u32[]{:S(2)}, u32[]{:S(2)}) %collective-permute-start.16) | collective-permute-done | bytes 196640 | tf_op jit(solution)/shard_map/ppermute | solution.py:461
  129.1 8.4 %shard_map.58 = (f32[3072,256]{1,0:T(8,128)S(1)}, bf16[3072,256]{1,0:T(8,128)(2,1)S(1)}) custom-call(s32[3]{0:T(128)S(1)} %get-tuple-element.114.s, bf16[2,3072,1536]{2,1,0:T(8,128)(2,1)} %shard_map.46.mat_ref, bf16[1536,256]{1,0:T(8,128)(2,1)S(1)} %get-tuple-element.93.own_ref, bf16[1536,256]{1,0:T(8,128)(2,1)S(1)} %collective-permute-done.18.other_ref), custom_call_target="tpu_custom_call" | custom-call | flops 1179648 | bytes 4608 | tf_op jit(solution)/shard_map/pallas_call | solution.py:159
  145.6 12.0 %collective-permute-done.19.refs_0_ = bf16[384,256]{1,0:T(8,128)(2,1)S(1)} collective-permute-done((bf16[384,256]{1,0:T(8,128)(2,1)S(1)}, bf16[384,256]{1,0:T(8,128)(2,1)S(1)}, u32[]{:S(2)}, u32[]{:S(2)}) %collective-permute-start.19) | collective-permute-done | bytes 196640 | tf_op jit(solution)/shard_map/ppermute | solution.py:516
  157.6 7.2 %collective-permute-done.21.refs_2_ = bf16[384,256]{1,0:T(8,128)(2,1)S(1)} collective-permute-done((bf16[384,256]{1,0:T(8,128)(2,1)S(1)}, bf16[384,256]{1,0:T(8,128)(2,1)S(1)}, u32[]{:S(2)}, u32[]{:S(2)}) %collective-permute-start.21) | collective-permute-done | bytes 196640 | tf_op jit(solution)/shard_map/ppermute | solution.py:516
  171.1 8.4 %shard_map.60 = (f32[3072,256]{1,0:T(8,128)S(1)}, bf16[3072,256]{1,0:T(8,128)(2,1)S(1)}) custom-call(s32[3]{0:T(128)S(1)} %get-tuple-element.114.s, bf16[2,3072,1536]{2,1,0:T(8,128)(2,1)} %shard_map.46.mat_ref, bf16[1536,256]{1,0:T(8,128)(2,1)S(1)} %get-tuple-element.97.own_ref, bf16[1536,256]{1,0:T(8,128)(2,1)S(1)} %collective-permute-done.23.other_ref), custom_call_target="tpu_custom_call" | custom-call | flops 1179648 | bytes 4608 | tf_op jit(solution)/shard_map/pallas_call | solution.py:159
  179.5 7.3 %shard_map.61 = (f32[1536,256]{1,0:T(8,128)S(1)}, bf16[3072,256]{1,0:T(8,128)(2,1)S(1)}) custom-call(s32[3]{0:T(128)S(1)} %get-tuple-element.114.s, bf16[1536,6144]{1,0:T(8,128)(2,1)} %bitcast.19, f32[3072,256]{1,0:T(8,128)S(1)} %get-tuple-element.94.refs_0_, f32[3072,256]{1,0:T(8,128)} %copy-done.2, bf16[3072,256]{1,0:T(8,128)(2,1)} %collective-permute-done.24.refs_2_), custom_call_target="tpu_custom_call" | custom-call | flops 589824 | bytes 2304 | tf_op jit(solution)/shard_map/pallas_call | solution.py:104
  192.1 5.5 %shard_map.62 = (bf16[384,256]{1,0:T(8,128)(2,1)S(1)}, bf16[384,256]{1,0:T(8,128)(2,1)S(1)}, bf16[384,256]{1,0:T(8,128)(2,1)S(1)}, f32[384,256]{1,0:T(8,128)S(1)}) custom-call(s32[3]{0:T(128)S(1)} %get-tuple-element.114.s, bf16[1536,6144]{1,0:T(8,128)(2,1)} %bitcast.20, bf16[3072,256]{1,0:T(8,128)(2,1)S(1)} %get-tuple-element.101.refs_0_, ...), custom_call_target="tpu_custom_call" | custom-call | flops 589824 | bytes 2304 | tf_op jit(solution)/shard_map/pallas_call | solution.py:104
  199.5 4.1 %collective-permute-start.28 = (bf16[384,256]{1,0:T(8,128)(2,1)S(1)}, bf16[384,256]{1,0:T(8,128)(2,1)S(1)}, u32[]{:S(2)}, u32[]{:S(2)}) collective-permute-start(bf16[384,256]{1,0:T(8,128)(2,1)S(1)} %get-tuple-element.107), channel_id=1, source_target_pairs={{16,28},{20,24},{24,20},{28,16},{17,29},{21,25},{25,21},{29,17},{1... | collective-permute-start | bytes 589832 | tf_op jit(solution)/shard_map/ppermute | solution.py:461
  206.8 8.3 %collective-permute-done.27 = bf16[384,256]{1,0:T(8,128)(2,1)S(1)} collective-permute-done((bf16[384,256]{1,0:T(8,128)(2,1)S(1)}, bf16[384,256]{1,0:T(8,128)(2,1)S(1)}, u32[]{:S(2)}, u32[]{:S(2)}) %collective-permute-start.27) | collective-permute-done | bytes 196640 | tf_op jit(solution)/shard_map/ppermute | solution.py:461
  215.1 4.1 %collective-permute-done.26 = bf16[384,256]{1,0:T(8,128)(2,1)S(1)} collective-permute-done((bf16[384,256]{1,0:T(8,128)(2,1)S(1)}, bf16[384,256]{1,0:T(8,128)(2,1)S(1)}, u32[]{:S(2)}, u32[]{:S(2)}) %collective-permute-start.26) | collective-permute-done | bytes 196640 | tf_op jit(solution)/shard_map/ppermute | solution.py:461
  220.0 6.2 %collective-permute-done.29.refs_3_ = bf16[384,256]{1,0:T(8,128)(2,1)S(1)} collective-permute-done((bf16[384,256]{1,0:T(8,128)(2,1)S(1)}, bf16[384,256]{1,0:T(8,128)(2,1)S(1)}, u32[]{:S(2)}, u32[]{:S(2)}) %collective-permute-start.29) | collective-permute-done | bytes 196640 | tf_op jit(solution)/shard_map/ppermute | solution.py:465
  227.4 6.8 %shard_map.63 = (f32[1536,256]{1,0:T(8,128)S(1)}, bf16[3072,256]{1,0:T(8,128)(2,1)S(1)}) custom-call(s32[3]{0:T(128)S(1)} %get-tuple-element.114.s, bf16[1536,6144]{1,0:T(8,128)(2,1)} %bitcast.21, f32[3072,256]{1,0:T(8,128)S(1)} %get-tuple-element.98.refs_0_, f32[3072,256]{1,0:T(8,128)} %copy-done.1, bf16[3072,256]{1,0:T(8,128)(2,1)S(1)} %collective-permute-done.30.refs_2_), custom_call_target="tpu_custom_call" | custom-call | flops 589824 | bytes 2304 | tf_op jit(solution)/shard_map/pallas_call | solution.py:104
  239.5 5.5 %shard_map.64 = (bf16[384,256]{1,0:T(8,128)(2,1)S(1)}, bf16[384,256]{1,0:T(8,128)(2,1)S(1)}, bf16[384,256]{1,0:T(8,128)(2,1)S(1)}, f32[384,256]{1,0:T(8,128)S(1)}) custom-call(s32[3]{0:T(128)S(1)} %get-tuple-element.114.s, bf16[1536,6144]{1,0:T(8,128)(2,1)} %bitcast.22, bf16[3072,256]{1,0:T(8,128)(2,1)S(1)} %get-tuple-element.111.refs_0_, ...), custom_call_target="tpu_custom_call" | custom-call | flops 589824 | bytes 2304 | tf_op jit(solution)/shard_map/pallas_call | solution.py:104
  247.1 5.2 %collective-permute-start.36 = (bf16[384,256]{1,0:T(8,128)(2,1)S(1)}, bf16[384,256]{1,0:T(8,128)(2,1)S(1)}, u32[]{:S(2)}, u32[]{:S(2)}) collective-permute-start(bf16[384,256]{1,0:T(8,128)(2,1)S(1)} %get-tuple-element.120), channel_id=1, source_target_pairs={{16,28},{20,24},{24,20},{28,16},{17,29},{21,25},{25,21},{29,17},{1... | collective-permute-start | bytes 589832 | tf_op jit(solution)/shard_map/ppermute | solution.py:461
  254.3 10.0 %collective-permute-done.32.refs_4_ = bf16[384,256]{1,0:T(8,128)(2,1)S(1)} collective-permute-done((bf16[384,256]{1,0:T(8,128)(2,1)S(1)}, bf16[384,256]{1,0:T(8,128)(2,1)S(1)}, u32[]{:S(2)}, u32[]{:S(2)}) %collective-permute-start.32) | collective-permute-done | bytes 196640 | tf_op jit(solution)/shard_map/ppermute | solution.py:465
  276.5 5.3 %collective-permute-done.39.refs_6_ = bf16[384,256]{1,0:T(8,128)(2,1)S(1)} collective-permute-done((bf16[384,256]{1,0:T(8,128)(2,1)S(1)}, bf16[384,256]{1,0:T(8,128)(2,1)S(1)}, u32[]{:S(2)}, u32[]{:S(2)}) %collective-permute-start.39) | collective-permute-done | bytes 196640 | tf_op jit(solution)/shard_map/ppermute | solution.py:465
  281.9 9.8 %collective-permute-done.38.refs_5_ = bf16[384,256]{1,0:T(8,128)(2,1)S(1)} collective-permute-done((bf16[384,256]{1,0:T(8,128)(2,1)S(1)}, bf16[384,256]{1,0:T(8,128)(2,1)S(1)}, u32[]{:S(2)}, u32[]{:S(2)}) %collective-permute-start.38) | collective-permute-done | bytes 196640 | tf_op jit(solution)/shard_map/ppermute | solution.py:465
  (93 shorter events, 84.7 us)
Async XLA Ops:
  19.0 20.4 %collective-permute-start.3 = (bf16[1024,256]{1,0:T(8,128)(2,1)S(1)}, bf16[1024,256]{1,0:T(8,128)(2,1)S(1)}, u32[]{:S(2)}, u32[]{:S(2)}) collective-permute-start(bf16[1024,256]{1,0:T(8,128)(2,1)S(1)} %get-tuple-element.76), channel_id=1, source_target_pairs={{0,18},{1,19},{2,16},{3,17},{4,22},{5,23},{6,20},{7,21},{8,26},{9,... | collective-permute-start | bytes 1572872 | tf_op jit(solution)/shard_map/ppermute | solution.py:507
  20.3 27.9 %collective-permute-start.2 = (bf16[2048,256]{1,0:T(8,128)(2,1)}, bf16[2048,256]{1,0:T(8,128)(2,1)S(1)}, u32[]{:S(2)}, u32[]{:S(2)}) collective-permute-start(bf16[2048,256]{1,0:T(8,128)(2,1)} %get-tuple-element.75), channel_id=1, source_target_pairs={{0,2},{1,3},{2,0},{3,1},{4,6},{5,7},{6,4},{7,5},{8,10},{9,11},{10,... | collective-permute-start | bytes 3145736 | tf_op jit(solution)/shard_map/ppermute | solution.py:461
  39.3 12.4 %collective-permute-start.4 = (bf16[1024,256]{1,0:T(8,128)(2,1)S(1)}, bf16[1024,256]{1,0:T(8,128)(2,1)S(1)}, u32[]{:S(2)}, u32[]{:S(2)}) collective-permute-start(bf16[1024,256]{1,0:T(8,128)(2,1)S(1)} %collective-permute-done.3), channel_id=1, source_target_pairs={{16,0},{17,1},{18,2},{19,3},{20,4},{21,5},{22,6},{23,7},{24,8},{25... | collective-permute-start | bytes 1572872 | tf_op jit(solution)/shard_map/ppermute | solution.py:511
  54.4 45.1 %collective-permute-start.10 = (bf16[3072,256]{1,0:T(8,128)(2,1)}, bf16[3072,256]{1,0:T(8,128)(2,1)S(1)}, u32[]{:S(2)}, u32[]{:S(2)}) collective-permute-start(bf16[3072,256]{1,0:T(8,128)(2,1)} %get-tuple-element.86), channel_id=1, source_target_pairs={{0,2},{1,3},{2,0},{3,1},{4,6},{5,7},{6,4},{7,5},{8,10},{9,11},{10,... | collective-permute-start | bytes 4718600 | tf_op jit(solution)/shard_map/ppermute | solution.py:461
  65.5 33.9 %collective-permute-start.9 = (bf16[384,256]{1,0:T(8,128)(2,1)S(1)}, bf16[384,256]{1,0:T(8,128)(2,1)S(1)}, u32[]{:S(2)}, u32[]{:S(2)}) collective-permute-start(bf16[384,256]{1,0:T(8,128)(2,1)S(1)} %add_convert_fusion.3), channel_id=1, source_target_pairs={{0,16},{4,20},{8,24},{12,28},{1,17},{5,21},{9,25},{13,29},{2,18},{... | collective-permute-start | bytes 589832 | tf_op jit(solution)/shard_map/ppermute | solution.py:516
  101.4 11.1 %collective-permute-start.11 = (bf16[3072,256]{1,0:T(8,128)(2,1)S(1)}, bf16[3072,256]{1,0:T(8,128)(2,1)S(1)}, u32[]{:S(2)}, u32[]{:S(2)}) collective-permute-start(bf16[3072,256]{1,0:T(8,128)(2,1)S(1)} %shard_map.55.own_ref), channel_id=1, source_target_pairs={{0,1},{1,0},{2,3},{3,2},{4,5},{5,4},{6,7},{7,6},{8,9},{9,8},{10,11... | collective-permute-start | bytes 4718600 | tf_op jit(solution)/shard_map/ppermute | solution.py:461
  107.5 16.4 %collective-permute-start.16 = (bf16[384,256]{1,0:T(8,128)(2,1)S(1)}, bf16[384,256]{1,0:T(8,128)(2,1)S(1)}, u32[]{:S(2)}, u32[]{:S(2)}) collective-permute-start(bf16[384,256]{1,0:T(8,128)(2,1)S(1)} %collective-permute-done.9.refs_0_), channel_id=1, source_target_pairs={{16,24},{20,28},{24,16},{28,20},{17,25},{21,29},{25,17},{29,21},{1... | collective-permute-start | bytes 589832 | tf_op jit(solution)/shard_map/ppermute | solution.py:461
  109.5 14.4 %collective-permute-start.15 = (bf16[384,256]{1,0:T(8,128)(2,1)S(1)}, bf16[384,256]{1,0:T(8,128)(2,1)S(1)}, u32[]{:S(2)}, u32[]{:S(2)}) collective-permute-start(bf16[384,256]{1,0:T(8,128)(2,1)S(1)} %collective-permute-done.9.refs_0_), channel_id=1, source_target_pairs={{16,20},{20,16},{24,28},{28,24},{17,21},{21,17},{25,29},{29,25},{1... | collective-permute-start | bytes 589832 | tf_op jit(solution)/shard_map/ppermute | solution.py:461
  137.5 41.9 %collective-permute-start.24 = (bf16[3072,256]{1,0:T(8,128)(2,1)S(1)}, bf16[3072,256]{1,0:T(8,128)(2,1)}, u32[]{:S(2)}, u32[]{:S(2)}) collective-permute-start(bf16[3072,256]{1,0:T(8,128)(2,1)S(1)} %get-tuple-element.100), channel_id=1, source_target_pairs={{16,18},{17,19},{18,16},{19,17},{20,22},{21,23},{22,20},{23,21},{2... | collective-permute-start | bytes 4718600 | tf_op jit(solution)/shard_map/ppermute | solution.py:461
  140.4 17.2 %collective-permute-start.19 = (bf16[384,256]{1,0:T(8,128)(2,1)S(1)}, bf16[384,256]{1,0:T(8,128)(2,1)S(1)}, u32[]{:S(2)}, u32[]{:S(2)}) collective-permute-start(bf16[384,256]{1,0:T(8,128)(2,1)S(1)} %add_convert_fusion.2), channel_id=1, source_target_pairs={{0,16},{4,20},{8,24},{12,28},{1,17},{5,21},{9,25},{13,29},{2,18},{... | collective-permute-start | bytes 589832 | tf_op jit(solution)/shard_map/ppermute | solution.py:516
  141.7 15.9 %collective-permute-start.22 = (bf16[384,256]{1,0:T(8,128)(2,1)S(1)}, bf16[384,256]{1,0:T(8,128)(2,1)S(1)}, u32[]{:S(2)}, u32[]{:S(2)}) collective-permute-start(bf16[384,256]{1,0:T(8,128)(2,1)S(1)} %add_convert_fusion.2), channel_id=1, source_target_pairs={{0,28},{4,24},{8,20},{12,16},{1,29},{5,25},{9,21},{13,17},{2,30},{... | collective-permute-start | bytes 589832 | tf_op jit(solution)/shard_map/ppermute | solution.py:516
  143.0 21.8 %collective-permute-start.21 = (bf16[384,256]{1,0:T(8,128)(2,1)S(1)}, bf16[384,256]{1,0:T(8,128)(2,1)S(1)}, u32[]{:S(2)}, u32[]{:S(2)}) collective-permute-start(bf16[384,256]{1,0:T(8,128)(2,1)S(1)} %add_convert_fusion.2), channel_id=1, source_target_pairs={{0,24},{4,28},{8,16},{12,20},{1,25},{5,29},{9,17},{13,21},{2,26},{... | collective-permute-start | bytes 589832 | tf_op jit(solution)/shard_map/ppermute | solution.py:516
  144.3 20.5 %collective-permute-start.20 = (bf16[384,256]{1,0:T(8,128)(2,1)S(1)}, bf16[384,256]{1,0:T(8,128)(2,1)S(1)}, u32[]{:S(2)}, u32[]{:S(2)}) collective-permute-start(bf16[384,256]{1,0:T(8,128)(2,1)S(1)} %add_convert_fusion.2), channel_id=1, source_target_pairs={{0,20},{4,16},{8,28},{12,24},{1,21},{5,17},{9,29},{13,25},{2,22},{... | collective-permute-start | bytes 589832 | tf_op jit(solution)/shard_map/ppermute | solution.py:516
  188.8 38.6 %collective-permute-start.30 = (bf16[3072,256]{1,0:T(8,128)(2,1)S(1)}, bf16[3072,256]{1,0:T(8,128)(2,1)S(1)}, u32[]{:S(2)}, u32[]{:S(2)}) collective-permute-start(bf16[3072,256]{1,0:T(8,128)(2,1)S(1)} %get-tuple-element.110), channel_id=1, source_target_pairs={{16,18},{17,19},{18,16},{19,17},{20,22},{21,23},{22,20},{23,21},{2... | collective-permute-start | bytes 4718600 | tf_op jit(solution)/shard_map/ppermute | solution.py:461
  197.6 17.5 %collective-permute-start.27 = (bf16[384,256]{1,0:T(8,128)(2,1)S(1)}, bf16[384,256]{1,0:T(8,128)(2,1)S(1)}, u32[]{:S(2)}, u32[]{:S(2)}) collective-permute-start(bf16[384,256]{1,0:T(8,128)(2,1)S(1)} %get-tuple-element.106), channel_id=1, source_target_pairs={{16,24},{20,28},{24,16},{28,20},{17,25},{21,29},{25,17},{29,21},{1... | collective-permute-start | bytes 589832 | tf_op jit(solution)/shard_map/ppermute | solution.py:461
  199.5 15.6 %collective-permute-start.28 = (bf16[384,256]{1,0:T(8,128)(2,1)S(1)}, bf16[384,256]{1,0:T(8,128)(2,1)S(1)}, u32[]{:S(2)}, u32[]{:S(2)}) collective-permute-start(bf16[384,256]{1,0:T(8,128)(2,1)S(1)} %get-tuple-element.107), channel_id=1, source_target_pairs={{16,28},{20,24},{24,20},{28,16},{17,29},{21,25},{25,21},{29,17},{1... | collective-permute-start | bytes 589832 | tf_op jit(solution)/shard_map/ppermute | solution.py:461
  203.6 15.6 %collective-permute-start.26 = (bf16[384,256]{1,0:T(8,128)(2,1)S(1)}, bf16[384,256]{1,0:T(8,128)(2,1)S(1)}, u32[]{:S(2)}, u32[]{:S(2)}) collective-permute-start(bf16[384,256]{1,0:T(8,128)(2,1)S(1)} %get-tuple-element.104), channel_id=1, source_target_pairs={{16,20},{20,16},{24,28},{28,24},{17,21},{21,17},{25,29},{29,25},{1... | collective-permute-start | bytes 589832 | tf_op jit(solution)/shard_map/ppermute | solution.py:461
  236.2 18.1 %collective-permute-start.33 = (bf16[384,256]{1,0:T(8,128)(2,1)S(1)}, bf16[384,256]{1,0:T(8,128)(2,1)S(1)}, u32[]{:S(2)}, u32[]{:S(2)}) collective-permute-start(bf16[384,256]{1,0:T(8,128)(2,1)S(1)} %fusion.refs_2_), channel_id=1, source_target_pairs={{0,12},{4,8},{8,4},{12,0},{1,13},{5,9},{9,5},{13,1},{2,14},{6,10},... | collective-permute-start | bytes 589832 | tf_op jit(solution)/shard_map/ppermute | solution.py:465
  236.8 27.5 %collective-permute-start.32 = (bf16[384,256]{1,0:T(8,128)(2,1)S(1)}, bf16[384,256]{1,0:T(8,128)(2,1)S(1)}, u32[]{:S(2)}, u32[]{:S(2)}) collective-permute-start(bf16[384,256]{1,0:T(8,128)(2,1)S(1)} %fusion.refs_2_), channel_id=1, source_target_pairs={{0,8},{4,12},{8,0},{12,4},{1,9},{5,13},{9,1},{13,5},{2,10},{6,14},... | collective-permute-start | bytes 589832 | tf_op jit(solution)/shard_map/ppermute | solution.py:465
  245.0 23.4 %collective-permute-start.35 = (bf16[384,256]{1,0:T(8,128)(2,1)S(1)}, bf16[384,256]{1,0:T(8,128)(2,1)S(1)}, u32[]{:S(2)}, u32[]{:S(2)}) collective-permute-start(bf16[384,256]{1,0:T(8,128)(2,1)S(1)} %get-tuple-element.119), channel_id=1, source_target_pairs={{16,24},{20,28},{24,16},{28,20},{17,25},{21,29},{25,17},{29,21},{1... | collective-permute-start | bytes 589832 | tf_op jit(solution)/shard_map/ppermute | solution.py:461
  247.1 21.3 %collective-permute-start.36 = (bf16[384,256]{1,0:T(8,128)(2,1)S(1)}, bf16[384,256]{1,0:T(8,128)(2,1)S(1)}, u32[]{:S(2)}, u32[]{:S(2)}) collective-permute-start(bf16[384,256]{1,0:T(8,128)(2,1)S(1)} %get-tuple-element.120), channel_id=1, source_target_pairs={{16,28},{20,24},{24,20},{28,16},{17,29},{21,25},{25,21},{29,17},{1... | collective-permute-start | bytes 589832 | tf_op jit(solution)/shard_map/ppermute | solution.py:461
  252.3 19.6 %collective-permute-start.34 = (bf16[384,256]{1,0:T(8,128)(2,1)S(1)}, bf16[384,256]{1,0:T(8,128)(2,1)S(1)}, u32[]{:S(2)}, u32[]{:S(2)}) collective-permute-start(bf16[384,256]{1,0:T(8,128)(2,1)S(1)} %get-tuple-element.113), channel_id=1, source_target_pairs={{16,20},{20,16},{24,28},{28,24},{17,21},{21,17},{25,29},{29,25},{1... | collective-permute-start | bytes 589832 | tf_op jit(solution)/shard_map/ppermute | solution.py:461
  273.4 18.2 %collective-permute-start.38 = (bf16[384,256]{1,0:T(8,128)(2,1)S(1)}, bf16[384,256]{1,0:T(8,128)(2,1)S(1)}, u32[]{:S(2)}, u32[]{:S(2)}) collective-permute-start(bf16[384,256]{1,0:T(8,128)(2,1)S(1)} %fusion.1.refs_3_), channel_id=1, source_target_pairs={{0,8},{4,12},{8,0},{12,4},{1,9},{5,13},{9,1},{13,5},{2,10},{6,14},... | collective-permute-start | bytes 589832 | tf_op jit(solution)/shard_map/ppermute | solution.py:465
  274.5 17.1 %collective-permute-start.37 = (bf16[384,256]{1,0:T(8,128)(2,1)S(1)}, bf16[384,256]{1,0:T(8,128)(2,1)S(1)}, u32[]{:S(2)}, u32[]{:S(2)}) collective-permute-start(bf16[384,256]{1,0:T(8,128)(2,1)S(1)} %fusion.1.refs_3_), channel_id=1, source_target_pairs={{0,4},{4,0},{8,12},{12,8},{1,5},{5,1},{9,13},{13,9},{2,6},{6,2},{1... | collective-permute-start | bytes 589832 | tf_op jit(solution)/shard_map/ppermute | solution.py:465
  (21 other events, 129.1 us)

commit v6 on v5

--- a/solution.py
+++ b/solution.py
@@ -502,13 +502,15 @@
             pieces = [lax.optimization_barrier((piece, earlier))[0] for piece in pieces]
         return [within(active, 2, piece) for piece in pieces]
 
-    def detour(piece):
+    def detour(active, piece):
         size = lax.axis_size("wid")
-        return lax.ppermute(piece, ("section", "wid"), [(i, size + (i ^ 2)) for i in range(size)])
-
-    def returned(piece):
+        pairs = [(active * size + i, (1 - active) * size + (i ^ 2)) for i in range(size)]
+        return lax.ppermute(piece, ("section", "wid"), pairs)
+
+    def returned(active, piece):
         size = lax.axis_size("wid")
-        return lax.ppermute(piece, ("section", "wid"), [(size + i, i) for i in range(size)])
+        pairs = [((1 - active) * size + i, active * size + i) for i in range(size)]
+        return lax.ppermute(piece, ("section", "wid"), pairs)
 
     def across(term, distance):
         size = lax.axis_size("hid")
@@ -576,10 +578,10 @@
         if k > 0:
             hidden_other[k] = exchange(0, pieces, hidden_other[0][0])
         else:
-            hidden_other[0] = [within(0, 2, pieces[0]), detour(pieces[1])]
+            hidden_other[0] = [within(0, 2, pieces[0]), detour(0, pieces[1])]
 
     def down_return():
-        hidden_other[0][1] = returned(steps.after(hidden_other[0][1]))
+        hidden_other[0][1] = returned(0, steps.after(hidden_other[0][1]))
 
     def slope(k):
         slopes[k] = slope_of(steps.after(down), pre, starts[k], sizes[k], half)
@@ -613,7 +615,14 @@
         full, low_grad = pair_product(flags, split_out, hid_rows, low, low_other)
         steps.last = full
         up_full[k] = full
-        up_other[k] = exchange(1, [low_grad], up_other[k - 1][0] if k else None)
+        up_other[k] = exchange(
+            1, [low_grad if k < last_chunk else low_grad[hid_rows:]], up_other[k - 1][0] if k else None
+        )
+        if k == last_chunk:
+            up_other[k].insert(0, detour(1, low_grad[:hid_rows]))
+
+    def up_return():
+        up_other[last_chunk][0] = returned(1, steps.after(up_other[last_chunk][0]))
 
     def place(part, core):
         row = core * (PARTS // 2) + lax.rem(part, PARTS // 2)
@@ -631,10 +640,11 @@
 
     def gather(k):
         own = steps.after(up_parts[k][-1])
+        if k < last_chunk:
+            own = lax.optimization_barrier((own, up_other[last_chunk][0]))[0]
         last = jnp.where(is_up, sum_hid(1, own, send_parts(1, up_parts[k])), terms[k])
         steps.last = last
         lasts[k] = [last] + [everywhere(d, last) for d in range(1, PARTS)]
-        steps.last = lasts[k][1]
 
     for k in chunks:
         down_send(k)
@@ -650,6 +660,7 @@
     cross(1)
     up_hidden(1)
     up_back(0)
+    up_return()
     gather(0)
     up_back(1)
     out = finish(steps.after(up), None, grad, starts[0], up_terms[0], lasts[0])

time: 296 us -> 290 us (0.980)
  waiting for transfers between devices: 138 us -> 126 us
  starting transfers between devices: 65.6 us -> 70.6 us
    ppermute x6, waiting for transfers between devices: 31.3 us -> 24.8 us  [everywhere(): return lax.ppermute(block, axis, [(i, i ^ distance) for i in range(size)])]
    ppermute x27, waiting for transfers between devices: 34.5 us -> 28.7 us  [within(): return lax.ppermute(block, ('section', axis), pairs)]
    ppermute x2 -> x4, waiting for transfers between devices: 20.1 us -> 20.8 us  [the longest x2 17.1 us: detour(): return lax.ppermute(piece, ('section', 'wid'), pairs)]
  transfers between devices with their start and end apart: 40 -> 42, of which waited for: 19 -> 18; matrix products, arithmetic and copies ran while one was open for 0% -> 0% of each run, Pallas kernels for 14% -> 14%
where the time goes in v6:
time: 290 us; the launch traced here: 289 us
  waiting for transfers between devices  126 us (43%)
  Pallas kernels  86.7 us (30%)
  starting transfers between devices  70.6 us (24%)
  local copies, waits for them, and re-layouts  4.59 us (2%)
    ppermute x5, waiting for transfers between devices, across(): return lax.ppermute(term, ('section', 'hid'), pairs)  51.8 us
    ppermute x27, starting transfers between devices, within(): return lax.ppermute(block, ('section', axis), pairs)  50.1 us
    pallas_call x8, Pallas kernels, product(): pl.pallas_call(body, in_specs=[SMEM, ANY] + [VMEM if first is None else A...  30.8 us
    ppermute x27, waiting for transfers between devices, within(): return lax.ppermute(block, ('section', axis), pairs)  28.7 us
    ppermute x6, waiting for transfers between devices, everywhere(): return lax.ppermute(block, axis, [(i, i ^ distance) for i in range(size)])  24.8 us
    ppermute x2, waiting for transfers between devices, detour(): return lax.ppermute(piece, ('section', 'wid'), pairs)  17.1 us
    pallas_call x2, Pallas kernels, pair_product(): pl.pallas_call(body, in_specs=[SMEM, ANY, VMEM, VMEM], out_specs=[VMEM, V...  16.8 us
    pallas_call x1, Pallas kernels, split_rows(): pl.pallas_call(body, in_specs=[SMEM, ANY], out_specs=ANY, out_shape=jax.S...  14.5 us
  transfers between devices with their start and end apart: 42, of which 18 were waited for; matrix products, arithmetic and copies ran while one was open for 0% of the time, Pallas kernels for 14%

profile of v6, /device:TPU:2, one launch (start us, length us, event | category | flops | bytes accessed | tf_op | source)
XLA Modules:
  0.0 289.2 jit_solution(16271493245021503991)
XLA Ops:
  0.1 14.5 %shard_map.46.mat_ref = bf16[2,3072,1536]{2,1,0:T(8,128)(2,1)} custom-call(s32[3]{0:T(128)S(1)} %get-tuple-element.118.s, bf16[6144,1536]{1,0:T(8,128)(2,1)} %bitcast.23), custom_call_target="tpu_custom_call" | custom-call | flops 1179648 | bytes 9216 | tf_op jit(solution)/shard_map/pallas_call | solution.py:320
  22.8 16.6 %collective-permute-done.3 = bf16[1024,256]{1,0:T(8,128)(2,1)S(1)} collective-permute-done((bf16[1024,256]{1,0:T(8,128)(2,1)S(1)}, bf16[1024,256]{1,0:T(8,128)(2,1)S(1)}, u32[]{:S(2)}, u32[]{:S(2)}) %collective-permute-start.3) | collective-permute-done | bytes 524320 | tf_op jit(solution)/shard_map/ppermute | solution.py:508
  40.6 5.9 %shard_map.51.slope_ref.refs_1_ = f32[3072,256]{1,0:T(8,128)S(1)} custom-call(s32[3]{0:T(128)S(1)} %get-tuple-element.86.s, f32[512,6144]{1,0:T(8,128)} %bitcast.28), custom_call_target="tpu_custom_call" | custom-call | flops 192 | bytes 1536 | tf_op jit(solution)/shard_map/pallas_call | solution.py:346
  48.2 3.5 %collective-permute-done.4.refs_1_ = bf16[1024,256]{1,0:T(8,128)(2,1)S(1)} collective-permute-done((bf16[1024,256]{1,0:T(8,128)(2,1)S(1)}, bf16[1024,256]{1,0:T(8,128)(2,1)S(1)}, u32[]{:S(2)}, u32[]{:S(2)}) %collective-permute-start.4) | collective-permute-done | bytes 524320 | tf_op jit(solution)/shard_map/ppermute | solution.py:513
  57.8 5.9 %shard_map.54.slope_ref.refs_1_ = f32[3072,256]{1,0:T(8,128)S(1)} custom-call(s32[3]{0:T(128)S(1)} %get-tuple-element.86.s, f32[512,6144]{1,0:T(8,128)} %bitcast.29), custom_call_target="tpu_custom_call" | custom-call | flops 192 | bytes 1536 | tf_op jit(solution)/shard_map/pallas_call | solution.py:346
  66.8 32.6 %collective-permute-done.9.refs_0_ = bf16[384,256]{1,0:T(8,128)(2,1)S(1)} collective-permute-done((bf16[384,256]{1,0:T(8,128)(2,1)S(1)}, bf16[384,256]{1,0:T(8,128)(2,1)S(1)}, u32[]{:S(2)}, u32[]{:S(2)}) %collective-permute-start.9) | collective-permute-done | bytes 196640 | tf_op jit(solution)/shard_map/ppermute | solution.py:518
  102.1 5.4 %collective-permute-start.17 = (bf16[384,256]{1,0:T(8,128)(2,1)S(1)}, bf16[384,256]{1,0:T(8,128)(2,1)S(1)}, u32[]{:S(2)}, u32[]{:S(2)}) collective-permute-start(bf16[384,256]{1,0:T(8,128)(2,1)S(1)} %collective-permute-done.9.refs_0_), channel_id=1, source_target_pairs={{16,28},{20,24},{24,20},{28,16},{17,29},{21,25},{25,21},{29,17},{1... | collective-permute-start | bytes 589832 | tf_op jit(solution)/shard_map/ppermute | solution.py:461
  113.1 10.8 %collective-permute-done.16.refs_2_ = bf16[384,256]{1,0:T(8,128)(2,1)S(1)} collective-permute-done((bf16[384,256]{1,0:T(8,128)(2,1)S(1)}, bf16[384,256]{1,0:T(8,128)(2,1)S(1)}, u32[]{:S(2)}, u32[]{:S(2)}) %collective-permute-start.16) | collective-permute-done | bytes 196640 | tf_op jit(solution)/shard_map/ppermute | solution.py:461
  129.1 8.4 %shard_map.58 = (f32[3072,256]{1,0:T(8,128)S(1)}, bf16[3072,256]{1,0:T(8,128)(2,1)S(1)}) custom-call(s32[3]{0:T(128)S(1)} %get-tuple-element.118.s, bf16[2,3072,1536]{2,1,0:T(8,128)(2,1)} %shard_map.46.mat_ref, bf16[1536,256]{1,0:T(8,128)(2,1)S(1)} %get-tuple-element.95.own_ref, bf16[1536,256]{1,0:T(8,128)(2,1)S(1)} %collective-permute-done.18.other_ref), custom_call_target="tpu_custom_call" | custom-call | flops 1179648 | bytes 4608 | tf_op jit(solution)/shard_map/pallas_call | solution.py:159
  145.6 12.0 %collective-permute-done.19.refs_0_ = bf16[384,256]{1,0:T(8,128)(2,1)S(1)} collective-permute-done((bf16[384,256]{1,0:T(8,128)(2,1)S(1)}, bf16[384,256]{1,0:T(8,128)(2,1)S(1)}, u32[]{:S(2)}, u32[]{:S(2)}) %collective-permute-start.19) | collective-permute-done | bytes 196640 | tf_op jit(solution)/shard_map/ppermute | solution.py:518
  157.6 7.2 %collective-permute-done.21.refs_2_ = bf16[384,256]{1,0:T(8,128)(2,1)S(1)} collective-permute-done((bf16[384,256]{1,0:T(8,128)(2,1)S(1)}, bf16[384,256]{1,0:T(8,128)(2,1)S(1)}, u32[]{:S(2)}, u32[]{:S(2)}) %collective-permute-start.21) | collective-permute-done | bytes 196640 | tf_op jit(solution)/shard_map/ppermute | solution.py:518
  171.1 8.4 %shard_map.60 = (f32[3072,256]{1,0:T(8,128)S(1)}, bf16[3072,256]{1,0:T(8,128)(2,1)S(1)}) custom-call(s32[3]{0:T(128)S(1)} %get-tuple-element.118.s, bf16[2,3072,1536]{2,1,0:T(8,128)(2,1)} %shard_map.46.mat_ref, bf16[1536,256]{1,0:T(8,128)(2,1)S(1)} %get-tuple-element.99.own_ref, bf16[1536,256]{1,0:T(8,128)(2,1)S(1)} %collective-permute-done.23.other_ref), custom_call_target="tpu_custom_call" | custom-call | flops 1179648 | bytes 4608 | tf_op jit(solution)/shard_map/pallas_call | solution.py:159
  179.5 8.5 %shard_map.61 = (f32[1536,256]{1,0:T(8,128)}, bf16[3072,256]{1,0:T(8,128)(2,1)S(1)}) custom-call(s32[3]{0:T(128)S(1)} %get-tuple-element.118.s, bf16[1536,6144]{1,0:T(8,128)(2,1)} %bitcast.19, f32[3072,256]{1,0:T(8,128)S(1)} %get-tuple-element.96.refs_0_, f32[3072,256]{1,0:T(8,128)} %copy-done.2, bf16[3072,256]{1,0:T(8,128)(2,1)} %collective-permute-done.24.refs_2_), custom_call_target="tpu_custom_call" | custom-call | flops 589824 | bytes 2304 | tf_op jit(solution)/shard_map/pallas_call | solution.py:104
  193.9 5.5 %shard_map.62 = (bf16[384,256]{1,0:T(8,128)(2,1)S(1)}, bf16[384,256]{1,0:T(8,128)(2,1)S(1)}, bf16[384,256]{1,0:T(8,128)(2,1)S(1)}, f32[384,256]{1,0:T(8,128)S(1)}) custom-call(s32[3]{0:T(128)S(1)} %get-tuple-element.118.s, bf16[1536,6144]{1,0:T(8,128)(2,1)} %bitcast.20, bf16[3072,256]{1,0:T(8,128)(2,1)S(1)} %get-tuple-element.103.refs_0_, ...), custom_call_target="tpu_custom_call" | custom-call | flops 589824 | bytes 2304 | tf_op jit(solution)/shard_map/pallas_call | solution.py:104
  203.1 4.4 %collective-permute-start.30 = (bf16[384,256]{1,0:T(8,128)(2,1)S(1)}, bf16[384,256]{1,0:T(8,128)(2,1)S(1)}, u32[]{:S(2)}, u32[]{:S(2)}) collective-permute-start(bf16[384,256]{1,0:T(8,128)(2,1)S(1)} %get-tuple-element.112), channel_id=1, source_target_pairs={{16,28},{20,24},{24,20},{28,16},{17,29},{21,25},{25,21},{29,17},{1... | collective-permute-start | bytes 589832 | tf_op jit(solution)/shard_map/ppermute | solution.py:461
  210.7 7.9 %collective-permute-done.29 = bf16[384,256]{1,0:T(8,128)(2,1)S(1)} collective-permute-done((bf16[384,256]{1,0:T(8,128)(2,1)S(1)}, bf16[384,256]{1,0:T(8,128)(2,1)S(1)}, u32[]{:S(2)}, u32[]{:S(2)}) %collective-permute-start.29) | collective-permute-done | bytes 196640 | tf_op jit(solution)/shard_map/ppermute | solution.py:461
  218.5 4.1 %collective-permute-done.28 = bf16[384,256]{1,0:T(8,128)(2,1)S(1)} collective-permute-done((bf16[384,256]{1,0:T(8,128)(2,1)S(1)}, bf16[384,256]{1,0:T(8,128)(2,1)S(1)}, u32[]{:S(2)}, u32[]{:S(2)}) %collective-permute-start.28) | collective-permute-done | bytes 196640 | tf_op jit(solution)/shard_map/ppermute | solution.py:461
  223.1 6.8 %shard_map.63 = (f32[1536,256]{1,0:T(8,128)S(1)}, bf16[3072,256]{1,0:T(8,128)(2,1)S(1)}) custom-call(s32[3]{0:T(128)S(1)} %get-tuple-element.118.s, bf16[1536,6144]{1,0:T(8,128)(2,1)} %bitcast.21, f32[3072,256]{1,0:T(8,128)S(1)} %get-tuple-element.100.refs_0_, f32[3072,256]{1,0:T(8,128)} %copy-done.1, bf16[512,256]{1,0:T(8,128)(2,1)S(1)} %collective-permute-done.27.refs_2_, ...), custom_call_target="tpu_custom_call" | custom-call | flops 589824 | bytes 2304 | tf_op jit(solution)/shard_map/pallas_call | solution.py:104
  236.3 5.5 %shard_map.64 = (bf16[384,256]{1,0:T(8,128)(2,1)S(1)}, bf16[384,256]{1,0:T(8,128)(2,1)S(1)}, bf16[384,256]{1,0:T(8,128)(2,1)S(1)}, f32[384,256]{1,0:T(8,128)S(1)}) custom-call(s32[3]{0:T(128)S(1)} %get-tuple-element.118.s, bf16[1536,6144]{1,0:T(8,128)(2,1)} %bitcast.22, bf16[3072,256]{1,0:T(8,128)(2,1)S(1)} %get-tuple-element.115.refs_0_, ...), custom_call_target="tpu_custom_call" | custom-call | flops 589824 | bytes 2304 | tf_op jit(solution)/shard_map/pallas_call | solution.py:104
  243.7 4.3 %collective-permute-start.38 = (bf16[384,256]{1,0:T(8,128)(2,1)S(1)}, bf16[384,256]{1,0:T(8,128)(2,1)S(1)}, u32[]{:S(2)}, u32[]{:S(2)}) collective-permute-start(bf16[384,256]{1,0:T(8,128)(2,1)S(1)} %get-tuple-element.124), channel_id=1, source_target_pairs={{16,28},{20,24},{24,20},{28,16},{17,29},{21,25},{25,21},{29,17},{1... | collective-permute-start | bytes 589832 | tf_op jit(solution)/shard_map/ppermute | solution.py:461
  248.0 3.0 %collective-permute-start.36 = (bf16[384,256]{1,0:T(8,128)(2,1)S(1)}, bf16[384,256]{1,0:T(8,128)(2,1)S(1)}, u32[]{:S(2)}, u32[]{:S(2)}) collective-permute-start(bf16[384,256]{1,0:T(8,128)(2,1)S(1)} %get-tuple-element.117), channel_id=1, source_target_pairs={{16,20},{20,16},{24,28},{28,24},{17,21},{21,17},{25,29},{29,25},{1... | collective-permute-start | bytes 589832 | tf_op jit(solution)/shard_map/ppermute | solution.py:461
  251.0 9.5 %collective-permute-done.34.refs_4_ = bf16[384,256]{1,0:T(8,128)(2,1)S(1)} collective-permute-done((bf16[384,256]{1,0:T(8,128)(2,1)S(1)}, bf16[384,256]{1,0:T(8,128)(2,1)S(1)}, u32[]{:S(2)}, u32[]{:S(2)}) %collective-permute-start.34) | collective-permute-done | bytes 196640 | tf_op jit(solution)/shard_map/ppermute | solution.py:465
  271.0 5.0 %collective-permute-done.41.refs_6_ = bf16[384,256]{1,0:T(8,128)(2,1)S(1)} collective-permute-done((bf16[384,256]{1,0:T(8,128)(2,1)S(1)}, bf16[384,256]{1,0:T(8,128)(2,1)S(1)}, u32[]{:S(2)}, u32[]{:S(2)}) %collective-permute-start.41) | collective-permute-done | bytes 196640 | tf_op jit(solution)/shard_map/ppermute | solution.py:465
  276.0 10.4 %collective-permute-done.40.refs_5_ = bf16[384,256]{1,0:T(8,128)(2,1)S(1)} collective-permute-done((bf16[384,256]{1,0:T(8,128)(2,1)S(1)}, bf16[384,256]{1,0:T(8,128)(2,1)S(1)}, u32[]{:S(2)}, u32[]{:S(2)}) %collective-permute-start.40) | collective-permute-done | bytes 196640 | tf_op jit(solution)/shard_map/ppermute | solution.py:465
  (99 shorter events, 82.7 us)
Async XLA Ops:
  19.0 20.3 %collective-permute-start.3 = (bf16[1024,256]{1,0:T(8,128)(2,1)S(1)}, bf16[1024,256]{1,0:T(8,128)(2,1)S(1)}, u32[]{:S(2)}, u32[]{:S(2)}) collective-permute-start(bf16[1024,256]{1,0:T(8,128)(2,1)S(1)} %get-tuple-element.78), channel_id=1, source_target_pairs={{0,18},{1,19},{2,16},{3,17},{4,22},{5,23},{6,20},{7,21},{8,26},{9,... | collective-permute-start | bytes 1572872 | tf_op jit(solution)/shard_map/ppermute | solution.py:508
  20.3 27.9 %collective-permute-start.2 = (bf16[2048,256]{1,0:T(8,128)(2,1)}, bf16[2048,256]{1,0:T(8,128)(2,1)S(1)}, u32[]{:S(2)}, u32[]{:S(2)}) collective-permute-start(bf16[2048,256]{1,0:T(8,128)(2,1)} %get-tuple-element.77), channel_id=1, source_target_pairs={{0,2},{1,3},{2,0},{3,1},{4,6},{5,7},{6,4},{7,5},{8,10},{9,11},{10,... | collective-permute-start | bytes 3145736 | tf_op jit(solution)/shard_map/ppermute | solution.py:461
  39.3 12.4 %collective-permute-start.4 = (bf16[1024,256]{1,0:T(8,128)(2,1)S(1)}, bf16[1024,256]{1,0:T(8,128)(2,1)S(1)}, u32[]{:S(2)}, u32[]{:S(2)}) collective-permute-start(bf16[1024,256]{1,0:T(8,128)(2,1)S(1)} %collective-permute-done.3), channel_id=1, source_target_pairs={{16,0},{17,1},{18,2},{19,3},{20,4},{21,5},{22,6},{23,7},{24,8},{25... | collective-permute-start | bytes 1572872 | tf_op jit(solution)/shard_map/ppermute | solution.py:513
  54.4 45.1 %collective-permute-start.10 = (bf16[3072,256]{1,0:T(8,128)(2,1)}, bf16[3072,256]{1,0:T(8,128)(2,1)S(1)}, u32[]{:S(2)}, u32[]{:S(2)}) collective-permute-start(bf16[3072,256]{1,0:T(8,128)(2,1)} %get-tuple-element.88), channel_id=1, source_target_pairs={{0,2},{1,3},{2,0},{3,1},{4,6},{5,7},{6,4},{7,5},{8,10},{9,11},{10,... | collective-permute-start | bytes 4718600 | tf_op jit(solution)/shard_map/ppermute | solution.py:461
  65.5 33.9 %collective-permute-start.9 = (bf16[384,256]{1,0:T(8,128)(2,1)S(1)}, bf16[384,256]{1,0:T(8,128)(2,1)S(1)}, u32[]{:S(2)}, u32[]{:S(2)}) collective-permute-start(bf16[384,256]{1,0:T(8,128)(2,1)S(1)} %add_convert_fusion.3), channel_id=1, source_target_pairs={{0,16},{4,20},{8,24},{12,28},{1,17},{5,21},{9,25},{13,29},{2,18},{... | collective-permute-start | bytes 589832 | tf_op jit(solution)/shard_map/ppermute | solution.py:518
  107.5 16.4 %collective-permute-start.16 = (bf16[384,256]{1,0:T(8,128)(2,1)S(1)}, bf16[384,256]{1,0:T(8,128)(2,1)S(1)}, u32[]{:S(2)}, u32[]{:S(2)}) collective-permute-start(bf16[384,256]{1,0:T(8,128)(2,1)S(1)} %collective-permute-done.9.refs_0_), channel_id=1, source_target_pairs={{16,24},{20,28},{24,16},{28,20},{17,25},{21,29},{25,17},{29,21},{1... | collective-permute-start | bytes 589832 | tf_op jit(solution)/shard_map/ppermute | solution.py:461
  109.5 14.4 %collective-permute-start.15 = (bf16[384,256]{1,0:T(8,128)(2,1)S(1)}, bf16[384,256]{1,0:T(8,128)(2,1)S(1)}, u32[]{:S(2)}, u32[]{:S(2)}) collective-permute-start(bf16[384,256]{1,0:T(8,128)(2,1)S(1)} %collective-permute-done.9.refs_0_), channel_id=1, source_target_pairs={{16,20},{20,16},{24,28},{28,24},{17,21},{21,17},{25,29},{29,25},{1... | collective-permute-start | bytes 589832 | tf_op jit(solution)/shard_map/ppermute | solution.py:461
  137.5 42.0 %collective-permute-start.24 = (bf16[3072,256]{1,0:T(8,128)(2,1)S(1)}, bf16[3072,256]{1,0:T(8,128)(2,1)}, u32[]{:S(2)}, u32[]{:S(2)}) collective-permute-start(bf16[3072,256]{1,0:T(8,128)(2,1)S(1)} %get-tuple-element.102), channel_id=1, source_target_pairs={{16,18},{17,19},{18,16},{19,17},{20,22},{21,23},{22,20},{23,21},{2... | collective-permute-start | bytes 4718600 | tf_op jit(solution)/shard_map/ppermute | solution.py:461
  140.4 17.2 %collective-permute-start.19 = (bf16[384,256]{1,0:T(8,128)(2,1)S(1)}, bf16[384,256]{1,0:T(8,128)(2,1)S(1)}, u32[]{:S(2)}, u32[]{:S(2)}) collective-permute-start(bf16[384,256]{1,0:T(8,128)(2,1)S(1)} %add_convert_fusion.2), channel_id=1, source_target_pairs={{0,16},{4,20},{8,24},{12,28},{1,17},{5,21},{9,25},{13,29},{2,18},{... | collective-permute-start | bytes 589832 | tf_op jit(solution)/shard_map/ppermute | solution.py:518
  141.7 15.9 %collective-permute-start.22 = (bf16[384,256]{1,0:T(8,128)(2,1)S(1)}, bf16[384,256]{1,0:T(8,128)(2,1)S(1)}, u32[]{:S(2)}, u32[]{:S(2)}) collective-permute-start(bf16[384,256]{1,0:T(8,128)(2,1)S(1)} %add_convert_fusion.2), channel_id=1, source_target_pairs={{0,28},{4,24},{8,20},{12,16},{1,29},{5,25},{9,21},{13,17},{2,30},{... | collective-permute-start | bytes 589832 | tf_op jit(solution)/shard_map/ppermute | solution.py:518
  143.0 21.8 %collective-permute-start.21 = (bf16[384,256]{1,0:T(8,128)(2,1)S(1)}, bf16[384,256]{1,0:T(8,128)(2,1)S(1)}, u32[]{:S(2)}, u32[]{:S(2)}) collective-permute-start(bf16[384,256]{1,0:T(8,128)(2,1)S(1)} %add_convert_fusion.2), channel_id=1, source_target_pairs={{0,24},{4,28},{8,16},{12,20},{1,25},{5,29},{9,17},{13,21},{2,26},{... | collective-permute-start | bytes 589832 | tf_op jit(solution)/shard_map/ppermute | solution.py:518
  144.3 20.5 %collective-permute-start.20 = (bf16[384,256]{1,0:T(8,128)(2,1)S(1)}, bf16[384,256]{1,0:T(8,128)(2,1)S(1)}, u32[]{:S(2)}, u32[]{:S(2)}) collective-permute-start(bf16[384,256]{1,0:T(8,128)(2,1)S(1)} %add_convert_fusion.2), channel_id=1, source_target_pairs={{0,20},{4,16},{8,28},{12,24},{1,21},{5,17},{9,29},{13,25},{2,22},{... | collective-permute-start | bytes 589832 | tf_op jit(solution)/shard_map/ppermute | solution.py:518
  190.1 32.9 %collective-permute-start.31 = (bf16[2560,256]{1,0:T(8,128)(2,1)S(1)}, bf16[2560,256]{1,0:T(8,128)(2,1)S(1)}, u32[]{:S(2)}, u32[]{:S(2)}) collective-permute-start(bf16[2560,256]{1,0:T(8,128)(2,1)S(1)} %slice.23), channel_id=1, source_target_pairs={{16,18},{17,19},{18,16},{19,17},{20,22},{21,23},{22,20},{23,21},{2... | collective-permute-start | bytes 3932168 | tf_op jit(solution)/shard_map/ppermute | solution.py:461
  201.2 17.3 %collective-permute-start.29 = (bf16[384,256]{1,0:T(8,128)(2,1)S(1)}, bf16[384,256]{1,0:T(8,128)(2,1)S(1)}, u32[]{:S(2)}, u32[]{:S(2)}) collective-permute-start(bf16[384,256]{1,0:T(8,128)(2,1)S(1)} %get-tuple-element.111), channel_id=1, source_target_pairs={{16,24},{20,28},{24,16},{28,20},{17,25},{21,29},{25,17},{29,21},{1... | collective-permute-start | bytes 589832 | tf_op jit(solution)/shard_map/ppermute | solution.py:461
  203.1 15.4 %collective-permute-start.30 = (bf16[384,256]{1,0:T(8,128)(2,1)S(1)}, bf16[384,256]{1,0:T(8,128)(2,1)S(1)}, u32[]{:S(2)}, u32[]{:S(2)}) collective-permute-start(bf16[384,256]{1,0:T(8,128)(2,1)S(1)} %get-tuple-element.112), channel_id=1, source_target_pairs={{16,28},{20,24},{24,20},{28,16},{17,29},{21,25},{25,21},{29,17},{1... | collective-permute-start | bytes 589832 | tf_op jit(solution)/shard_map/ppermute | solution.py:461
  207.6 15.1 %collective-permute-start.28 = (bf16[384,256]{1,0:T(8,128)(2,1)S(1)}, bf16[384,256]{1,0:T(8,128)(2,1)S(1)}, u32[]{:S(2)}, u32[]{:S(2)}) collective-permute-start(bf16[384,256]{1,0:T(8,128)(2,1)S(1)} %get-tuple-element.106), channel_id=1, source_target_pairs={{16,20},{20,16},{24,28},{28,24},{17,21},{21,17},{25,29},{29,25},{1... | collective-permute-start | bytes 589832 | tf_op jit(solution)/shard_map/ppermute | solution.py:461
  231.8 16.2 %collective-permute-start.35 = (bf16[384,256]{1,0:T(8,128)(2,1)S(1)}, bf16[384,256]{1,0:T(8,128)(2,1)S(1)}, u32[]{:S(2)}, u32[]{:S(2)}) collective-permute-start(bf16[384,256]{1,0:T(8,128)(2,1)S(1)} %fusion.refs_2_), channel_id=1, source_target_pairs={{0,12},{4,8},{8,4},{12,0},{1,13},{5,9},{9,5},{13,1},{2,14},{6,10},... | collective-permute-start | bytes 589832 | tf_op jit(solution)/shard_map/ppermute | solution.py:465
  233.2 27.3 %collective-permute-start.34 = (bf16[384,256]{1,0:T(8,128)(2,1)S(1)}, bf16[384,256]{1,0:T(8,128)(2,1)S(1)}, u32[]{:S(2)}, u32[]{:S(2)}) collective-permute-start(bf16[384,256]{1,0:T(8,128)(2,1)S(1)} %fusion.refs_2_), channel_id=1, source_target_pairs={{0,8},{4,12},{8,0},{12,4},{1,9},{5,13},{9,1},{13,5},{2,10},{6,14},... | collective-permute-start | bytes 589832 | tf_op jit(solution)/shard_map/ppermute | solution.py:465
  233.7 26.8 %collective-permute-start.33 = (bf16[384,256]{1,0:T(8,128)(2,1)S(1)}, bf16[384,256]{1,0:T(8,128)(2,1)S(1)}, u32[]{:S(2)}, u32[]{:S(2)}) collective-permute-start(bf16[384,256]{1,0:T(8,128)(2,1)S(1)} %fusion.refs_2_), channel_id=1, source_target_pairs={{0,4},{4,0},{8,12},{12,8},{1,5},{5,1},{9,13},{13,9},{2,6},{6,2},{1... | collective-permute-start | bytes 589832 | tf_op jit(solution)/shard_map/ppermute | solution.py:465
  241.8 22.9 %collective-permute-start.37 = (bf16[384,256]{1,0:T(8,128)(2,1)S(1)}, bf16[384,256]{1,0:T(8,128)(2,1)S(1)}, u32[]{:S(2)}, u32[]{:S(2)}) collective-permute-start(bf16[384,256]{1,0:T(8,128)(2,1)S(1)} %get-tuple-element.123), channel_id=1, source_target_pairs={{16,24},{20,28},{24,16},{28,20},{17,25},{21,29},{25,17},{29,21},{1... | collective-permute-start | bytes 589832 | tf_op jit(solution)/shard_map/ppermute | solution.py:461
  243.7 21.0 %collective-permute-start.38 = (bf16[384,256]{1,0:T(8,128)(2,1)S(1)}, bf16[384,256]{1,0:T(8,128)(2,1)S(1)}, u32[]{:S(2)}, u32[]{:S(2)}) collective-permute-start(bf16[384,256]{1,0:T(8,128)(2,1)S(1)} %get-tuple-element.124), channel_id=1, source_target_pairs={{16,28},{20,24},{24,20},{28,16},{17,29},{21,25},{25,21},{29,17},{1... | collective-permute-start | bytes 589832 | tf_op jit(solution)/shard_map/ppermute | solution.py:461
  248.0 18.5 %collective-permute-start.36 = (bf16[384,256]{1,0:T(8,128)(2,1)S(1)}, bf16[384,256]{1,0:T(8,128)(2,1)S(1)}, u32[]{:S(2)}, u32[]{:S(2)}) collective-permute-start(bf16[384,256]{1,0:T(8,128)(2,1)S(1)} %get-tuple-element.117), channel_id=1, source_target_pairs={{16,20},{20,16},{24,28},{28,24},{17,21},{21,17},{25,29},{29,25},{1... | collective-permute-start | bytes 589832 | tf_op jit(solution)/shard_map/ppermute | solution.py:461
  268.4 17.9 %collective-permute-start.40 = (bf16[384,256]{1,0:T(8,128)(2,1)S(1)}, bf16[384,256]{1,0:T(8,128)(2,1)S(1)}, u32[]{:S(2)}, u32[]{:S(2)}) collective-permute-start(bf16[384,256]{1,0:T(8,128)(2,1)S(1)} %fusion.1.refs_3_), channel_id=1, source_target_pairs={{0,8},{4,12},{8,0},{12,4},{1,9},{5,13},{9,1},{13,5},{2,10},{6,14},... | collective-permute-start | bytes 589832 | tf_op jit(solution)/shard_map/ppermute | solution.py:465
  270.7 15.7 %collective-permute-start.39 = (bf16[384,256]{1,0:T(8,128)(2,1)S(1)}, bf16[384,256]{1,0:T(8,128)(2,1)S(1)}, u32[]{:S(2)}, u32[]{:S(2)}) collective-permute-start(bf16[384,256]{1,0:T(8,128)(2,1)S(1)} %fusion.1.refs_3_), channel_id=1, source_target_pairs={{0,4},{4,0},{8,12},{12,8},{1,5},{5,1},{9,13},{13,9},{2,6},{6,2},{1... | collective-permute-start | bytes 589832 | tf_op jit(solution)/shard_map/ppermute | solution.py:465
  (23 other events, 151.3 us)

commit v7 on v6

--- a/solution.py
+++ b/solution.py
@@ -602,7 +602,8 @@
             steps.last = crossed
             gathered[k] = [crossed] + [within(1, d, crossed, "hid") for d in range(1, PARTS)]
         else:
-            gathered[k] = [across(terms[k], d) for d in range(PARTS)]
+            far = within(0, PARTS - 1, terms[k], "hid")
+            gathered[k] = [across(terms[k], d) for d in range(PARTS - 1)] + [across(far, 0)]
             steps.last = gathered[k][0]
 
     def up_hidden(k):

time: 290 us -> 292 us (level)
    ppermute x27 -> x28, starting transfers between devices: 50.1 us -> 51.1 us  [within(): return lax.ppermute(block, ('section', axis), pairs)]
    ppermute x27 -> x28, waiting for transfers between devices: 28.7 us -> 28.7 us  [within(): return lax.ppermute(block, ('section', axis), pairs)]
  transfers between devices with their start and end apart: 42 -> 43, of which waited for: 18 -> 17; matrix products, arithmetic and copies ran while one was open for 0% -> 0% of each run, Pallas kernels for 14% -> 14%
where the time goes in v7:
time: 292 us; the launch traced here: 291 us
  waiting for transfers between devices  127 us (43%)
  Pallas kernels  86.7 us (30%)
  starting transfers between devices  71.7 us (25%)
  local copies, waits for them, and re-layouts  4.6 us (2%)
    ppermute x5, waiting for transfers between devices, across(): return lax.ppermute(term, ('section', 'hid'), pairs)  52.1 us
    ppermute x28, starting transfers between devices, within(): return lax.ppermute(block, ('section', axis), pairs)  51.1 us
    pallas_call x8, Pallas kernels, product(): pl.pallas_call(body, in_specs=[SMEM, ANY] + [VMEM if first is None else A...  30.8 us
    ppermute x28, waiting for transfers between devices, within(): return lax.ppermute(block, ('section', axis), pairs)  28.7 us
    ppermute x6, waiting for transfers between devices, everywhere(): return lax.ppermute(block, axis, [(i, i ^ distance) for i in range(size)])  25.1 us
    ppermute x2, waiting for transfers between devices, detour(): return lax.ppermute(piece, ('section', 'wid'), pairs)  17.1 us
    pallas_call x2, Pallas kernels, pair_product(): pl.pallas_call(body, in_specs=[SMEM, ANY, VMEM, VMEM], out_specs=[VMEM, V...  16.8 us
    pallas_call x1, Pallas kernels, split_rows(): pl.pallas_call(body, in_specs=[SMEM, ANY], out_specs=ANY, out_shape=jax.S...  14.5 us
  transfers between devices with their start and end apart: 43, of which 17 were waited for; matrix products, arithmetic and copies ran while one was open for 0% of the time, Pallas kernels for 14%

profile of v7, /device:TPU:2, one launch (start us, length us, event | category | flops | bytes accessed | tf_op | source)
XLA Modules:
  0.0 290.6 jit_solution(17588747010990529740)
XLA Ops:
  0.1 14.5 %shard_map.46.mat_ref = bf16[2,3072,1536]{2,1,0:T(8,128)(2,1)} custom-call(s32[3]{0:T(128)S(1)} %get-tuple-element.118.s, bf16[6144,1536]{1,0:T(8,128)(2,1)} %bitcast.23), custom_call_target="tpu_custom_call" | custom-call | flops 1179648 | bytes 9216 | tf_op jit(solution)/shard_map/pallas_call | solution.py:320
  22.8 16.6 %collective-permute-done.3 = bf16[1024,256]{1,0:T(8,128)(2,1)S(1)} collective-permute-done((bf16[1024,256]{1,0:T(8,128)(2,1)S(1)}, bf16[1024,256]{1,0:T(8,128)(2,1)S(1)}, u32[]{:S(2)}, u32[]{:S(2)}) %collective-permute-start.3) | collective-permute-done | bytes 524320 | tf_op jit(solution)/shard_map/ppermute | solution.py:508
  40.6 5.9 %shard_map.51.slope_ref.refs_1_ = f32[3072,256]{1,0:T(8,128)S(1)} custom-call(s32[3]{0:T(128)S(1)} %get-tuple-element.86.s, f32[512,6144]{1,0:T(8,128)} %bitcast.28), custom_call_target="tpu_custom_call" | custom-call | flops 192 | bytes 1536 | tf_op jit(solution)/shard_map/pallas_call | solution.py:346
  48.2 3.5 %collective-permute-done.4.refs_1_ = bf16[1024,256]{1,0:T(8,128)(2,1)S(1)} collective-permute-done((bf16[1024,256]{1,0:T(8,128)(2,1)S(1)}, bf16[1024,256]{1,0:T(8,128)(2,1)S(1)}, u32[]{:S(2)}, u32[]{:S(2)}) %collective-permute-start.4) | collective-permute-done | bytes 524320 | tf_op jit(solution)/shard_map/ppermute | solution.py:513
  57.8 5.9 %shard_map.54.slope_ref.refs_1_ = f32[3072,256]{1,0:T(8,128)S(1)} custom-call(s32[3]{0:T(128)S(1)} %get-tuple-element.86.s, f32[512,6144]{1,0:T(8,128)} %bitcast.29), custom_call_target="tpu_custom_call" | custom-call | flops 192 | bytes 1536 | tf_op jit(solution)/shard_map/pallas_call | solution.py:346
  66.8 32.6 %collective-permute-done.9.refs_0_ = bf16[384,256]{1,0:T(8,128)(2,1)S(1)} collective-permute-done((bf16[384,256]{1,0:T(8,128)(2,1)S(1)}, bf16[384,256]{1,0:T(8,128)(2,1)S(1)}, u32[]{:S(2)}, u32[]{:S(2)}) %collective-permute-start.9) | collective-permute-done | bytes 196640 | tf_op jit(solution)/shard_map/ppermute | solution.py:518
  102.1 5.4 %collective-permute-start.17 = (bf16[384,256]{1,0:T(8,128)(2,1)S(1)}, bf16[384,256]{1,0:T(8,128)(2,1)S(1)}, u32[]{:S(2)}, u32[]{:S(2)}) collective-permute-start(bf16[384,256]{1,0:T(8,128)(2,1)S(1)} %collective-permute-done.9.refs_0_), channel_id=1, source_target_pairs={{16,28},{20,24},{24,20},{28,16},{17,29},{21,25},{25,21},{29,17},{1... | collective-permute-start | bytes 589832 | tf_op jit(solution)/shard_map/ppermute | solution.py:461
  113.1 10.8 %collective-permute-done.16.refs_2_ = bf16[384,256]{1,0:T(8,128)(2,1)S(1)} collective-permute-done((bf16[384,256]{1,0:T(8,128)(2,1)S(1)}, bf16[384,256]{1,0:T(8,128)(2,1)S(1)}, u32[]{:S(2)}, u32[]{:S(2)}) %collective-permute-start.16) | collective-permute-done | bytes 196640 | tf_op jit(solution)/shard_map/ppermute | solution.py:461
  129.1 8.4 %shard_map.58 = (f32[3072,256]{1,0:T(8,128)S(1)}, bf16[3072,256]{1,0:T(8,128)(2,1)S(1)}) custom-call(s32[3]{0:T(128)S(1)} %get-tuple-element.118.s, bf16[2,3072,1536]{2,1,0:T(8,128)(2,1)} %shard_map.46.mat_ref, bf16[1536,256]{1,0:T(8,128)(2,1)S(1)} %get-tuple-element.95.own_ref, bf16[1536,256]{1,0:T(8,128)(2,1)S(1)} %collective-permute-done.18.other_ref), custom_call_target="tpu_custom_call" | custom-call | flops 1179648 | bytes 4608 | tf_op jit(solution)/shard_map/pallas_call | solution.py:159
  146.3 12.0 %collective-permute-done.19.refs_0_ = bf16[384,256]{1,0:T(8,128)(2,1)S(1)} collective-permute-done((bf16[384,256]{1,0:T(8,128)(2,1)S(1)}, bf16[384,256]{1,0:T(8,128)(2,1)S(1)}, u32[]{:S(2)}, u32[]{:S(2)}) %collective-permute-start.19) | collective-permute-done | bytes 196640 | tf_op jit(solution)/shard_map/ppermute | solution.py:518
  158.3 5.1 %collective-permute-done.21.refs_2_ = bf16[384,256]{1,0:T(8,128)(2,1)S(1)} collective-permute-done((bf16[384,256]{1,0:T(8,128)(2,1)S(1)}, bf16[384,256]{1,0:T(8,128)(2,1)S(1)}, u32[]{:S(2)}, u32[]{:S(2)}) %collective-permute-start.21) | collective-permute-done | bytes 196640 | tf_op jit(solution)/shard_map/ppermute | solution.py:518
  172.1 8.4 %shard_map.60 = (f32[3072,256]{1,0:T(8,128)S(1)}, bf16[3072,256]{1,0:T(8,128)(2,1)S(1)}) custom-call(s32[3]{0:T(128)S(1)} %get-tuple-element.118.s, bf16[2,3072,1536]{2,1,0:T(8,128)(2,1)} %shard_map.46.mat_ref, bf16[1536,256]{1,0:T(8,128)(2,1)S(1)} %get-tuple-element.99.own_ref, bf16[1536,256]{1,0:T(8,128)(2,1)S(1)} %collective-permute-done.24.other_ref), custom_call_target="tpu_custom_call" | custom-call | flops 1179648 | bytes 4608 | tf_op jit(solution)/shard_map/pallas_call | solution.py:159
  180.5 8.5 %shard_map.61 = (f32[1536,256]{1,0:T(8,128)}, bf16[3072,256]{1,0:T(8,128)(2,1)S(1)}) custom-call(s32[3]{0:T(128)S(1)} %get-tuple-element.118.s, bf16[1536,6144]{1,0:T(8,128)(2,1)} %bitcast.19, f32[3072,256]{1,0:T(8,128)S(1)} %get-tuple-element.96.refs_0_, f32[3072,256]{1,0:T(8,128)} %copy-done.2, bf16[3072,256]{1,0:T(8,128)(2,1)} %collective-permute-done.25.refs_2_), custom_call_target="tpu_custom_call" | custom-call | flops 589824 | bytes 2304 | tf_op jit(solution)/shard_map/pallas_call | solution.py:104
  195.2 5.5 %shard_map.62 = (bf16[384,256]{1,0:T(8,128)(2,1)S(1)}, bf16[384,256]{1,0:T(8,128)(2,1)S(1)}, bf16[384,256]{1,0:T(8,128)(2,1)S(1)}, f32[384,256]{1,0:T(8,128)S(1)}) custom-call(s32[3]{0:T(128)S(1)} %get-tuple-element.118.s, bf16[1536,6144]{1,0:T(8,128)(2,1)} %bitcast.20, bf16[3072,256]{1,0:T(8,128)(2,1)S(1)} %get-tuple-element.103.refs_0_, ...), custom_call_target="tpu_custom_call" | custom-call | flops 589824 | bytes 2304 | tf_op jit(solution)/shard_map/pallas_call | solution.py:104
  202.6 3.4 %collective-permute-start.30 = (bf16[384,256]{1,0:T(8,128)(2,1)S(1)}, bf16[384,256]{1,0:T(8,128)(2,1)S(1)}, u32[]{:S(2)}, u32[]{:S(2)}) collective-permute-start(bf16[384,256]{1,0:T(8,128)(2,1)S(1)} %get-tuple-element.111), channel_id=1, source_target_pairs={{16,24},{20,28},{24,16},{28,20},{17,25},{21,29},{25,17},{29,21},{1... | collective-permute-start | bytes 589832 | tf_op jit(solution)/shard_map/ppermute | solution.py:461
  211.8 8.2 %collective-permute-done.30 = bf16[384,256]{1,0:T(8,128)(2,1)S(1)} collective-permute-done((bf16[384,256]{1,0:T(8,128)(2,1)S(1)}, bf16[384,256]{1,0:T(8,128)(2,1)S(1)}, u32[]{:S(2)}, u32[]{:S(2)}) %collective-permute-start.30) | collective-permute-done | bytes 196640 | tf_op jit(solution)/shard_map/ppermute | solution.py:461
  220.0 4.1 %collective-permute-done.29 = bf16[384,256]{1,0:T(8,128)(2,1)S(1)} collective-permute-done((bf16[384,256]{1,0:T(8,128)(2,1)S(1)}, bf16[384,256]{1,0:T(8,128)(2,1)S(1)}, u32[]{:S(2)}, u32[]{:S(2)}) %collective-permute-start.29) | collective-permute-done | bytes 196640 | tf_op jit(solution)/shard_map/ppermute | solution.py:461
  224.2 6.8 %shard_map.63 = (f32[1536,256]{1,0:T(8,128)S(1)}, bf16[3072,256]{1,0:T(8,128)(2,1)S(1)}) custom-call(s32[3]{0:T(128)S(1)} %get-tuple-element.118.s, bf16[1536,6144]{1,0:T(8,128)(2,1)} %bitcast.21, f32[3072,256]{1,0:T(8,128)S(1)} %get-tuple-element.100.refs_0_, f32[3072,256]{1,0:T(8,128)} %copy-done.1, bf16[512,256]{1,0:T(8,128)(2,1)S(1)} %collective-permute-done.28.refs_2_, ...), custom_call_target="tpu_custom_call" | custom-call | flops 589824 | bytes 2304 | tf_op jit(solution)/shard_map/pallas_call | solution.py:104
  237.4 5.5 %shard_map.64 = (bf16[384,256]{1,0:T(8,128)(2,1)S(1)}, bf16[384,256]{1,0:T(8,128)(2,1)S(1)}, bf16[384,256]{1,0:T(8,128)(2,1)S(1)}, f32[384,256]{1,0:T(8,128)S(1)}) custom-call(s32[3]{0:T(128)S(1)} %get-tuple-element.118.s, bf16[1536,6144]{1,0:T(8,128)(2,1)} %bitcast.22, bf16[3072,256]{1,0:T(8,128)(2,1)S(1)} %get-tuple-element.115.refs_0_, ...), custom_call_target="tpu_custom_call" | custom-call | flops 589824 | bytes 2304 | tf_op jit(solution)/shard_map/pallas_call | solution.py:104
  245.5 3.6 %collective-permute-start.39 = (bf16[384,256]{1,0:T(8,128)(2,1)S(1)}, bf16[384,256]{1,0:T(8,128)(2,1)S(1)}, u32[]{:S(2)}, u32[]{:S(2)}) collective-permute-start(bf16[384,256]{1,0:T(8,128)(2,1)S(1)} %get-tuple-element.124), channel_id=1, source_target_pairs={{16,28},{20,24},{24,20},{28,16},{17,29},{21,25},{25,21},{29,17},{1... | collective-permute-start | bytes 589832 | tf_op jit(solution)/shard_map/ppermute | solution.py:461
  249.2 3.0 %collective-permute-start.37 = (bf16[384,256]{1,0:T(8,128)(2,1)S(1)}, bf16[384,256]{1,0:T(8,128)(2,1)S(1)}, u32[]{:S(2)}, u32[]{:S(2)}) collective-permute-start(bf16[384,256]{1,0:T(8,128)(2,1)S(1)} %get-tuple-element.117), channel_id=1, source_target_pairs={{16,20},{20,16},{24,28},{28,24},{17,21},{21,17},{25,29},{29,25},{1... | collective-permute-start | bytes 589832 | tf_op jit(solution)/shard_map/ppermute | solution.py:461
  252.2 9.7 %collective-permute-done.35.refs_4_ = bf16[384,256]{1,0:T(8,128)(2,1)S(1)} collective-permute-done((bf16[384,256]{1,0:T(8,128)(2,1)S(1)}, bf16[384,256]{1,0:T(8,128)(2,1)S(1)}, u32[]{:S(2)}, u32[]{:S(2)}) %collective-permute-start.35) | collective-permute-done | bytes 196640 | tf_op jit(solution)/shard_map/ppermute | solution.py:465
  272.5 4.2 %collective-permute-done.42.refs_6_ = bf16[384,256]{1,0:T(8,128)(2,1)S(1)} collective-permute-done((bf16[384,256]{1,0:T(8,128)(2,1)S(1)}, bf16[384,256]{1,0:T(8,128)(2,1)S(1)}, u32[]{:S(2)}, u32[]{:S(2)}) %collective-permute-start.42) | collective-permute-done | bytes 196640 | tf_op jit(solution)/shard_map/ppermute | solution.py:465
  276.7 11.2 %collective-permute-done.41.refs_5_ = bf16[384,256]{1,0:T(8,128)(2,1)S(1)} collective-permute-done((bf16[384,256]{1,0:T(8,128)(2,1)S(1)}, bf16[384,256]{1,0:T(8,128)(2,1)S(1)}, u32[]{:S(2)}, u32[]{:S(2)}) %collective-permute-start.41) | collective-permute-done | bytes 196640 | tf_op jit(solution)/shard_map/ppermute | solution.py:465
  (101 shorter events, 87.2 us)
Async XLA Ops:
  19.0 20.4 %collective-permute-start.3 = (bf16[1024,256]{1,0:T(8,128)(2,1)S(1)}, bf16[1024,256]{1,0:T(8,128)(2,1)S(1)}, u32[]{:S(2)}, u32[]{:S(2)}) collective-permute-start(bf16[1024,256]{1,0:T(8,128)(2,1)S(1)} %get-tuple-element.78), channel_id=1, source_target_pairs={{0,18},{1,19},{2,16},{3,17},{4,22},{5,23},{6,20},{7,21},{8,26},{9,... | collective-permute-start | bytes 1572872 | tf_op jit(solution)/shard_map/ppermute | solution.py:508
  20.3 27.9 %collective-permute-start.2 = (bf16[2048,256]{1,0:T(8,128)(2,1)}, bf16[2048,256]{1,0:T(8,128)(2,1)S(1)}, u32[]{:S(2)}, u32[]{:S(2)}) collective-permute-start(bf16[2048,256]{1,0:T(8,128)(2,1)} %get-tuple-element.77), channel_id=1, source_target_pairs={{0,2},{1,3},{2,0},{3,1},{4,6},{5,7},{6,4},{7,5},{8,10},{9,11},{10,... | collective-permute-start | bytes 3145736 | tf_op jit(solution)/shard_map/ppermute | solution.py:461
  39.3 12.4 %collective-permute-start.4 = (bf16[1024,256]{1,0:T(8,128)(2,1)S(1)}, bf16[1024,256]{1,0:T(8,128)(2,1)S(1)}, u32[]{:S(2)}, u32[]{:S(2)}) collective-permute-start(bf16[1024,256]{1,0:T(8,128)(2,1)S(1)} %collective-permute-done.3), channel_id=1, source_target_pairs={{16,0},{17,1},{18,2},{19,3},{20,4},{21,5},{22,6},{23,7},{24,8},{25... | collective-permute-start | bytes 1572872 | tf_op jit(solution)/shard_map/ppermute | solution.py:513
  54.4 45.1 %collective-permute-start.10 = (bf16[3072,256]{1,0:T(8,128)(2,1)}, bf16[3072,256]{1,0:T(8,128)(2,1)S(1)}, u32[]{:S(2)}, u32[]{:S(2)}) collective-permute-start(bf16[3072,256]{1,0:T(8,128)(2,1)} %get-tuple-element.88), channel_id=1, source_target_pairs={{0,2},{1,3},{2,0},{3,1},{4,6},{5,7},{6,4},{7,5},{8,10},{9,11},{10,... | collective-permute-start | bytes 4718600 | tf_op jit(solution)/shard_map/ppermute | solution.py:461
  65.5 33.9 %collective-permute-start.9 = (bf16[384,256]{1,0:T(8,128)(2,1)S(1)}, bf16[384,256]{1,0:T(8,128)(2,1)S(1)}, u32[]{:S(2)}, u32[]{:S(2)}) collective-permute-start(bf16[384,256]{1,0:T(8,128)(2,1)S(1)} %add_convert_fusion.3), channel_id=1, source_target_pairs={{0,16},{4,20},{8,24},{12,28},{1,17},{5,21},{9,25},{13,29},{2,18},{... | collective-permute-start | bytes 589832 | tf_op jit(solution)/shard_map/ppermute | solution.py:518
  107.5 16.4 %collective-permute-start.16 = (bf16[384,256]{1,0:T(8,128)(2,1)S(1)}, bf16[384,256]{1,0:T(8,128)(2,1)S(1)}, u32[]{:S(2)}, u32[]{:S(2)}) collective-permute-start(bf16[384,256]{1,0:T(8,128)(2,1)S(1)} %collective-permute-done.9.refs_0_), channel_id=1, source_target_pairs={{16,24},{20,28},{24,16},{28,20},{17,25},{21,29},{25,17},{29,21},{1... | collective-permute-start | bytes 589832 | tf_op jit(solution)/shard_map/ppermute | solution.py:461
  109.5 14.4 %collective-permute-start.15 = (bf16[384,256]{1,0:T(8,128)(2,1)S(1)}, bf16[384,256]{1,0:T(8,128)(2,1)S(1)}, u32[]{:S(2)}, u32[]{:S(2)}) collective-permute-start(bf16[384,256]{1,0:T(8,128)(2,1)S(1)} %collective-permute-done.9.refs_0_), channel_id=1, source_target_pairs={{16,20},{20,16},{24,28},{28,24},{17,21},{21,17},{25,29},{29,25},{1... | collective-permute-start | bytes 589832 | tf_op jit(solution)/shard_map/ppermute | solution.py:461
  137.5 42.9 %collective-permute-start.25 = (bf16[3072,256]{1,0:T(8,128)(2,1)S(1)}, bf16[3072,256]{1,0:T(8,128)(2,1)}, u32[]{:S(2)}, u32[]{:S(2)}) collective-permute-start(bf16[3072,256]{1,0:T(8,128)(2,1)S(1)} %get-tuple-element.102), channel_id=1, source_target_pairs={{16,18},{17,19},{18,16},{19,17},{20,22},{21,23},{22,20},{23,21},{2... | collective-permute-start | bytes 4718600 | tf_op jit(solution)/shard_map/ppermute | solution.py:461
  141.1 17.2 %collective-permute-start.19 = (bf16[384,256]{1,0:T(8,128)(2,1)S(1)}, bf16[384,256]{1,0:T(8,128)(2,1)S(1)}, u32[]{:S(2)}, u32[]{:S(2)}) collective-permute-start(bf16[384,256]{1,0:T(8,128)(2,1)S(1)} %add_convert_fusion.2), channel_id=1, source_target_pairs={{0,16},{4,20},{8,24},{12,28},{1,17},{5,21},{9,25},{13,29},{2,18},{... | collective-permute-start | bytes 589832 | tf_op jit(solution)/shard_map/ppermute | solution.py:518
  142.4 21.0 %collective-permute-start.21 = (bf16[384,256]{1,0:T(8,128)(2,1)S(1)}, bf16[384,256]{1,0:T(8,128)(2,1)S(1)}, u32[]{:S(2)}, u32[]{:S(2)}) collective-permute-start(bf16[384,256]{1,0:T(8,128)(2,1)S(1)} %add_convert_fusion.2), channel_id=1, source_target_pairs={{0,24},{4,28},{8,16},{12,20},{1,25},{5,29},{9,17},{13,21},{2,26},{... | collective-permute-start | bytes 589832 | tf_op jit(solution)/shard_map/ppermute | solution.py:518
  143.7 19.7 %collective-permute-start.20 = (bf16[384,256]{1,0:T(8,128)(2,1)S(1)}, bf16[384,256]{1,0:T(8,128)(2,1)S(1)}, u32[]{:S(2)}, u32[]{:S(2)}) collective-permute-start(bf16[384,256]{1,0:T(8,128)(2,1)S(1)} %add_convert_fusion.2), channel_id=1, source_target_pairs={{0,20},{4,16},{8,28},{12,24},{1,21},{5,17},{9,29},{13,25},{2,22},{... | collective-permute-start | bytes 589832 | tf_op jit(solution)/shard_map/ppermute | solution.py:518
  145.0 20.8 %collective-permute-start.23 = (bf16[384,256]{1,0:T(8,128)(2,1)S(1)}, bf16[384,256]{1,0:T(8,128)(2,1)S(1)}, u32[]{:S(2)}, u32[]{:S(2)}) collective-permute-start(bf16[384,256]{1,0:T(8,128)(2,1)S(1)} %collective-permute-done.22), channel_id=1, source_target_pairs={{0,16},{4,20},{8,24},{12,28},{1,17},{5,21},{9,25},{13,29},{2,18},{... | collective-permute-start | bytes 589832 | tf_op jit(solution)/shard_map/ppermute | solution.py:518
  191.1 33.1 %collective-permute-start.32 = (bf16[2560,256]{1,0:T(8,128)(2,1)S(1)}, bf16[2560,256]{1,0:T(8,128)(2,1)S(1)}, u32[]{:S(2)}, u32[]{:S(2)}) collective-permute-start(bf16[2560,256]{1,0:T(8,128)(2,1)S(1)} %slice.23), channel_id=1, source_target_pairs={{16,18},{17,19},{18,16},{19,17},{20,22},{21,23},{22,20},{23,21},{2... | collective-permute-start | bytes 3932168 | tf_op jit(solution)/shard_map/ppermute | solution.py:461
  202.6 17.4 %collective-permute-start.30 = (bf16[384,256]{1,0:T(8,128)(2,1)S(1)}, bf16[384,256]{1,0:T(8,128)(2,1)S(1)}, u32[]{:S(2)}, u32[]{:S(2)}) collective-permute-start(bf16[384,256]{1,0:T(8,128)(2,1)S(1)} %get-tuple-element.111), channel_id=1, source_target_pairs={{16,24},{20,28},{24,16},{28,20},{17,25},{21,29},{25,17},{29,21},{1... | collective-permute-start | bytes 589832 | tf_op jit(solution)/shard_map/ppermute | solution.py:461
  206.0 14.0 %collective-permute-start.31 = (bf16[384,256]{1,0:T(8,128)(2,1)S(1)}, bf16[384,256]{1,0:T(8,128)(2,1)S(1)}, u32[]{:S(2)}, u32[]{:S(2)}) collective-permute-start(bf16[384,256]{1,0:T(8,128)(2,1)S(1)} %get-tuple-element.112), channel_id=1, source_target_pairs={{16,28},{20,24},{24,20},{28,16},{17,29},{21,25},{25,21},{29,17},{1... | collective-permute-start | bytes 589832 | tf_op jit(solution)/shard_map/ppermute | solution.py:461
  209.0 15.1 %collective-permute-start.29 = (bf16[384,256]{1,0:T(8,128)(2,1)S(1)}, bf16[384,256]{1,0:T(8,128)(2,1)S(1)}, u32[]{:S(2)}, u32[]{:S(2)}) collective-permute-start(bf16[384,256]{1,0:T(8,128)(2,1)S(1)} %get-tuple-element.106), channel_id=1, source_target_pairs={{16,20},{20,16},{24,28},{28,24},{17,21},{21,17},{25,29},{29,25},{1... | collective-permute-start | bytes 589832 | tf_op jit(solution)/shard_map/ppermute | solution.py:461
  233.0 16.2 %collective-permute-start.36 = (bf16[384,256]{1,0:T(8,128)(2,1)S(1)}, bf16[384,256]{1,0:T(8,128)(2,1)S(1)}, u32[]{:S(2)}, u32[]{:S(2)}) collective-permute-start(bf16[384,256]{1,0:T(8,128)(2,1)S(1)} %fusion.refs_2_), channel_id=1, source_target_pairs={{0,12},{4,8},{8,4},{12,0},{1,13},{5,9},{9,5},{13,1},{2,14},{6,10},... | collective-permute-start | bytes 589832 | tf_op jit(solution)/shard_map/ppermute | solution.py:465
  235.2 26.8 %collective-permute-start.35 = (bf16[384,256]{1,0:T(8,128)(2,1)S(1)}, bf16[384,256]{1,0:T(8,128)(2,1)S(1)}, u32[]{:S(2)}, u32[]{:S(2)}) collective-permute-start(bf16[384,256]{1,0:T(8,128)(2,1)S(1)} %fusion.refs_2_), channel_id=1, source_target_pairs={{0,8},{4,12},{8,0},{12,4},{1,9},{5,13},{9,1},{13,5},{2,10},{6,14},... | collective-permute-start | bytes 589832 | tf_op jit(solution)/shard_map/ppermute | solution.py:465
  235.2 26.8 %collective-permute-start.34 = (bf16[384,256]{1,0:T(8,128)(2,1)S(1)}, bf16[384,256]{1,0:T(8,128)(2,1)S(1)}, u32[]{:S(2)}, u32[]{:S(2)}) collective-permute-start(bf16[384,256]{1,0:T(8,128)(2,1)S(1)} %fusion.refs_2_), channel_id=1, source_target_pairs={{0,4},{4,0},{8,12},{12,8},{1,5},{5,1},{9,13},{13,9},{2,6},{6,2},{1... | collective-permute-start | bytes 589832 | tf_op jit(solution)/shard_map/ppermute | solution.py:465
  242.9 23.2 %collective-permute-start.38 = (bf16[384,256]{1,0:T(8,128)(2,1)S(1)}, bf16[384,256]{1,0:T(8,128)(2,1)S(1)}, u32[]{:S(2)}, u32[]{:S(2)}) collective-permute-start(bf16[384,256]{1,0:T(8,128)(2,1)S(1)} %get-tuple-element.123), channel_id=1, source_target_pairs={{16,24},{20,28},{24,16},{28,20},{17,25},{21,29},{25,17},{29,21},{1... | collective-permute-start | bytes 589832 | tf_op jit(solution)/shard_map/ppermute | solution.py:461
  245.5 20.6 %collective-permute-start.39 = (bf16[384,256]{1,0:T(8,128)(2,1)S(1)}, bf16[384,256]{1,0:T(8,128)(2,1)S(1)}, u32[]{:S(2)}, u32[]{:S(2)}) collective-permute-start(bf16[384,256]{1,0:T(8,128)(2,1)S(1)} %get-tuple-element.124), channel_id=1, source_target_pairs={{16,28},{20,24},{24,20},{28,16},{17,29},{21,25},{25,21},{29,17},{1... | collective-permute-start | bytes 589832 | tf_op jit(solution)/shard_map/ppermute | solution.py:461
  249.2 18.8 %collective-permute-start.37 = (bf16[384,256]{1,0:T(8,128)(2,1)S(1)}, bf16[384,256]{1,0:T(8,128)(2,1)S(1)}, u32[]{:S(2)}, u32[]{:S(2)}) collective-permute-start(bf16[384,256]{1,0:T(8,128)(2,1)S(1)} %get-tuple-element.117), channel_id=1, source_target_pairs={{16,20},{20,16},{24,28},{28,24},{17,21},{21,17},{25,29},{29,25},{1... | collective-permute-start | bytes 589832 | tf_op jit(solution)/shard_map/ppermute | solution.py:461
  270.5 17.3 %collective-permute-start.41 = (bf16[384,256]{1,0:T(8,128)(2,1)S(1)}, bf16[384,256]{1,0:T(8,128)(2,1)S(1)}, u32[]{:S(2)}, u32[]{:S(2)}) collective-permute-start(bf16[384,256]{1,0:T(8,128)(2,1)S(1)} %fusion.1.refs_3_), channel_id=1, source_target_pairs={{0,8},{4,12},{8,0},{12,4},{1,9},{5,13},{9,1},{13,5},{2,10},{6,14},... | collective-permute-start | bytes 589832 | tf_op jit(solution)/shard_map/ppermute | solution.py:465
  272.1 15.7 %collective-permute-start.40 = (bf16[384,256]{1,0:T(8,128)(2,1)S(1)}, bf16[384,256]{1,0:T(8,128)(2,1)S(1)}, u32[]{:S(2)}, u32[]{:S(2)}) collective-permute-start(bf16[384,256]{1,0:T(8,128)(2,1)S(1)} %fusion.1.refs_3_), channel_id=1, source_target_pairs={{0,4},{4,0},{8,12},{12,8},{1,5},{5,1},{9,13},{13,9},{2,6},{6,2},{1... | collective-permute-start | bytes 589832 | tf_op jit(solution)/shard_map/ppermute | solution.py:465
  (24 other events, 155.3 us)
